TPU v7x, 768 devices: a whole 4x8x12 slice. The times are simulated.
768 devices in a mesh: row: 16 (over y_lo, x, core), col: 48 (over y_hi, z).
Axes of the slice: x: 4, y: 8 (y_hi: 4, y_lo: 2; y = y_hi * 2 + y_lo), z: 12, core: 2. Of those that a mesh axis runs over, the one named last changes fastest.
Arguments:
- tiles: bfloat16 [98304, 4096], P(('row', 'col')), may hold values from -0.25 to 0.25
- tile_row: int32 [98304], P(('row', 'col')), may hold values from 0 to 383
- tile_col: int32 [98304], P(('row', 'col')), may hold values from 0 to 127
- tile_count: int32 [768], P(('row', 'col')), may hold values from 1 to 128, as said below
- block: float32 [8, 393216], P(None, ('row', 'col')), may hold values from -6 to 6
- previous: float32 [8, 393216], P(None, ('row', 'col')), may hold values from -6 to 6
- coupling: float32 [8, 8], replicated, may hold values from -3 to 3
Outputs:
- lanczos_block: float32 [8, 393216], P(None, ('row', 'col'))
- alphas: float32 [2, 8, 8], replicated
Inputs may be any that keep to these rules, and one draw needn't show every extreme that they name: tile_count gives how many leading slots of a device are live; some device has exactly 128.
All inputs are finite; a program needn't handle non-finite values.
Results may differ from a plain program's by a relative error of at most 0.0042.
Values may be sent and summed in bfloat16 or wider, within the bound.
No kernel may reach another device: no remote copies, remote signals or barrier semaphores. Data moves between devices by JAX's collectives and lax.ppermute only.
A program may use at most 32 MiB of HBM per device.

v0:
```python
import jax
import jax.numpy as jnp
from jax import lax
from jax.sharding import PartitionSpec as P

TILE = 64
NV = 8
STEPS = 2


def shards(tiles, tile_row, tile_col, tile_count, block, previous, coupling):
    slots = tiles.shape[0]
    sub = block.shape[1]
    n_row = lax.axis_size("row")
    n_col = lax.axis_size("col")
    total = float(sub * n_row * n_col)
    row_tiles = n_col * sub // TILE
    col_tiles = n_row * sub // TILE
    squares = tiles.reshape(slots, TILE, TILE)
    live = (lax.iota(jnp.int32, slots) < tile_count[0]).astype(jnp.float32)[:, None, None]
    high = lax.Precision.HIGHEST

    def inner_product(left, right):
        local = jnp.dot(left, right.T, precision=high)
        return lax.psum(local, ("row", "col")) / total

    current, prior, beta = (block, previous, coupling)
    found = []
    for step in range(STEPS):
        narrow = current.astype(jnp.bfloat16)
        band = lax.all_gather(narrow, "row", axis=1, tiled=True)
        across = lax.all_gather(narrow, "col", axis=1, tiled=True)
        picked = band.reshape(NV, col_tiles, TILE)[:, tile_col]
        front = (
            jnp.einsum("kij,vkj->kvi", squares, picked, preferred_element_type=jnp.float32) * live
        )
        front = jax.ops.segment_sum(front, tile_row, num_segments=row_tiles)
        front = front.transpose(1, 0, 2).reshape(NV, n_col * sub)
        moved = lax.all_to_all(
            front.reshape(NV, n_col, sub), "col", split_axis=1, concat_axis=1, tiled=True
        )
        owned = jnp.sum(moved, axis=1)
        chosen = across.reshape(NV, row_tiles, TILE)[:, tile_row]
        back = (
            jnp.einsum("kij,vki->kvj", squares, chosen, preferred_element_type=jnp.float32) * live
        )
        back = jax.ops.segment_sum(back, tile_col, num_segments=col_tiles)
        back = back.transpose(1, 0, 2).reshape(NV, n_row * sub)
        returned = lax.psum_scatter(back, "row", scatter_dimension=1, tiled=True)
        image = owned + returned
        alpha = inner_product(current, image)
        found.append(alpha)
        resid = (
            image - jnp.dot(alpha.T, current, precision=high) - jnp.dot(beta, prior, precision=high)
        )
        gram = inner_product(resid, resid)
        lower = jnp.linalg.cholesky(gram)
        following = lax.linalg.triangular_solve(lower, resid, left_side=True, lower=True)
        prior, current, beta = (current, following, lower.T)
    return (current, jnp.stack(found))


def solution(mesh):
    in_specs = (
        P(("row", "col"), None),
        P(("row", "col")),
        P(("row", "col")),
        P(("row", "col")),
        P(None, ("row", "col")),
        P(None, ("row", "col")),
        P(),
    )
    out_specs = (P(None, ("row", "col")), P())
    return jax.shard_map(shards, mesh=mesh, in_specs=in_specs, out_specs=out_specs, check_vma=False)
```

profile of v0, /device:TPU:1, one launch (start us, length us, event | category | flops | bytes accessed | tf_op | source)
XLA Modules:
  0.0 997.0 jit_solution(3091057680233506666)
XLA Ops:
  7.2 1.6 copy.61
  8.8 3.0 copy.62
  12.5 26.7 %all_gather.12 = bf16[8,8192]{1,0:T(8,128)(2,1)S(1)} all-gather(bf16[8,512]{1,0:T(8,128)(2,1)S(1)} %convert_element_type.13), channel_id=1, replica_groups=mesh['row'=16,'col'=48] {'row'}, dimensions={1}, use_global_device_ids=true | all-gather | bytes 139264 | tf_op jit(solution)/shard_map/all_gather | solution.py:31
  42.8 13.0 %scatter_fusion = f32[384,8,64]{2,1,0:T(8,128)} fusion(f32[384,8,64]{2,1,0:T(8,128)} %broadcast.58.clone, s32[128]{0:T(128)S(1)} %copy-done.3, f32[128,8,64]{2,1,0:T(8,128)S(1)} %convolution_multiply_fusion.3), kind=kCustom, calls=%fused_computation.4 | custom fusion | flops 65536 | bytes 786944 | tf_op jit(solution)/shard_map/scatter-add | solution.py:37
  55.8 2.9 copy.63
  58.6 1.8 reshape_reshape.6
  60.5 1.3 copy.64
  61.8 14.7 %all-to-all-start = ((f32[8,48,512]{2,0,1:T(8,128)}), f32[8,48,512]{2,0,1:T(8,128)S(1)}, u32[]{:S(2)}, u32[]{:S(2)}) async-start(f32[8,48,512]{2,0,1:T(8,128)} %copy.64), calls=%async_computation | async-start | bytes 1572864 | tf_op jit(solution)/shard_map/all_to_all | solution.py:39
  76.5 115.9 %all_gather.13 = bf16[8,24576]{1,0:T(8,128)(2,1)S(1)} all-gather(bf16[8,512]{1,0:T(8,128)(2,1)S(1)} %convert_element_type.13), channel_id=1, replica_groups=mesh['row'=16,'col'=48] {'col'}, dimensions={1}, use_global_device_ids=true | all-gather | bytes 401408 | tf_op jit(solution)/shard_map/all_gather | solution.py:32
  192.4 1.7 reshape.43
  194.2 2.5 copy.65
  196.7 1.8 gather_fusion.1
  198.5 1.5 convolution_multiply_fusion.2
  200.0 9.5 scatter_fusion.1
  210.4 1.9 reshape.44
  212.5 77.4 %reduce-scatter.3.cloned.1.call-done = f32[8,512]{1,0:T(8,128)} async-done(((f32[8,8192]{1,0:T(8,128)}), f32[8,512]{1,0:T(8,128)}) %reduce-scatter.3.cloned.1.call-update) | async-done | bytes 16400 | tf_op jit(solution)/shard_map/reduce_scatter | solution.py:49
  290.7 112.0 %psum.28 = f32[8,8]{0,1:T(8,128)S(1)} all-reduce(f32[8,8]{0,1:T(8,128)S(1)} %convolution_bitcast_fusion), channel_id=1, replica_groups=mesh['row'=16,'col'=48] {'row','col'}, use_global_device_ids=true, to_apply=%region_4.0 | all-reduce | flops 64 | bytes 512 | tf_op jit(solution)/shard_map/psum | solution.py:25
  403.1 103.7 %psum.29 = f32[8,8]{0,1:T(8,128)S(1)} all-reduce(f32[8,8]{0,1:T(8,128)S(1)} %fusion.23), channel_id=1, replica_groups=mesh['row'=16,'col'=48] {'row','col'}, use_global_device_ids=true, to_apply=%region_5.0 | all-reduce | flops 64 | bytes 512 | tf_op jit(solution)/shard_map/psum | solution.py:25
  509.8 19.0 %all_gather.14 = bf16[8,8192]{1,0:T(8,128)(2,1)S(1)} all-gather(bf16[8,512]{1,0:T(8,128)(2,1)S(1)} %get-tuple-element.4), channel_id=1, replica_groups=mesh['row'=16,'col'=48] {'row'}, dimensions={1}, use_global_device_ids=true | all-gather | bytes 139264 | tf_op jit(solution)/shard_map/all_gather | solution.py:31
  532.3 13.0 %scatter_fusion.2 = f32[384,8,64]{2,1,0:T(8,128)} fusion(f32[384,8,64]{2,1,0:T(8,128)} %broadcast.58, s32[128]{0:T(128)S(1)} %copy-done.3, f32[128,8,64]{2,1,0:T(8,128)S(1)} %convolution_multiply_fusion.1), kind=kCustom, calls=%fused_computation.6 | custom fusion | flops 65536 | bytes 786944 | tf_op jit(solution)/shard_map/scatter-add | solution.py:37
  545.3 2.9 copy.73
  548.2 1.8 reshape_reshape.7
  551.3 8.8 all-to-all-start.1
  560.2 116.3 %all_gather.15 = bf16[8,24576]{1,0:T(8,128)(2,1)S(1)} all-gather(bf16[8,512]{1,0:T(8,128)(2,1)S(1)} %get-tuple-element.4), channel_id=1, replica_groups=mesh['row'=16,'col'=48] {'col'}, dimensions={1}, use_global_device_ids=true | all-gather | bytes 401408 | tf_op jit(solution)/shard_map/all_gather | solution.py:32
  676.5 1.7 reshape.46
  678.2 2.5 copy.75
  680.8 2.5 gather_fusion.3
  683.3 1.6 convolution_multiply_fusion
  684.9 4.9 scatter_fusion.3
  691.0 77.3 %reduce-scatter.5.cloned.1.call-done = f32[8,512]{1,0:T(8,128)} async-done(((f32[8,8192]{1,0:T(8,128)}), f32[8,512]{1,0:T(8,128)}) %reduce-scatter.5.cloned.1.call-update) | async-done | bytes 16400 | tf_op jit(solution)/shard_map/reduce_scatter | solution.py:49
  769.2 111.9 %psum.30 = f32[8,8]{0,1:T(8,128)S(1)} all-reduce(f32[8,8]{0,1:T(8,128)S(1)} %fusion.24), channel_id=1, replica_groups=mesh['row'=16,'col'=48] {'row','col'}, use_global_device_ids=true, to_apply=%region_12.15 | all-reduce | flops 64 | bytes 512 | tf_op jit(solution)/shard_map/psum | solution.py:25
  882.3 103.7 %psum.31 = f32[8,8]{0,1:T(8,128)S(1)} all-reduce(f32[8,8]{0,1:T(8,128)S(1)} %fusion.25), channel_id=1, replica_groups=mesh['row'=16,'col'=48] {'row','col'}, use_global_device_ids=true, to_apply=%region_13.16 | all-reduce | flops 64 | bytes 512 | tf_op jit(solution)/shard_map/psum | solution.py:25
  (73 shorter events, 21.3 us)
Async XLA Ops:
  7.2 395.7 %copy-start = (f32[8,512]{1,0:T(8,128)S(1)}, f32[8,512]{1,0:T(8,128)}, u32[]{:S(2)}) copy-start(f32[8,512]{1,0:T(8,128)} %param.15) | copy-start | bytes 49156
  8.8 3.7 copy-start.1
  8.8 30.8 %copy-start.4 = (s32[128]{0:T(128)S(1)}, s32[128]{0:T(128)}, u32[]{:S(2)}) copy-start(s32[128]{0:T(128)} %param.12) | copy-start | bytes 1540
  40.3 2.5 copy-start.3
  61.8 150.6 %all-to-all-start = ((f32[8,48,512]{2,0,1:T(8,128)}), f32[8,48,512]{2,0,1:T(8,128)S(1)}, u32[]{:S(2)}, u32[]{:S(2)}) async-start(f32[8,48,512]{2,0,1:T(8,128)} %copy.64), calls=%async_computation | async-start | bytes 1572864 | tf_op jit(solution)/shard_map/all_to_all | solution.py:39
  76.5 213.4 %reduce-scatter.3.cloned.1.call-start = ((), (), s32[]{:S(2)}) async-start(), calls=%async_computation.4 | async-start | bytes 278528 | tf_op jit(solution)/shard_map/reduce_scatter | solution.py:49
  200.0 202.8 %copy-start.2 = (f32[8,8]{1,0:T(8,128)S(1)}, f32[8,8]{1,0:T(8,128)}, u32[]{:S(2)}) copy-start(f32[8,8]{1,0:T(8,128)} %param.16) | copy-start | bytes 772
  551.3 139.6 %all-to-all-start.1 = ((f32[8,48,512]{2,0,1:T(8,128)}), f32[8,48,512]{2,0,1:T(8,128)S(1)}, u32[]{:S(2)}, u32[]{:S(2)}) async-start(f32[8,48,512]{2,0,1:T(8,128)} %copy.74), calls=%async_computation.2 | async-start | bytes 1572864 | tf_op jit(solution)/shard_map/all_to_all | solution.py:39
  560.2 208.2 %reduce-scatter.5.cloned.1.call-start = ((), (), s32[]{:S(2)}) async-start(), calls=%async_computation.5 | async-start | bytes 278528 | tf_op jit(solution)/shard_map/reduce_scatter | solution.py:49
Sparse Core Ops, SparseCore 0:
  212.5 77.3 reduce-scatter.2
  691.0 77.3 reduce-scatter.4
where the time goes:
time: 999 us; the launch traced here: 997 us
  blocking collectives  709 us (71%)
  waiting for transfers between devices  155 us (16%)
  other arithmetic  47.9 us (5%)
  local copies, waits for them, and re-layouts  38.5 us (4%)
  starting transfers between devices  23.6 us (2%)
  between operations  15 us (2%)
    psum x4, blocking collectives, inner_product(): return lax.psum(local, ('row', 'col')) / total  431 us
    all_gather x2, blocking collectives, shards(): across = lax.all_gather(narrow, 'col', axis=1, tiled=True)  232 us
    reduce_scatter x2, waiting for transfers between devices, shards(): returned = lax.psum_scatter(back, 'row', scatter_dimension=1, tiled=True)  155 us
    all_gather x2, blocking collectives, shards(): band = lax.all_gather(narrow, 'row', axis=1, tiled=True)  45.6 us
    scatter-add x2, other arithmetic, shards(): front = jax.ops.segment_sum(front, tile_row, num_segments=row_tiles)  26 us
    all_to_all x2, starting transfers between devices, shards(): lax.all_to_all(front.reshape(NV, n_col, sub), 'col', split_axis=1, concat...  23.5 us
  transfers between devices with their start and end apart: 4, of which 2 were waited for; matrix products, arithmetic and copies ran while one was open for 3% of the time, Pallas kernels for 0%

commit v1 on v0

v1 whole, which is shorter than its diff:
```python
import functools

import jax
import jax.numpy as jnp
from jax import lax
from jax.experimental import pallas as pl
from jax.experimental.pallas import tpu as pltpu
from jax.sharding import PartitionSpec as P

TILE = 64
NV = 8
STEPS = 2
LANES = 128
GROUP = 16
HIGH = lax.Precision.HIGHEST
F32 = jnp.float32
BF16 = jnp.bfloat16
VMEM = pl.BlockSpec(memory_space=pltpu.VMEM)
SMEM = pl.BlockSpec(memory_space=pltpu.SMEM)
PARAMS = pltpu.CompilerParams(vmem_limit_bytes=40 * 1024 * 1024)


def dot(left, right):
    return jnp.dot(left, right, precision=HIGH, preferred_element_type=F32)


def dot_t(left, right):
    return lax.dot_general(
        left, right, (((1,), (1,)), ((), ())), precision=HIGH, preferred_element_type=F32
    )


def dot_tn(left, right):
    return lax.dot_general(
        left, right, (((0,), (0,)), ((), ())), precision=HIGH, preferred_element_type=F32
    )


def apply_kernel(rows, cols, count, tiles, band, across, front, back, band32, across32, front32):
    slots = tiles.shape[0]
    per_segment = front.shape[2] // TILE
    band32[...] = band[...].astype(F32)
    across32[...] = across[...].astype(F32)
    front32[...] = jnp.zeros_like(front32)
    back[...] = jnp.zeros_like(back)
    half = lax.broadcasted_iota(jnp.int32, (NV, LANES), 1) // TILE

    def place(index):
        within = index % per_segment
        lane = pl.multiple_of(within // 2 * LANES, LANES)
        return index // per_segment, pl.ds(lane, LANES), index % 2

    def group(g, carry):
        updates = []
        for u in range(GROUP):
            k = g * GROUP + u
            live = k < count[0]
            row_segment, row_lanes, row_half = place(rows[k])
            col_segment, col_lanes, col_half = place(cols[k])
            row_mask = half == jnp.where(live, row_half, 2)
            col_mask = half == jnp.where(live, col_half, 2)
            tile = tiles[k]
            picked = jnp.where(col_mask, band32[col_segment, :, col_lanes], 0.0)
            chosen = jnp.where(row_mask, across32[row_segment, :, row_lanes], 0.0)
            chosen = (chosen + pltpu.roll(chosen, TILE, 1))[:, :TILE]
            ahead = lax.dot_general(
                picked.astype(BF16), tile, (((1,), (1,)), ((), ())), preferred_element_type=F32
            )
            behind = jnp.dot(chosen.astype(BF16), tile, preferred_element_type=F32)
            ahead = jnp.where(row_mask, jnp.concatenate([ahead, ahead], axis=1), 0.0)
            behind = jnp.where(col_mask, behind, 0.0)
            updates.append((row_segment, row_lanes, ahead, col_segment, col_lanes, behind))
        for row_segment, row_lanes, ahead, col_segment, col_lanes, behind in updates:
            front32[row_segment, :, row_lanes] += ahead
            back[col_segment, :, col_lanes] += behind
        return carry

    lax.fori_loop(0, slots // GROUP, group, 0)
    front[...] = front32[...].astype(front.dtype)


def apply(rows, cols, count, tiles, band, across):
    return pl.pallas_call(
        apply_kernel,
        out_shape=(
            jax.ShapeDtypeStruct(across.shape, BF16),
            jax.ShapeDtypeStruct(band.shape, F32),
        ),
        in_specs=[SMEM, SMEM, SMEM, VMEM, VMEM, VMEM],
        out_specs=(VMEM, VMEM),
        scratch_shapes=[
            pltpu.VMEM(band.shape, F32),
            pltpu.VMEM(across.shape, F32),
            pltpu.VMEM(across.shape, F32),
        ],
        compiler_params=PARAMS,
        name="apply_tiles",
    )(rows, cols, count, tiles, band, across)


def local_kernel(moved, returned, current, prior, beta, ahead, sums):
    image = jnp.sum(moved[...].astype(F32), axis=0) + jnp.sum(returned[...], axis=0)
    now = current[...]
    rest = image - dot(beta[...], prior[...])
    ahead[...] = rest
    left = jnp.concatenate([now, rest], axis=0)
    right = jnp.concatenate([image, rest, now], axis=0)
    inner = dot_t(left, right)
    pad = jnp.zeros((NV, LANES - 4 * NV), F32)
    one = jnp.concatenate([inner[:NV], inner[NV:, NV : 2 * NV], pad], axis=1)
    sums[...] = jnp.broadcast_to(one[None], sums.shape)


def local(moved, returned, current, prior, beta, n_row):
    return pl.pallas_call(
        local_kernel,
        out_shape=(
            jax.ShapeDtypeStruct(current.shape, F32),
            jax.ShapeDtypeStruct((n_row, NV, LANES), F32),
        ),
        in_specs=[VMEM] * 5,
        out_specs=(VMEM, VMEM),
        compiler_params=PARAMS,
        name="local_sums",
    )(moved, returned, current, prior, beta)


def spread_kernel(parts, sums):
    one = jnp.sum(parts[...], axis=0)
    sums[...] = jnp.broadcast_to(one[None], sums.shape)


def spread(parts, n_col):
    return pl.pallas_call(
        spread_kernel,
        out_shape=jax.ShapeDtypeStruct((n_col, NV, LANES), F32),
        in_specs=[VMEM],
        out_specs=VMEM,
        compiler_params=PARAMS,
        name="spread_sums",
    )(parts)


def next_kernel(total, last, parts, rest, current, alpha_out, upper_out, following, *copies):
    summed = jnp.sum(parts[...], axis=0) / total
    alpha = summed[:, :NV]
    mixed = summed[:, NV : 2 * NV]
    own = summed[:, 2 * NV : 3 * NV]
    square = summed[:, 3 * NV : 4 * NV]
    alpha_out[...] = alpha
    cross = dot_tn(alpha, mixed)
    cross_t = dot_tn(mixed, alpha)
    gram = square - cross - cross_t + dot_tn(alpha, dot(own, alpha))
    row = lax.broadcasted_iota(jnp.int32, (NV, 2 * NV), 0)
    lane = lax.broadcasted_iota(jnp.int32, (NV, 2 * NV), 1)
    unit = jnp.where(row + NV == lane, 1.0, 0.0).astype(F32)
    work = jnp.concatenate([gram, unit[:, NV:]], axis=1)
    for j in range(NV):
        pivot = jnp.sqrt(work[j : j + 1, j : j + 1])
        scaled = work[j : j + 1, :] / pivot
        factor = work[:, j : j + 1] / pivot
        work = jnp.where(row == j, scaled, jnp.where(row > j, work - factor * scaled, work))
    upper_out[...] = jnp.where(row <= lane, work, 0.0)[:, :NV]
    inverse = work[:, NV:]
    resid = rest[...] - dot_tn(alpha, current[...])
    block = dot(inverse, resid)
    following[...] = block
    if not last:
        narrow = block.astype(BF16)
        for copy in copies:
            copy[...] = jnp.broadcast_to(narrow[None], copy.shape)


def advance(parts, rest, current, total, n_row, n_col, last):
    sub = current.shape[1]
    shapes = [
        jax.ShapeDtypeStruct((NV, NV), F32),
        jax.ShapeDtypeStruct((NV, NV), F32),
        jax.ShapeDtypeStruct(current.shape, F32),
    ]
    if not last:
        shapes.append(jax.ShapeDtypeStruct((n_row, NV, sub), BF16))
        shapes.append(jax.ShapeDtypeStruct((n_col, NV, sub), BF16))
    return pl.pallas_call(
        functools.partial(next_kernel, total, last),
        out_shape=tuple(shapes),
        in_specs=[VMEM] * 3,
        out_specs=(VMEM,) * len(shapes),
        compiler_params=PARAMS,
        name="next_block",
    )(parts, rest, current)


def swap(blocks, axis):
    return lax.all_to_all(blocks, axis, 0, 0, tiled=True)


def shards(tiles, tile_row, tile_col, tile_count, block, previous, coupling):
    slots = tiles.shape[0]
    sub = block.shape[1]
    n_row = lax.axis_size("row")
    n_col = lax.axis_size("col")
    total = float(sub * n_row * n_col)
    squares = tiles.reshape(slots, TILE, TILE)
    squares = jnp.concatenate([squares, squares], axis=2)
    current, prior, beta = (block, previous, coupling)
    narrow = current.astype(BF16)
    to_row = jnp.broadcast_to(narrow[None], (n_row, NV, sub))
    to_col = jnp.broadcast_to(narrow[None], (n_col, NV, sub))
    found = []
    for step in range(STEPS):
        last = step == STEPS - 1
        band = swap(to_row, "row")
        across = swap(to_col, "col")
        front, back = apply(tile_row, tile_col, tile_count, squares, band, across)
        moved = swap(front, "col")
        returned = swap(back, "row")
        rest, sums = local(moved, returned, current, prior, beta, n_row)
        sums = spread(swap(sums, "row"), n_col)
        parts = swap(sums, "col")
        alpha, upper, following, *copies = advance(
            parts, rest, current, total, n_row, n_col, last
        )
        found.append(alpha)
        if not last:
            to_row, to_col = copies
        prior, current, beta = (current, following, upper)
    return (current, jnp.stack(found))


def solution(mesh):
    in_specs = (
        P(("row", "col"), None),
        P(("row", "col")),
        P(("row", "col")),
        P(("row", "col")),
        P(None, ("row", "col")),
        P(None, ("row", "col")),
        P(),
    )
    out_specs = (P(None, ("row", "col")), P())
    return jax.shard_map(shards, mesh=mesh, in_specs=in_specs, out_specs=out_specs, check_vma=False)
```

time: 999 us -> 255 us (0.26)
  blocking collectives: 709 us -> 200 us
  waiting for transfers between devices: 155 us -> 12.9 us
  other arithmetic: 47.9 us -> 4.8 us
  local copies, waits for them, and re-layouts: 38.5 us -> 5.26 us
  Pallas kernels: 0 us -> 16.2 us
  between operations: 15 us -> 1.4 us
  starting transfers between devices: 23.6 us -> 13.5 us
    psum x4 -> x0, blocking collectives: 431 us -> none  [inner_product(): return lax.psum(local, ('row', 'col')) / total]
    all_gather x4 -> x0, blocking collectives: 278 us -> none  [the longest x2 232 us: shards(): across = lax.all_gather(narrow, 'col', axis=1, tiled=True)]
    all_to_all x0 -> x11, blocking collectives: none -> 200 us  [swap(): return lax.all_to_all(blocks, axis, 0, 0, tiled=True)]
    reduce_scatter x2 -> x0, waiting for transfers between devices: 155 us -> none  [shards(): returned = lax.psum_scatter(back, 'row', scatter_dimension=1, tiled=True)]
    scatter-add x4 -> x0, other arithmetic: 40.4 us -> none  [the longest x2 26 us: shards(): front = jax.ops.segment_sum(front, tile_row, num_segments=row_tiles)]
    pallas_call x0 -> x8, Pallas kernels: none -> 16.2 us  [the longest x2 11.8 us: apply(): pl.pallas_call(apply_kernel, out_shape=(jax.ShapeDtypeStruct(across.shape...]
    all_to_all x2 -> x1, waiting for transfers between devices: 0.01 us -> 12.9 us  [swap(): return lax.all_to_all(blocks, axis, 0, 0, tiled=True)]
    reshape x10 -> x0, local copies, waits for them, and re-layouts: 12.2 us -> none  [the longest x4 8.55 us: shards(): chosen = across.reshape(NV, row_tiles, TILE)[:, tile_row]]
  transfers between devices with their start and end apart: 4 -> 1, of which waited for: 2 -> 1; matrix products, arithmetic and copies ran while one was open for 3% -> 3% of each run, Pallas kernels for 0% -> 0%
where the time goes in v1:
time: 255 us; the launch traced here: 254 us
  blocking collectives  200 us (78%)
  Pallas kernels  16.2 us (6%)
  starting transfers between devices  13.5 us (5%)
  waiting for transfers between devices  12.9 us (5%)
  local copies, waits for them, and re-layouts  5.26 us (2%)
  other arithmetic  4.8 us (2%)
    all_to_all x11, blocking collectives, swap(): return lax.all_to_all(blocks, axis, 0, 0, tiled=True)  200 us
    all_to_all x1, starting transfers between devices, swap(): return lax.all_to_all(blocks, axis, 0, 0, tiled=True)  13.5 us
    all_to_all x1, waiting for transfers between devices, swap(): return lax.all_to_all(blocks, axis, 0, 0, tiled=True)  12.9 us
    pallas_call x2, Pallas kernels, apply(): pl.pallas_call(apply_kernel, out_shape=(jax.ShapeDtypeStruct(across.shape...  11.8 us
  transfers between devices with their start and end apart: 1, of which 1 were waited for; matrix products, arithmetic and copies ran while one was open for 3% of the time, Pallas kernels for 0%

profile of v1, /device:TPU:1, one launch (start us, length us, event | category | flops | bytes accessed | tf_op | source)
XLA Modules:
  0.0 253.7 jit_solution(12821389362240475461)
XLA Ops:
  0.6 0.8 convert_element_type.3
  1.5 19.1 %all_to_all.60.band = bf16[16,8,512]{2,1,0:T(8,128)(2,1)S(1)} all-to-all(bf16[16,8,512]{2,1,0:T(8,128)(2,1)S(1)} %broadcast_in_dim.4), channel_id=1, replica_groups=mesh['row'=16,'col'=48] {'row'}, dimensions={0} | all-to-all | bytes 262144 | tf_op jit(solution)/shard_map/all_to_all | solution.py:195
  20.6 0.8 broadcast_in_dim.5
  21.4 13.5 %all-to-all-start.1 = ((bf16[48,8,512]{2,1,0:T(8,128)(2,1)}), bf16[48,8,512]{2,1,0:T(8,128)(2,1)S(1)}, u32[]{:S(2)}, u32[]{:S(2)}) async-start(bf16[48,8,512]{2,1,0:T(8,128)(2,1)} %broadcast_in_dim.5), calls=%async_computation.1 | async-start | bytes 786432 | tf_op jit(solution)/shard_map/all_to_all | solution.py:195
  34.9 0.7 copy.9
  35.6 3.8 %copy.10 = bf16[128,64,64]{2,1,0:T(8,128)(2,1)} copy(bf16[128,64,64]{0,2,1:T(8,128)(2,1)S(1)} %bitcast.5) | data formatting | bytes 2097152 | tf_op jit(solution)/shard_map/reshape | solution.py:204
  40.0 0.0 copy-start.3
  40.0 0.0 copy-start.4
  40.1 3.4 %pad_maximum_fusion.tiles = bf16[128,64,128]{2,1,0:T(8,128)(2,1)S(1)} fusion(bf16[128,64,64]{2,1,0:T(8,128)(2,1)} %copy.10), kind=kLoop, calls=%fused_computation | loop fusion | flops 4194304 | bytes 3145728 | tf_op jit(solution)/shard_map/concatenate | solution.py:205
  43.4 0.0 copy-start
  43.5 0.0 copy-start.1
  43.5 0.0 copy-start.2
  43.5 12.9 %all-to-all-done.1.across = bf16[48,8,512]{2,1,0:T(8,128)(2,1)S(1)} async-done(((bf16[48,8,512]{2,1,0:T(8,128)(2,1)}), bf16[48,8,512]{2,1,0:T(8,128)(2,1)S(1)}, u32[]{:S(2)}, u32[]{:S(2)}) %all-to-all-start.1) | async-done | bytes 393248 | tf_op jit(solution)/shard_map/all_to_all | solution.py:195
  56.4 0.0 copy-done.4
  56.4 5.9 %apply_tiles.2 = (bf16[48,8,512]{2,1,0:T(8,128)(2,1)S(1)}, f32[16,8,512]{2,1,0:T(8,128)S(1)}) custom-call(s32[128]{0:T(128)S(1)} %copy-done.3, s32[128]{0:T(128)S(1)} %copy-done.4, s32[1]{0:T(128)S(6)} %copy.12.count, bf16[128,64,128]{2,1,0:T(8,128)(2,1)S(1)} %pad_maximum_fusion.tiles, bf16[16,8,512]{2,1,0:T(8,128)(2,1)S(1)} %all_to_all.60.band, ...), custom_call_target="tpu_custom_call" | custom-call | tf_op jit(solution)/shard_map/apply_tiles/pallas_call | solution.py:83
  62.3 12.9 %all_to_all.61.returned = f32[16,8,512]{2,1,0:T(8,128)S(1)} all-to-all(f32[16,8,512]{2,1,0:T(8,128)S(1)} %get-tuple-element.18), channel_id=1, replica_groups=mesh['row'=16,'col'=48] {'row'}, dimensions={0} | all-to-all | bytes 524288 | tf_op jit(solution)/shard_map/all_to_all | solution.py:195
  75.3 26.2 %all_to_all.62.moved = bf16[48,8,512]{2,1,0:T(8,128)(2,1)S(1)} all-to-all(bf16[48,8,512]{2,1,0:T(8,128)(2,1)S(1)} %get-tuple-element.17), channel_id=1, replica_groups=mesh['row'=16,'col'=48] {'col'}, dimensions={0} | all-to-all | bytes 786432 | tf_op jit(solution)/shard_map/all_to_all | solution.py:195
  101.5 0.0 copy-done.1
  101.5 0.4 local_sums.2
  101.8 11.8 %all_to_all.63.parts = f32[16,8,128]{2,1,0:T(8,128)S(1)} all-to-all(f32[16,8,128]{2,1,0:T(8,128)S(1)} %get-tuple-element.19), channel_id=1, replica_groups=mesh['row'=16,'col'=48] {'row'}, dimensions={0} | all-to-all | bytes 131072 | tf_op jit(solution)/shard_map/all_to_all | solution.py:195
  113.7 20.7 %all_to_all.64.parts = f32[48,8,128]{2,1,0:T(8,128)S(1)} all-to-all(f32[48,8,128]{2,1,0:T(8,128)S(1)} %spread_sums.2), channel_id=1, replica_groups=mesh['row'=16,'col'=48] {'col'}, dimensions={0} | all-to-all | bytes 393216 | tf_op jit(solution)/shard_map/all_to_all | solution.py:195
  134.4 1.5 next_block.2
  135.9 11.8 %all_to_all.65.band = bf16[16,8,512]{2,1,0:T(8,128)(2,1)S(1)} all-to-all(bf16[16,8,512]{2,1,0:T(8,128)(2,1)S(1)} %get-tuple-element.21), channel_id=1, replica_groups=mesh['row'=16,'col'=48] {'row'}, dimensions={0} | all-to-all | bytes 262144 | tf_op jit(solution)/shard_map/all_to_all | solution.py:195
  147.6 25.4 %all_to_all.66.across = bf16[48,8,512]{2,1,0:T(8,128)(2,1)S(1)} all-to-all(bf16[48,8,512]{2,1,0:T(8,128)(2,1)S(1)} %get-tuple-element.22), channel_id=1, replica_groups=mesh['row'=16,'col'=48] {'col'}, dimensions={0} | all-to-all | bytes 786432 | tf_op jit(solution)/shard_map/all_to_all | solution.py:195
  173.1 5.9 %apply_tiles.3 = (bf16[48,8,512]{2,1,0:T(8,128)(2,1)S(1)}, f32[16,8,512]{2,1,0:T(8,128)S(1)}) custom-call(s32[128]{0:T(128)S(1)} %copy-done.3, s32[128]{0:T(128)S(1)} %copy-done.4, s32[1]{0:T(128)S(6)} %copy.12.count, bf16[128,64,128]{2,1,0:T(8,128)(2,1)S(1)} %pad_maximum_fusion.tiles, bf16[16,8,512]{2,1,0:T(8,128)(2,1)S(1)} %all_to_all.65.band, ...), custom_call_target="tpu_custom_call" | custom-call | tf_op jit(solution)/shard_map/apply_tiles/pallas_call | solution.py:83
  179.0 12.9 %all_to_all.67.returned = f32[16,8,512]{2,1,0:T(8,128)S(1)} all-to-all(f32[16,8,512]{2,1,0:T(8,128)S(1)} %get-tuple-element.24), channel_id=1, replica_groups=mesh['row'=16,'col'=48] {'row'}, dimensions={0} | all-to-all | bytes 524288 | tf_op jit(solution)/shard_map/all_to_all | solution.py:195
  191.9 26.2 %all_to_all.68.moved = bf16[48,8,512]{2,1,0:T(8,128)(2,1)S(1)} all-to-all(bf16[48,8,512]{2,1,0:T(8,128)(2,1)S(1)} %get-tuple-element.23), channel_id=1, replica_groups=mesh['row'=16,'col'=48] {'col'}, dimensions={0} | all-to-all | bytes 786432 | tf_op jit(solution)/shard_map/all_to_all | solution.py:195
  218.1 0.4 local_sums.3
  218.5 11.8 %all_to_all.69.parts = f32[16,8,128]{2,1,0:T(8,128)S(1)} all-to-all(f32[16,8,128]{2,1,0:T(8,128)S(1)} %get-tuple-element.27), channel_id=1, replica_groups=mesh['row'=16,'col'=48] {'row'}, dimensions={0} | all-to-all | bytes 131072 | tf_op jit(solution)/shard_map/all_to_all | solution.py:195
  230.4 20.7 %all_to_all.70.parts = f32[48,8,128]{2,1,0:T(8,128)S(1)} all-to-all(f32[48,8,128]{2,1,0:T(8,128)S(1)} %spread_sums.3), channel_id=1, replica_groups=mesh['row'=16,'col'=48] {'col'}, dimensions={0} | all-to-all | bytes 393216 | tf_op jit(solution)/shard_map/all_to_all | solution.py:195
  251.1 2.1 next_block.3
  253.1 0.6 pad_maximum_fusion.1
  (8 shorter events, 0.1 us)
Async XLA Ops:
  0.6 34.3 %copy-start.5 = (bf16[128,4096]{1,0:T(8,128)(2,1)S(1)}, bf16[128,4096]{1,0:T(8,128)(2,1)}, u32[]{:S(2)}) copy-start(bf16[128,4096]{1,0:T(8,128)(2,1)} %param.7) | copy-start | bytes 3145732
  21.4 35.0 %all-to-all-start.1 = ((bf16[48,8,512]{2,1,0:T(8,128)(2,1)}), bf16[48,8,512]{2,1,0:T(8,128)(2,1)S(1)}, u32[]{:S(2)}, u32[]{:S(2)}) async-start(bf16[48,8,512]{2,1,0:T(8,128)(2,1)} %broadcast_in_dim.5), calls=%async_computation.1 | async-start | bytes 786432 | tf_op jit(solution)/shard_map/all_to_all | solution.py:195
  40.0 16.4 %copy-start.3 = (s32[128]{0:T(128)S(1)}, s32[128]{0:T(128)}, u32[]{:S(2)}) copy-start(s32[128]{0:T(128)} %rows.3) | copy-start | bytes 1540
  40.0 16.4 %copy-start.4 = (s32[128]{0:T(128)S(1)}, s32[128]{0:T(128)}, u32[]{:S(2)}) copy-start(s32[128]{0:T(128)} %cols.3) | copy-start | bytes 1540
  43.4 58.0 %copy-start = (f32[8,512]{1,0:T(8,128)S(1)}, f32[8,512]{1,0:T(8,128)}, u32[]{:S(2)}) copy-start(f32[8,512]{1,0:T(8,128)} %prior.3) | copy-start | bytes 49156
  43.5 58.0 %copy-start.1 = (f32[8,512]{1,0:T(8,128)S(1)}, f32[8,512]{1,0:T(8,128)}, u32[]{:S(2)}) copy-start(f32[8,512]{1,0:T(8,128)} %prior.2) | copy-start | bytes 49156
  43.5 58.0 %copy-start.2 = (f32[8,8]{1,0:T(8,128)S(1)}, f32[8,8]{1,0:T(8,128)}, u32[]{:S(2)}) copy-start(f32[8,8]{1,0:T(8,128)} %beta.1) | copy-start | bytes 772

commit v2 on v1

v2 whole, which is shorter than its diff:
```python
import functools

import jax
import jax.numpy as jnp
from jax import lax
from jax.experimental import pallas as pl
from jax.experimental.pallas import tpu as pltpu
from jax.sharding import PartitionSpec as P

TILE = 64
NV = 8
STEPS = 2
LANES = 128
GROUP = 16
HIGH = lax.Precision.HIGHEST
F32 = jnp.float32
BF16 = jnp.bfloat16
VMEM = pl.BlockSpec(memory_space=pltpu.VMEM)
SMEM = pl.BlockSpec(memory_space=pltpu.SMEM)
PARAMS = pltpu.CompilerParams(vmem_limit_bytes=40 * 1024 * 1024)


def dot(left, right):
    return jnp.dot(left, right, precision=HIGH, preferred_element_type=F32)


def dot_t(left, right):
    return lax.dot_general(
        left, right, (((1,), (1,)), ((), ())), precision=HIGH, preferred_element_type=F32
    )


def dot_tn(left, right):
    return lax.dot_general(
        left, right, (((0,), (0,)), ((), ())), precision=HIGH, preferred_element_type=F32
    )


def place(index, per_segment):
    within = index % per_segment
    lane = pl.multiple_of(within // 2 * LANES, LANES)
    return index // per_segment, pl.ds(lane, LANES), index % 2


def lane_half():
    return lax.broadcasted_iota(jnp.int32, (NV, LANES), 1) // TILE


def narrowed(pair, mask):
    held = jnp.where(mask, pair, 0.0)
    return (held + pltpu.roll(held, TILE, 1))[:, :TILE].astype(BF16)


def both_halves(product, mask):
    return jnp.where(mask, jnp.concatenate([product, product], axis=1), 0.0)


def front_kernel(rows, cols, count, tiles, band, narrow, message, band32, front32):
    slots = tiles.shape[0]
    per_segment = message.shape[2] // TILE
    band32[...] = band[...].astype(F32)
    front32[...] = jnp.zeros_like(front32)
    half = lane_half()

    def group(g, carry):
        updates = []
        for u in range(GROUP):
            k = g * GROUP + u
            row_segment, row_lanes, row_half = place(rows[k], per_segment)
            col_segment, col_lanes, col_half = place(cols[k], per_segment)
            col_mask = half == jnp.where(k < count[0], col_half, 2)
            picked = narrowed(band32[col_segment, :, col_lanes], col_mask)
            ahead = lax.dot_general(
                picked, tiles[k], (((1,), (1,)), ((), ())), preferred_element_type=F32
            )
            updates.append((row_segment, row_lanes, both_halves(ahead, half == row_half)))
        for segment, lanes, ahead in updates:
            front32[segment, :, lanes] += ahead
        return carry

    lax.fori_loop(0, slots // GROUP, group, 0)
    own = jnp.broadcast_to(narrow[...][None], (message.shape[0],) + narrow.shape)
    message[...] = jnp.concatenate([own, front32[...].astype(BF16)], axis=1)


def front(rows, cols, count, tiles, band, narrow, n_col):
    sub = band.shape[2]
    return pl.pallas_call(
        front_kernel,
        out_shape=jax.ShapeDtypeStruct((n_col, 2 * NV, sub), BF16),
        in_specs=[SMEM, SMEM, SMEM, VMEM, VMEM, VMEM],
        out_specs=VMEM,
        scratch_shapes=[pltpu.VMEM(band.shape, F32), pltpu.VMEM((n_col, NV, sub), F32)],
        compiler_params=PARAMS,
        name="front_tiles",
    )(rows, cols, count, tiles, band, narrow)


def back_kernel(rows, cols, count, tiles, moved, back, owned, across32):
    slots = tiles.shape[0]
    per_segment = moved.shape[2] // TILE
    arrived = moved[...].astype(F32)
    across32[...] = arrived[:, :NV]
    owned[...] = jnp.sum(arrived[:, NV:], axis=0)
    back[...] = jnp.zeros_like(back)
    half = lane_half()

    def group(g, carry):
        updates = []
        for u in range(GROUP):
            k = g * GROUP + u
            row_segment, row_lanes, row_half = place(rows[k], per_segment)
            col_segment, col_lanes, col_half = place(cols[k], per_segment)
            row_mask = half == jnp.where(k < count[0], row_half, 2)
            chosen = narrowed(across32[row_segment, :, row_lanes], row_mask)
            behind = jnp.dot(chosen, tiles[k], preferred_element_type=F32)
            updates.append((col_segment, col_lanes, both_halves(behind, half == col_half)))
        for segment, lanes, behind in updates:
            back[segment, :, lanes] += behind
        return carry

    lax.fori_loop(0, slots // GROUP, group, 0)


def back(rows, cols, count, tiles, moved, n_row):
    sub = moved.shape[2]
    return pl.pallas_call(
        back_kernel,
        out_shape=(
            jax.ShapeDtypeStruct((n_row, NV, sub), F32),
            jax.ShapeDtypeStruct((NV, sub), F32),
        ),
        in_specs=[SMEM, SMEM, SMEM, VMEM, VMEM],
        out_specs=(VMEM, VMEM),
        scratch_shapes=[pltpu.VMEM((moved.shape[0], NV, sub), F32)],
        compiler_params=PARAMS,
        name="back_tiles",
    )(rows, cols, count, tiles, moved)


def local_kernel(owned, returned, current, prior, beta, ahead, sums):
    image = owned[...] + jnp.sum(returned[...], axis=0)
    now = current[...]
    rest = image - dot(beta[...], prior[...])
    ahead[...] = rest
    left = jnp.concatenate([now, rest], axis=0)
    right = jnp.concatenate([image, rest, now], axis=0)
    inner = dot_t(left, right)
    blocks = jnp.concatenate([inner[:NV], inner[NV:, NV : 2 * NV]], axis=1)
    packed = [
        jnp.concatenate([blocks[v : v + 1] for v in range(part, part + 4)], axis=1)
        for part in (0, 4)
    ]
    one = jnp.concatenate(packed, axis=0)
    sums[...] = jnp.broadcast_to(one[None], sums.shape)


def local(owned, returned, current, prior, beta, n_row):
    return pl.pallas_call(
        local_kernel,
        out_shape=(
            jax.ShapeDtypeStruct(current.shape, F32),
            jax.ShapeDtypeStruct((n_row, 2, LANES), F32),
        ),
        in_specs=[VMEM] * 5,
        out_specs=(VMEM, VMEM),
        compiler_params=PARAMS,
        name="local_sums",
    )(owned, returned, current, prior, beta)


def spread_kernel(parts, sums):
    one = jnp.sum(parts[...], axis=0)
    sums[...] = jnp.broadcast_to(one[None], sums.shape)


def spread(parts, n_col):
    return pl.pallas_call(
        spread_kernel,
        out_shape=jax.ShapeDtypeStruct((n_col, 2, LANES), F32),
        in_specs=[VMEM],
        out_specs=VMEM,
        compiler_params=PARAMS,
        name="spread_sums",
    )(parts)


def next_kernel(total, last, parts, rest, current, alpha_out, upper_out, following, *sent):
    packed = jnp.sum(parts[...], axis=0) / total
    width = LANES // 4
    summed = jnp.concatenate(
        [packed[v // 4 : v // 4 + 1, v % 4 * width : (v % 4 + 1) * width] for v in range(NV)],
        axis=0,
    )
    alpha = summed[:, :NV]
    mixed = summed[:, NV : 2 * NV]
    own = summed[:, 2 * NV : 3 * NV]
    square = summed[:, 3 * NV : 4 * NV]
    alpha_out[...] = alpha
    cross = dot_tn(alpha, mixed)
    cross_t = dot_tn(mixed, alpha)
    gram = square - cross - cross_t + dot_tn(alpha, dot(own, alpha))
    row = lax.broadcasted_iota(jnp.int32, (NV, 2 * NV), 0)
    lane = lax.broadcasted_iota(jnp.int32, (NV, 2 * NV), 1)
    unit = jnp.where(row + NV == lane, 1.0, 0.0).astype(F32)
    work = jnp.concatenate([gram, unit[:, NV:]], axis=1)
    for j in range(NV):
        pivot = jnp.sqrt(work[j : j + 1, j : j + 1])
        scaled = work[j : j + 1, :] / pivot
        factor = work[:, j : j + 1] / pivot
        work = jnp.where(row == j, scaled, jnp.where(row > j, work - factor * scaled, work))
    upper_out[...] = jnp.where(row <= lane, work, 0.0)[:, :NV]
    inverse = work[:, NV:]
    resid = rest[...] - dot_tn(alpha, current[...])
    block = dot(inverse, resid)
    following[...] = block
    if not last:
        narrow = block.astype(BF16)
        to_row, own = sent
        to_row[...] = jnp.broadcast_to(narrow[None], to_row.shape)
        own[...] = narrow


def advance(parts, rest, current, total, n_row, last):
    sub = current.shape[1]
    shapes = [
        jax.ShapeDtypeStruct((NV, NV), F32),
        jax.ShapeDtypeStruct((NV, NV), F32),
        jax.ShapeDtypeStruct(current.shape, F32),
    ]
    if not last:
        shapes.append(jax.ShapeDtypeStruct((n_row, NV, sub), BF16))
        shapes.append(jax.ShapeDtypeStruct((NV, sub), BF16))
    return pl.pallas_call(
        functools.partial(next_kernel, total, last),
        out_shape=tuple(shapes),
        in_specs=[VMEM] * 3,
        out_specs=(VMEM,) * len(shapes),
        compiler_params=PARAMS,
        name="next_block",
    )(parts, rest, current)


def swap(blocks, axis):
    return lax.all_to_all(blocks, axis, 0, 0, tiled=True)


def shards(tiles, tile_row, tile_col, tile_count, block, previous, coupling):
    slots = tiles.shape[0]
    sub = block.shape[1]
    n_row = lax.axis_size("row")
    n_col = lax.axis_size("col")
    total = float(sub * n_row * n_col)
    squares = tiles.reshape(slots, TILE, TILE)
    current, prior, beta = (block, previous, coupling)
    narrow = current.astype(BF16)
    to_row = jnp.broadcast_to(narrow[None], (n_row, NV, sub))
    found = []
    for step in range(STEPS):
        last = step == STEPS - 1
        band = swap(to_row, "row")
        message = front(tile_row, tile_col, tile_count, squares, band, narrow, n_col)
        moved = swap(message, "col")
        partial, owned = back(tile_row, tile_col, tile_count, squares, moved, n_row)
        returned = swap(partial, "row")
        rest, sums = local(owned, returned, current, prior, beta, n_row)
        sums = spread(swap(sums, "row"), n_col)
        parts = swap(sums, "col")
        alpha, upper, following, *sent = advance(parts, rest, current, total, n_row, last)
        found.append(alpha)
        if not last:
            to_row, narrow = sent
        prior, current, beta = (current, following, upper)
    return (current, jnp.stack(found))


def solution(mesh):
    in_specs = (
        P(("row", "col"), None),
        P(("row", "col")),
        P(("row", "col")),
        P(("row", "col")),
        P(None, ("row", "col")),
        P(None, ("row", "col")),
        P(),
    )
    out_specs = (P(None, ("row", "col")), P())
    return jax.shard_map(shards, mesh=mesh, in_specs=in_specs, out_specs=out_specs, check_vma=False)
```

time: 255 us -> 226 us (0.89)
  blocking collectives: 200 us -> 179 us
  waiting for transfers between devices: 12.9 us -> 0.93 us
  Pallas kernels: 16.2 us -> 23.4 us
  other arithmetic: 4.8 us -> 1.32 us
    all_to_all x11 -> x9, blocking collectives: 200 us -> 179 us  [swap(): return lax.all_to_all(blocks, axis, 0, 0, tiled=True)]
    all_to_all x1, waiting for transfers between devices: 12.9 us -> 0.93 us  [swap(): return lax.all_to_all(blocks, axis, 0, 0, tiled=True)]
    pallas_call x4 -> x6, Pallas kernels: 11.8 us -> 18.8 us  [the longest x2 9.68 us: back(): pl.pallas_call(back_kernel, out_shape=(jax.ShapeDtypeStruct((n_row, NV, s...]
    concatenate x1 -> x0, other arithmetic: 3.39 us -> none  [shards(): squares = jnp.concatenate([squares, squares], axis=2)]
  transfers between devices with their start and end apart: 1 -> 1, of which waited for: 1 -> 1; matrix products, arithmetic and copies ran while one was open for 3% -> 2% of each run, Pallas kernels for 0% -> 0%
where the time goes in v2:
time: 226 us; the launch traced here: 225 us
  blocking collectives  179 us (79%)
  Pallas kernels  23.4 us (10%)
  starting transfers between devices  13.8 us (6%)
  local copies, waits for them, and re-layouts  5.29 us (2%)
    all_to_all x9, blocking collectives, swap(): return lax.all_to_all(blocks, axis, 0, 0, tiled=True)  179 us
    all_to_all x1, starting transfers between devices, swap(): return lax.all_to_all(blocks, axis, 0, 0, tiled=True)  13.8 us
    pallas_call x2, Pallas kernels, back(): pl.pallas_call(back_kernel, out_shape=(jax.ShapeDtypeStruct((n_row, NV, s...  9.68 us
    pallas_call x2, Pallas kernels, front(): pl.pallas_call(front_kernel, out_shape=jax.ShapeDtypeStruct((n_col, 2 * N...  9.08 us
  transfers between devices with their start and end apart: 1, of which 1 were waited for; matrix products, arithmetic and copies ran while one was open for 2% of the time, Pallas kernels for 0%

profile of v2, /device:TPU:1, one launch (start us, length us, event | category | flops | bytes accessed | tf_op | source)
XLA Modules:
  0.0 225.1 jit_solution(4563432965511557656)
XLA Ops:
  0.6 0.7 convert_element_type.3.narrow
  1.4 0.7 broadcast_in_dim.2
  2.0 13.8 %all-to-all-start = ((bf16[16,8,512]{2,1,0:T(8,128)(2,1)}), bf16[16,8,512]{2,1,0:T(8,128)(2,1)S(1)}, u32[]{:S(2)}, u32[]{:S(2)}) async-start(bf16[16,8,512]{2,1,0:T(8,128)(2,1)} %broadcast_in_dim.2), calls=%async_computation | async-start | bytes 262144 | tf_op jit(solution)/shard_map/all_to_all | solution.py:245
  16.5 1.6 copy.9
  18.1 0.0 copy-start.2
  18.1 0.0 copy-start.3
  18.1 3.0 %copy.13.tiles = bf16[128,64,64]{2,1,0:T(8,128)(2,1)S(1)} copy(bf16[128,64,64]{0,2,1:T(8,128)(2,1)S(1)} %bitcast.5) | data formatting | bytes 2097152 | tf_op jit(solution)/shard_map/reshape | solution.py:254
  21.1 0.9 all-to-all-done.band
  22.1 0.0 copy-done.2
  22.1 0.0 copy-done.3
  22.1 4.5 %front_tiles.2 = bf16[48,16,512]{2,1,0:T(8,128)(2,1)S(1)} custom-call(s32[128]{0:T(128)S(1)} %copy-done.2, s32[128]{0:T(128)S(1)} %copy-done.3, s32[1]{0:T(128)S(6)} %copy.14.count, bf16[128,64,64]{2,1,0:T(8,128)(2,1)S(1)} %copy.13.tiles, bf16[16,8,512]{2,1,0:T(8,128)(2,1)S(1)} %all-to-all-done.band, bf16[8,512]{1,0:T(8,128)(2,1)S(1)} %convert_element_type.3.narrow), custom_call_target="tpu_custom_call" | custom-call | tf_op jit(solution)/shard_map/front_tiles/pallas_call | solution.py:88
  26.6 44.6 %all_to_all.50.moved = bf16[48,16,512]{2,1,0:T(8,128)(2,1)S(1)} all-to-all(bf16[48,16,512]{2,1,0:T(8,128)(2,1)S(1)} %front_tiles.2), channel_id=1, replica_groups=mesh['row'=16,'col'=48] {'col'}, dimensions={0} | all-to-all | bytes 1572864 | tf_op jit(solution)/shard_map/all_to_all | solution.py:245
  71.2 0.0 copy-start
  71.2 4.8 %back_tiles.2 = (f32[16,8,512]{2,1,0:T(8,128)S(1)}, f32[8,512]{1,0:T(8,128)S(1)}) custom-call(s32[128]{0:T(128)S(1)} %copy-done.2, s32[128]{0:T(128)S(1)} %copy-done.3, s32[1]{0:T(128)S(6)} %copy.14.count, bf16[128,64,64]{2,1,0:T(8,128)(2,1)S(1)} %copy.13.tiles, bf16[48,16,512]{2,1,0:T(8,128)(2,1)S(1)} %all_to_all.50.moved), custom_call_target="tpu_custom_call" | custom-call | tf_op jit(solution)/shard_map/back_tiles/pallas_call | solution.py:127
  76.0 15.4 %all_to_all.51.returned = f32[16,8,512]{2,1,0:T(8,128)S(1)} all-to-all(f32[16,8,512]{2,1,0:T(8,128)S(1)} %get-tuple-element.18), channel_id=1, replica_groups=mesh['row'=16,'col'=48] {'row'}, dimensions={0} | all-to-all | bytes 524288 | tf_op jit(solution)/shard_map/all_to_all | solution.py:245
  91.4 0.0 copy-done
  91.4 0.0 copy-done.1
  91.4 0.0 copy-done.4
  91.4 0.5 local_sums.2
  91.8 9.2 %all_to_all.52.parts = f32[16,2,128]{2,1,0:T(2,128)S(1)} all-to-all(f32[16,2,128]{2,1,0:T(2,128)S(1)} %get-tuple-element.19), channel_id=1, replica_groups=mesh['row'=16,'col'=48] {'row'}, dimensions={0} | all-to-all | bytes 32768 | tf_op jit(solution)/shard_map/all_to_all | solution.py:245
  101.1 20.2 %all_to_all.53.parts = f32[48,2,128]{2,1,0:T(2,128)S(1)} all-to-all(f32[48,2,128]{2,1,0:T(2,128)S(1)} %spread_sums.2), channel_id=1, replica_groups=mesh['row'=16,'col'=48] {'col'}, dimensions={0} | all-to-all | bytes 98304 | tf_op jit(solution)/shard_map/all_to_all | solution.py:245
  121.3 1.5 next_block.2
  122.9 10.5 %all_to_all.54.band = bf16[16,8,512]{2,1,0:T(8,128)(2,1)S(1)} all-to-all(bf16[16,8,512]{2,1,0:T(8,128)(2,1)S(1)} %get-tuple-element.21), channel_id=1, replica_groups=mesh['row'=16,'col'=48] {'row'}, dimensions={0} | all-to-all | bytes 262144 | tf_op jit(solution)/shard_map/all_to_all | solution.py:245
  133.3 4.5 %front_tiles.3 = bf16[48,16,512]{2,1,0:T(8,128)(2,1)S(1)} custom-call(s32[128]{0:T(128)S(1)} %copy-done.2, s32[128]{0:T(128)S(1)} %copy-done.3, s32[1]{0:T(128)S(6)} %copy.14.count, bf16[128,64,64]{2,1,0:T(8,128)(2,1)S(1)} %copy.13.tiles, bf16[16,8,512]{2,1,0:T(8,128)(2,1)S(1)} %all_to_all.54.band, bf16[8,512]{1,0:T(8,128)(2,1)S(1)} %get-tuple-element.22.narrow), custom_call_target="tpu_custom_call" | custom-call | tf_op jit(solution)/shard_map/front_tiles/pallas_call | solution.py:88
  137.9 36.3 %all_to_all.55.moved = bf16[48,16,512]{2,1,0:T(8,128)(2,1)S(1)} all-to-all(bf16[48,16,512]{2,1,0:T(8,128)(2,1)S(1)} %front_tiles.3), channel_id=1, replica_groups=mesh['row'=16,'col'=48] {'col'}, dimensions={0} | all-to-all | bytes 1572864 | tf_op jit(solution)/shard_map/all_to_all | solution.py:245
  174.2 4.8 %back_tiles.3 = (f32[16,8,512]{2,1,0:T(8,128)S(1)}, f32[8,512]{1,0:T(8,128)S(1)}) custom-call(s32[128]{0:T(128)S(1)} %copy-done.2, s32[128]{0:T(128)S(1)} %copy-done.3, s32[1]{0:T(128)S(6)} %copy.14.count, bf16[128,64,64]{2,1,0:T(8,128)(2,1)S(1)} %copy.13.tiles, bf16[48,16,512]{2,1,0:T(8,128)(2,1)S(1)} %all_to_all.55.moved), custom_call_target="tpu_custom_call" | custom-call | tf_op jit(solution)/shard_map/back_tiles/pallas_call | solution.py:127
  179.0 13.2 %all_to_all.56.returned = f32[16,8,512]{2,1,0:T(8,128)S(1)} all-to-all(f32[16,8,512]{2,1,0:T(8,128)S(1)} %get-tuple-element.24), channel_id=1, replica_groups=mesh['row'=16,'col'=48] {'row'}, dimensions={0} | all-to-all | bytes 524288 | tf_op jit(solution)/shard_map/all_to_all | solution.py:245
  192.2 0.4 local_sums.3
  192.7 9.2 %all_to_all.57.parts = f32[16,2,128]{2,1,0:T(2,128)S(1)} all-to-all(f32[16,2,128]{2,1,0:T(2,128)S(1)} %get-tuple-element.27), channel_id=1, replica_groups=mesh['row'=16,'col'=48] {'row'}, dimensions={0} | all-to-all | bytes 32768 | tf_op jit(solution)/shard_map/all_to_all | solution.py:245
  202.0 20.4 %all_to_all.58.parts = f32[48,2,128]{2,1,0:T(2,128)S(1)} all-to-all(f32[48,2,128]{2,1,0:T(2,128)S(1)} %spread_sums.3), channel_id=1, replica_groups=mesh['row'=16,'col'=48] {'col'}, dimensions={0} | all-to-all | bytes 98304 | tf_op jit(solution)/shard_map/all_to_all | solution.py:245
  222.3 2.1 next_block.3
  224.5 0.6 pad_maximum_fusion
  (4 shorter events, 0.1 us)
Async XLA Ops:
  2.0 20.0 %all-to-all-start = ((bf16[16,8,512]{2,1,0:T(8,128)(2,1)}), bf16[16,8,512]{2,1,0:T(8,128)(2,1)S(1)}, u32[]{:S(2)}, u32[]{:S(2)}) async-start(bf16[16,8,512]{2,1,0:T(8,128)(2,1)} %broadcast_in_dim.2), calls=%async_computation | async-start | bytes 262144 | tf_op jit(solution)/shard_map/all_to_all | solution.py:245
  18.1 4.0 %copy-start.2 = (s32[128]{0:T(128)S(1)}, s32[128]{0:T(128)}, u32[]{:S(2)}) copy-start(s32[128]{0:T(128)} %rows.7) | copy-start | bytes 1540
  18.1 3.9 %copy-start.3 = (s32[128]{0:T(128)S(1)}, s32[128]{0:T(128)}, u32[]{:S(2)}) copy-start(s32[128]{0:T(128)} %cols.7) | copy-start | bytes 1540
  71.2 20.2 %copy-start = (f32[8,512]{1,0:T(8,128)S(1)}, f32[8,512]{1,0:T(8,128)}, u32[]{:S(2)}) copy-start(f32[8,512]{1,0:T(8,128)} %prior.3) | copy-start | bytes 49156
  71.2 20.2 %copy-start.1 = (f32[8,512]{1,0:T(8,128)S(1)}, f32[8,512]{1,0:T(8,128)}, u32[]{:S(2)}) copy-start(f32[8,512]{1,0:T(8,128)} %prior.2) | copy-start | bytes 49156
  71.2 20.2 %copy-start.4 = (f32[8,8]{1,0:T(8,128)S(1)}, f32[8,8]{1,0:T(8,128)}, u32[]{:S(2)}) copy-start(f32[8,8]{1,0:T(8,128)} %beta.1) | copy-start | bytes 772

commit v3 on v2

v3 whole, which is shorter than its diff:
```python
import functools

import jax
import jax.numpy as jnp
from jax import lax
from jax.experimental import pallas as pl
from jax.experimental.pallas import tpu as pltpu
from jax.sharding import PartitionSpec as P

TILE = 64
NV = 8
STEPS = 2
LANES = 128
GROUP = 32
DEPTH = 12
BOTH = ("row", "col")
HIGH = lax.Precision.HIGHEST
F32 = jnp.float32
BF16 = jnp.bfloat16
VMEM = pl.BlockSpec(memory_space=pltpu.VMEM)
SMEM = pl.BlockSpec(memory_space=pltpu.SMEM)
PARAMS = pltpu.CompilerParams(vmem_limit_bytes=40 * 1024 * 1024)


def dot(left, right):
    return jnp.dot(left, right, precision=HIGH, preferred_element_type=F32)


def dot_t(left, right):
    return lax.dot_general(
        left, right, (((1,), (1,)), ((), ())), precision=HIGH, preferred_element_type=F32
    )


def dot_tn(left, right):
    return lax.dot_general(
        left, right, (((0,), (0,)), ((), ())), precision=HIGH, preferred_element_type=F32
    )


def lane_half():
    return lax.broadcasted_iota(jnp.int32, (NV, LANES), 1) // TILE


def narrowed(pair, mask):
    held = jnp.where(mask, pair, 0.0)
    return (held + pltpu.roll(held, TILE, 1))[:, :TILE].astype(BF16)


def both_halves(product, mask):
    return jnp.where(mask, jnp.concatenate([product, product], axis=1), 0.0)


def to_pairs(segments, pairs):
    count, _, sub = segments.shape
    per = sub // LANES
    for segment in range(count):
        held = segments[segment, :NV].astype(F32)
        for part in range(per):
            pairs[segment * per + part] = held[:, part * LANES : (part + 1) * LANES]
    pairs[count * per] = jnp.zeros((NV, LANES), F32)


def segment_of(pairs, segment, per):
    parts = [pairs[segment * per + part] for part in range(per)]
    return jnp.concatenate(parts, axis=1)


def pair_scratch(count, sub):
    return pltpu.VMEM((count * sub // LANES + 1, NV, LANES), F32)


def accumulate(reads, writes, tiles, pairs, sums, product):
    half = lane_half()
    sums[...] = jnp.zeros_like(sums)

    def group(g, carry):
        updates = []
        for u in range(GROUP):
            k = g * GROUP + u
            read, write = reads[k], writes[k]
            picked = narrowed(pairs[lax.shift_right_logical(read, 1)], half == (read & 1))
            out = both_halves(product(picked, tiles[k]), half == (write & 1))
            updates.append((lax.shift_right_logical(write, 1), out))
        for pair, out in updates:
            sums[pair] += out
        return carry

    lax.fori_loop(0, tiles.shape[0] // GROUP, group, 0)


def front_kernel(rows, cols, tiles, band, narrow, message, band_pairs, sums):
    to_pairs(band, band_pairs)

    def product(picked, tile):
        return lax.dot_general(
            picked, tile, (((1,), (1,)), ((), ())), preferred_element_type=F32
        )

    accumulate(cols, rows, tiles, band_pairs, sums, product)
    per = message.shape[2] // LANES
    own = narrow[...]
    for segment in range(message.shape[0]):
        partial = segment_of(sums, segment, per).astype(BF16)
        message[segment] = jnp.concatenate([own, partial], axis=0)


def front(rows, cols, tiles, band, narrow, n_col):
    n_row, _, sub = band.shape
    return pl.pallas_call(
        front_kernel,
        out_shape=jax.ShapeDtypeStruct((n_col, 2 * NV, sub), BF16),
        in_specs=[SMEM, SMEM, VMEM, VMEM, VMEM],
        out_specs=VMEM,
        scratch_shapes=[pair_scratch(n_row, sub), pair_scratch(n_col, sub)],
        compiler_params=PARAMS,
        name="front_tiles",
    )(rows, cols, tiles, band, narrow)


def back_kernel(rows, cols, tiles, moved, back, owned, across_pairs, sums):
    to_pairs(moved, across_pairs)
    owned[...] = jnp.sum(moved[:, NV:].astype(F32), axis=0)

    def product(picked, tile):
        return jnp.dot(picked, tile, preferred_element_type=F32)

    accumulate(rows, cols, tiles, across_pairs, sums, product)
    per = back.shape[2] // LANES
    for segment in range(back.shape[0]):
        back[segment] = segment_of(sums, segment, per)


def back(rows, cols, tiles, moved, n_row):
    n_col, _, sub = moved.shape
    return pl.pallas_call(
        back_kernel,
        out_shape=(
            jax.ShapeDtypeStruct((n_row, NV, sub), F32),
            jax.ShapeDtypeStruct((NV, sub), F32),
        ),
        in_specs=[SMEM, SMEM, VMEM, VMEM],
        out_specs=(VMEM, VMEM),
        scratch_shapes=[pair_scratch(n_col, sub), pair_scratch(n_row, sub)],
        compiler_params=PARAMS,
        name="back_tiles",
    )(rows, cols, tiles, moved)


def local_kernel(owned, returned, current, prior, beta, ahead, sums):
    image = owned[...] + jnp.sum(returned[...], axis=0)
    now = current[...]
    rest = image - dot(beta[...], prior[...])
    ahead[...] = rest
    left = jnp.concatenate([now, rest], axis=0)
    right = jnp.concatenate([image, rest, now], axis=0)
    inner = dot_t(left, right)
    blocks = jnp.concatenate([inner[:NV], inner[NV:, NV : 2 * NV]], axis=1)
    packed = [
        jnp.concatenate([blocks[v : v + 1] for v in range(part, part + 4)], axis=1)
        for part in (0, 4)
    ]
    one = jnp.concatenate(packed, axis=0)
    sums[...] = jnp.broadcast_to(one[None], sums.shape)


def local(owned, returned, current, prior, beta, copies):
    return pl.pallas_call(
        local_kernel,
        out_shape=(
            jax.ShapeDtypeStruct(current.shape, F32),
            jax.ShapeDtypeStruct((copies, 2, LANES), F32),
        ),
        in_specs=[VMEM] * 5,
        out_specs=(VMEM, VMEM),
        compiler_params=PARAMS,
        name="local_sums",
    )(owned, returned, current, prior, beta)


def spread_kernel(parts, sums):
    one = jnp.sum(parts[...], axis=0)
    sums[...] = jnp.broadcast_to(one[None], sums.shape)


def spread(parts, copies):
    return pl.pallas_call(
        spread_kernel,
        out_shape=jax.ShapeDtypeStruct((copies, 2, LANES), F32),
        in_specs=[VMEM],
        out_specs=VMEM,
        compiler_params=PARAMS,
        name="spread_sums",
    )(parts)


def next_kernel(total, step, last, parts, rest, current, found, alphas, upper_out, following, *sent):
    packed = jnp.sum(parts[...], axis=0) / total
    width = LANES // 4
    summed = jnp.concatenate(
        [packed[v // 4 : v // 4 + 1, v % 4 * width : (v % 4 + 1) * width] for v in range(NV)],
        axis=0,
    )
    alpha = summed[:, :NV]
    mixed = summed[:, NV : 2 * NV]
    own = summed[:, 2 * NV : 3 * NV]
    square = summed[:, 3 * NV : 4 * NV]
    alphas[...] = found[...]
    alphas[step] = alpha
    cross = dot_tn(alpha, mixed)
    cross_t = dot_tn(mixed, alpha)
    gram = square - cross - cross_t + dot_tn(alpha, dot(own, alpha))
    row = lax.broadcasted_iota(jnp.int32, (NV, 2 * NV), 0)
    lane = lax.broadcasted_iota(jnp.int32, (NV, 2 * NV), 1)
    unit = jnp.where(row + NV == lane, 1.0, 0.0).astype(F32)
    work = jnp.concatenate([gram, unit[:, NV:]], axis=1)
    for j in range(NV):
        pivot = jnp.sqrt(work[j : j + 1, j : j + 1])
        scaled = work[j : j + 1, :] / pivot
        factor = work[:, j : j + 1] / pivot
        work = jnp.where(row == j, scaled, jnp.where(row > j, work - factor * scaled, work))
    upper_out[...] = jnp.where(row <= lane, work, 0.0)[:, :NV]
    inverse = work[:, NV:]
    resid = rest[...] - dot_tn(alpha, current[...])
    block = dot(inverse, resid)
    following[...] = block
    if not last:
        narrow = block.astype(BF16)
        to_row, own = sent
        to_row[...] = jnp.broadcast_to(narrow[None], to_row.shape)
        own[...] = narrow


def advance(parts, rest, current, found, total, n_row, step, last):
    sub = current.shape[1]
    shapes = [
        jax.ShapeDtypeStruct(found.shape, F32),
        jax.ShapeDtypeStruct((NV, NV), F32),
        jax.ShapeDtypeStruct(current.shape, F32),
    ]
    if not last:
        shapes.append(jax.ShapeDtypeStruct((n_row, NV, sub), BF16))
        shapes.append(jax.ShapeDtypeStruct((NV, sub), BF16))
    return pl.pallas_call(
        functools.partial(next_kernel, total, step, last),
        out_shape=tuple(shapes),
        in_specs=[VMEM] * 4,
        out_specs=(VMEM,) * len(shapes),
        compiler_params=PARAMS,
        name="next_block",
    )(parts, rest, current, found)


def swap(blocks, axis, groups=None):
    return lax.all_to_all(blocks, axis, 0, 0, tiled=True, axis_index_groups=groups)


def planes_and_lines(n_row, n_col):
    depth = DEPTH if n_col % DEPTH == 0 else n_col
    lines = [
        [row * n_col + high * depth + z for z in range(depth)]
        for row in range(n_row)
        for high in range(n_col // depth)
    ]
    planes = [[line[z] for line in lines] for z in range(depth)]
    return planes, lines


def shards(tiles, tile_row, tile_col, tile_count, block, previous, coupling):
    slots = tiles.shape[0]
    sub = block.shape[1]
    n_row = lax.axis_size("row")
    n_col = lax.axis_size("col")
    total = float(sub * n_row * n_col)
    squares = tiles.reshape(slots, TILE, TILE)
    current, prior, beta = (block, previous, coupling)
    narrow = current.astype(BF16)
    to_row = jnp.broadcast_to(narrow[None], (n_row, NV, sub))
    live = lax.iota(jnp.int32, slots) < tile_count[0]
    rows = jnp.where(live, tile_row, n_col * sub // TILE)
    cols = jnp.where(live, tile_col, n_row * sub // TILE)
    planes, lines = planes_and_lines(n_row, n_col)
    found = jnp.zeros((STEPS, NV, NV), F32)
    for step in range(STEPS):
        last = step == STEPS - 1
        band = swap(to_row, "row")
        moved = swap(front(rows, cols, squares, band, narrow, n_col), "col")
        partial, owned = back(rows, cols, squares, moved, n_row)
        returned = swap(partial, "row")
        rest, sums = local(owned, returned, current, prior, beta, len(planes[0]))
        sums = spread(swap(sums, BOTH, planes), len(lines[0]))
        parts = swap(sums, BOTH, lines)
        found, upper, following, *sent = advance(
            parts, rest, current, found, total, n_row, step, last
        )
        if not last:
            to_row, narrow = sent
        prior, current, beta = (current, following, upper)
    return (current, found)


def solution(mesh):
    in_specs = (
        P(("row", "col"), None),
        P(("row", "col")),
        P(("row", "col")),
        P(("row", "col")),
        P(None, ("row", "col")),
        P(None, ("row", "col")),
        P(),
    )
    out_specs = (P(None, ("row", "col")), P())
    return jax.shard_map(shards, mesh=mesh, in_specs=in_specs, out_specs=out_specs, check_vma=False)
```

time: 226 us -> 215 us (0.951)
  Pallas kernels: 23.4 us -> 15 us
    pallas_call x2, Pallas kernels: 9.68 us -> 4.74 us  [back(): pl.pallas_call(back_kernel, out_shape=(jax.ShapeDtypeStruct((n_row, NV, s...]
    pallas_call x2, Pallas kernels: 9.08 us -> 5.59 us  [front(): pl.pallas_call(front_kernel, out_shape=jax.ShapeDtypeStruct((n_col, 2 * N...]
where the time goes in v3:
time: 215 us; the launch traced here: 214 us
  blocking collectives  177 us (82%)
  Pallas kernels  15 us (7%)
  starting transfers between devices  13.8 us (6%)
  local copies, waits for them, and re-layouts  5.29 us (2%)
    all_to_all x9, blocking collectives, swap(): lax.all_to_all(blocks, axis, 0, 0, tiled=True, axis_index_groups=groups)  177 us
    all_to_all x1, starting transfers between devices, swap(): lax.all_to_all(blocks, axis, 0, 0, tiled=True, axis_index_groups=groups)  13.8 us
    pallas_call x2, Pallas kernels, front(): pl.pallas_call(front_kernel, out_shape=jax.ShapeDtypeStruct((n_col, 2 * N...  5.59 us
    pallas_call x2, Pallas kernels, back(): pl.pallas_call(back_kernel, out_shape=(jax.ShapeDtypeStruct((n_row, NV, s...  4.74 us
  transfers between devices with their start and end apart: 1, of which 1 were waited for; matrix products, arithmetic and copies ran while one was open for 2% of the time, Pallas kernels for 0%

profile of v3, /device:TPU:1, one launch (start us, length us, event | category | flops | bytes accessed | tf_op | source)
XLA Modules:
  0.0 214.0 jit_solution(3785298666871216642)
XLA Ops:
  0.6 0.7 convert_element_type.3.narrow
  1.4 0.7 broadcast_in_dim.18
  2.0 13.8 %all-to-all-start = ((bf16[16,8,512]{2,1,0:T(8,128)(2,1)}), bf16[16,8,512]{2,1,0:T(8,128)(2,1)S(1)}, u32[]{:S(2)}, u32[]{:S(2)}) async-start(bf16[16,8,512]{2,1,0:T(8,128)(2,1)} %broadcast_in_dim.18), calls=%async_computation | async-start | bytes 262144 | tf_op jit(solution)/shard_map/all_to_all | solution.py:255
  16.5 1.6 copy.9
  18.1 0.0 copy-start.3
  18.1 0.0 copy-start.4
  18.1 3.0 %copy.13.tiles = bf16[128,64,64]{2,1,0:T(8,128)(2,1)S(1)} copy(bf16[128,64,64]{0,2,1:T(8,128)(2,1)S(1)} %bitcast.3) | data formatting | bytes 2097152 | tf_op jit(solution)/shard_map/reshape | solution.py:275
  21.1 0.0 copy-done.3
  21.1 0.0 copy-done.4
  21.2 0.9 all-to-all-done.band
  22.1 2.8 %front_tiles.2 = bf16[48,16,512]{2,1,0:T(8,128)(2,1)S(1)} custom-call(s32[128]{0:T(128)S(1)} %get-tuple-element.33.rows, s32[128]{0:T(128)S(1)} %get-tuple-element.32.cols, bf16[128,64,64]{2,1,0:T(8,128)(2,1)S(1)} %copy.13.tiles, bf16[16,8,512]{2,1,0:T(8,128)(2,1)S(1)} %all-to-all-done.band, bf16[8,512]{1,0:T(8,128)(2,1)S(1)} %convert_element_type.3.narrow), custom_call_target="tpu_custom_call" | custom-call | tf_op jit(solution)/shard_map/front_tiles/pallas_call | solution.py:110
  24.9 44.6 %all_to_all.50.moved = bf16[48,16,512]{2,1,0:T(8,128)(2,1)S(1)} all-to-all(bf16[48,16,512]{2,1,0:T(8,128)(2,1)S(1)} %front_tiles.2), channel_id=1, replica_groups=mesh['row'=16,'col'=48] {'col'}, dimensions={0} | all-to-all | bytes 1572864 | tf_op jit(solution)/shard_map/all_to_all | solution.py:255
  69.4 2.4 %back_tiles.2 = (f32[16,8,512]{2,1,0:T(8,128)S(1)}, f32[8,512]{1,0:T(8,128)S(1)}) custom-call(s32[128]{0:T(128)S(1)} %get-tuple-element.33.rows, s32[128]{0:T(128)S(1)} %get-tuple-element.32.cols, bf16[128,64,64]{2,1,0:T(8,128)(2,1)S(1)} %copy.13.tiles, bf16[48,16,512]{2,1,0:T(8,128)(2,1)S(1)} %all_to_all.50.moved), custom_call_target="tpu_custom_call" | custom-call | tf_op jit(solution)/shard_map/back_tiles/pallas_call | solution.py:136
  71.8 15.4 %all_to_all.51.returned = f32[16,8,512]{2,1,0:T(8,128)S(1)} all-to-all(f32[16,8,512]{2,1,0:T(8,128)S(1)} %get-tuple-element.18), channel_id=1, replica_groups=mesh['row'=16,'col'=48] {'row'}, dimensions={0} | all-to-all | bytes 524288 | tf_op jit(solution)/shard_map/all_to_all | solution.py:255
  87.2 0.0 copy-done
  87.2 0.0 copy-done.1
  87.2 0.0 copy-done.2
  87.2 0.5 local_sums.2
  87.7 16.5 %all_to_all.52.parts = f32[64,2,128]{2,1,0:T(2,128)S(1)} all-to-all(f32[64,2,128]{2,1,0:T(2,128)S(1)} %get-tuple-element.19), channel_id=1, replica_groups={{0,12,24,36,48,60,72,84,96,108,120,132,144,156,168,180,192,204,216,228,..., dimensions={0} | all-to-all | bytes 131072 | tf_op jit(solution)/shard_map/all_to_all | solution.py:255
  104.2 0.1 spread_sums.2
  104.3 11.6 %all_to_all.53.parts = f32[12,2,128]{2,1,0:T(2,128)S(1)} all-to-all(f32[12,2,128]{2,1,0:T(2,128)S(1)} %spread_sums.2), channel_id=1, replica_groups={{0,1,2,3,4,5,6,7,8,9,10,11},{12,13,14,15,16,17,18,19,20,21,22,23},{24,2..., dimensions={0} | all-to-all | bytes 24576 | tf_op jit(solution)/shard_map/all_to_all | solution.py:255
  115.9 1.5 next_block.2
  117.4 11.0 %all_to_all.54.band = bf16[16,8,512]{2,1,0:T(8,128)(2,1)S(1)} all-to-all(bf16[16,8,512]{2,1,0:T(8,128)(2,1)S(1)} %get-tuple-element.21), channel_id=1, replica_groups=mesh['row'=16,'col'=48] {'row'}, dimensions={0} | all-to-all | bytes 262144 | tf_op jit(solution)/shard_map/all_to_all | solution.py:255
  128.5 2.8 %front_tiles.3 = bf16[48,16,512]{2,1,0:T(8,128)(2,1)S(1)} custom-call(s32[128]{0:T(128)S(1)} %get-tuple-element.33.rows, s32[128]{0:T(128)S(1)} %get-tuple-element.32.cols, bf16[128,64,64]{2,1,0:T(8,128)(2,1)S(1)} %copy.13.tiles, bf16[16,8,512]{2,1,0:T(8,128)(2,1)S(1)} %all_to_all.54.band, bf16[8,512]{1,0:T(8,128)(2,1)S(1)} %get-tuple-element.22.narrow), custom_call_target="tpu_custom_call" | custom-call | tf_op jit(solution)/shard_map/front_tiles/pallas_call | solution.py:110
  131.3 35.9 %all_to_all.55.moved = bf16[48,16,512]{2,1,0:T(8,128)(2,1)S(1)} all-to-all(bf16[48,16,512]{2,1,0:T(8,128)(2,1)S(1)} %front_tiles.3), channel_id=1, replica_groups=mesh['row'=16,'col'=48] {'col'}, dimensions={0} | all-to-all | bytes 1572864 | tf_op jit(solution)/shard_map/all_to_all | solution.py:255
  167.2 2.4 %back_tiles.3 = (f32[16,8,512]{2,1,0:T(8,128)S(1)}, f32[8,512]{1,0:T(8,128)S(1)}) custom-call(s32[128]{0:T(128)S(1)} %get-tuple-element.33.rows, s32[128]{0:T(128)S(1)} %get-tuple-element.32.cols, bf16[128,64,64]{2,1,0:T(8,128)(2,1)S(1)} %copy.13.tiles, bf16[48,16,512]{2,1,0:T(8,128)(2,1)S(1)} %all_to_all.55.moved), custom_call_target="tpu_custom_call" | custom-call | tf_op jit(solution)/shard_map/back_tiles/pallas_call | solution.py:136
  169.6 13.3 %all_to_all.56.returned = f32[16,8,512]{2,1,0:T(8,128)S(1)} all-to-all(f32[16,8,512]{2,1,0:T(8,128)S(1)} %get-tuple-element.24), channel_id=1, replica_groups=mesh['row'=16,'col'=48] {'row'}, dimensions={0} | all-to-all | bytes 524288 | tf_op jit(solution)/shard_map/all_to_all | solution.py:255
  182.9 0.5 local_sums.3
  183.4 16.5 %all_to_all.57.parts = f32[64,2,128]{2,1,0:T(2,128)S(1)} all-to-all(f32[64,2,128]{2,1,0:T(2,128)S(1)} %get-tuple-element.27), channel_id=1, replica_groups={{0,12,24,36,48,60,72,84,96,108,120,132,144,156,168,180,192,204,216,228,..., dimensions={0} | all-to-all | bytes 131072 | tf_op jit(solution)/shard_map/all_to_all | solution.py:255
  199.9 0.1 spread_sums.3
  199.9 11.9 %all_to_all.58.parts = f32[12,2,128]{2,1,0:T(2,128)S(1)} all-to-all(f32[12,2,128]{2,1,0:T(2,128)S(1)} %spread_sums.3), channel_id=1, replica_groups={{0,1,2,3,4,5,6,7,8,9,10,11},{12,13,14,15,16,17,18,19,20,21,22,23},{24,2..., dimensions={0} | all-to-all | bytes 24576 | tf_op jit(solution)/shard_map/all_to_all | solution.py:255
  211.9 2.1 next_block.3
  (5 shorter events, 0.0 us)
Async XLA Ops:
  2.0 20.0 %all-to-all-start = ((bf16[16,8,512]{2,1,0:T(8,128)(2,1)}), bf16[16,8,512]{2,1,0:T(8,128)(2,1)S(1)}, u32[]{:S(2)}, u32[]{:S(2)}) async-start(bf16[16,8,512]{2,1,0:T(8,128)(2,1)} %broadcast_in_dim.18), calls=%async_computation | async-start | bytes 262144 | tf_op jit(solution)/shard_map/all_to_all | solution.py:255
  18.1 3.0 %copy-start.3 = (s32[128]{0:T(128)S(1)}, s32[128]{0:T(128)}, u32[]{:S(2)}) copy-start(s32[128]{0:T(128)} %param.9) | copy-start | bytes 1540
  18.1 3.0 %copy-start.4 = (s32[128]{0:T(128)S(1)}, s32[128]{0:T(128)}, u32[]{:S(2)}) copy-start(s32[128]{0:T(128)} %param.8) | copy-start | bytes 1540
  69.4 17.8 %copy-start = (f32[8,512]{1,0:T(8,128)S(1)}, f32[8,512]{1,0:T(8,128)}, u32[]{:S(2)}) copy-start(f32[8,512]{1,0:T(8,128)} %prior.3) | copy-start | bytes 49156
  69.4 17.8 %copy-start.1 = (f32[8,512]{1,0:T(8,128)S(1)}, f32[8,512]{1,0:T(8,128)}, u32[]{:S(2)}) copy-start(f32[8,512]{1,0:T(8,128)} %prior.2) | copy-start | bytes 49156
  69.4 17.8 %copy-start.2 = (f32[8,8]{1,0:T(8,128)S(1)}, f32[8,8]{1,0:T(8,128)}, u32[]{:S(2)}) copy-start(f32[8,8]{1,0:T(8,128)} %beta.1) | copy-start | bytes 772

commit v4 on v3

v4 whole, which is shorter than its diff:
```python
import functools

import jax
import jax.numpy as jnp
from jax import lax
from jax.experimental import pallas as pl
from jax.experimental.pallas import tpu as pltpu
from jax.sharding import PartitionSpec as P

TILE = 64
NV = 8
STEPS = 2
LANES = 128
GROUP = 32
DEPTH = 12
BOTH = ("row", "col")
AHEAD = (((1,), (1,)), ((), ()))
BEHIND = (((1,), (0,)), ((), ()))
HIGH = lax.Precision.HIGHEST
F32 = jnp.float32
BF16 = jnp.bfloat16
VMEM = pl.BlockSpec(memory_space=pltpu.VMEM)
SMEM = pl.BlockSpec(memory_space=pltpu.SMEM)
PARAMS = pltpu.CompilerParams(vmem_limit_bytes=40 * 1024 * 1024)


def dot(left, right):
    return jnp.dot(left, right, precision=HIGH, preferred_element_type=F32)


def dot_t(left, right):
    return lax.dot_general(
        left, right, (((1,), (1,)), ((), ())), precision=HIGH, preferred_element_type=F32
    )


def dot_tn(left, right):
    return lax.dot_general(
        left, right, (((0,), (0,)), ((), ())), precision=HIGH, preferred_element_type=F32
    )


def lane_half():
    return lax.broadcasted_iota(jnp.int32, (NV, LANES), 1) // TILE


def narrowed(pair, mask):
    held = jnp.where(mask, pair, 0.0)
    return (held + pltpu.roll(held, TILE, 1))[:, :TILE]


def pieces(value, count):
    found = []
    for _ in range(count):
        piece = value.astype(BF16)
        value = value - piece.astype(F32)
        found.append(piece)
    return found


def product_of(picked, tile, dims, split):
    if split == 1:
        return lax.dot_general(picked.astype(BF16), tile, dims, preferred_element_type=F32)
    both = jnp.concatenate(pieces(picked, 2), axis=0)
    out = lax.dot_general(both, tile, dims, preferred_element_type=F32)
    return out[:NV] + out[NV:]


def both_halves(product, mask):
    return jnp.where(mask, jnp.concatenate([product, product], axis=1), 0.0)


def mix(coefficients, rows):
    out = coefficients[:, 0:1] * rows[0:1]
    for v in range(1, NV):
        out = out + coefficients[:, v : v + 1] * rows[v : v + 1]
    return out


def factor(gram):
    row = lax.broadcasted_iota(jnp.int32, (NV, 2 * NV), 0)
    lane = lax.broadcasted_iota(jnp.int32, (NV, 2 * NV), 1)
    unit = jnp.where(row + NV == lane, 1.0, 0.0).astype(F32)
    work = jnp.concatenate([gram, unit[:, NV:]], axis=1)
    for j in range(NV):
        pivot = jnp.sqrt(work[j : j + 1, j : j + 1])
        scaled = work[j : j + 1, :] / pivot
        column = work[:, j : j + 1] / pivot
        work = jnp.where(row == j, scaled, jnp.where(row > j, work - column * scaled, work))
    return jnp.where(row <= lane, work, 0.0)[:, :NV], work[:, NV:]


def factor_of_sums(summed):
    alpha = summed[:, :NV]
    mixed = summed[:, NV : 2 * NV]
    own = summed[:, 2 * NV : 3 * NV]
    square = summed[:, 3 * NV : 4 * NV]
    gram = square - dot_tn(alpha, mixed) - dot_tn(mixed, alpha) + dot_tn(alpha, dot(own, alpha))
    return (alpha, *factor(gram))


def identity():
    row = lax.broadcasted_iota(jnp.int32, (NV, NV), 0)
    lane = lax.broadcasted_iota(jnp.int32, (NV, NV), 1)
    return jnp.where(row == lane, 1.0, 0.0).astype(F32)


def put_pairs(held, segment, pairs):
    per = held.shape[1] // LANES
    for part in range(per):
        pairs[segment * per + part] = held[:, part * LANES : (part + 1) * LANES]


def end_pairs(pairs):
    pairs[pairs.shape[0] - 1] = jnp.zeros((NV, LANES), F32)


def to_pairs(segments, pairs):
    for segment in range(segments.shape[0]):
        put_pairs(segments[segment, :NV].astype(F32), segment, pairs)
    end_pairs(pairs)


def segment_of(pairs, segment, per):
    parts = [pairs[segment * per + part] for part in range(per)]
    return jnp.concatenate(parts, axis=1)


def pair_scratch(count, sub):
    return pltpu.VMEM((count * sub // LANES + 1, NV, LANES), F32)


def accumulate(reads, writes, tiles, pairs, sums, dims, split=1):
    half = lane_half()
    sums[...] = jnp.zeros_like(sums)

    def group(g, carry):
        updates = []
        for u in range(GROUP):
            k = g * GROUP + u
            read, write = reads[k], writes[k]
            picked = narrowed(pairs[lax.shift_right_logical(read, 1)], half == (read & 1))
            out = both_halves(product_of(picked, tiles[k], dims, split), half == (write & 1))
            updates.append((lax.shift_right_logical(write, 1), out))
        for pair, out in updates:
            sums[pair] += out
        return carry

    lax.fori_loop(0, tiles.shape[0] // GROUP, group, 0)


def front_kernel(rows, cols, tiles, band, narrow, message, band_pairs, sums):
    to_pairs(band, band_pairs)
    accumulate(cols, rows, tiles, band_pairs, sums, AHEAD)
    per = message.shape[2] // LANES
    own = narrow[...]
    for segment in range(message.shape[0]):
        partial = segment_of(sums, segment, per).astype(BF16)
        message[segment] = jnp.concatenate([own, partial], axis=0)


def front(rows, cols, tiles, band, narrow, n_col):
    n_row, _, sub = band.shape
    return pl.pallas_call(
        front_kernel,
        out_shape=jax.ShapeDtypeStruct((n_col, 2 * NV, sub), BF16),
        in_specs=[SMEM, SMEM, VMEM, VMEM, VMEM],
        out_specs=VMEM,
        scratch_shapes=[pair_scratch(n_row, sub), pair_scratch(n_col, sub)],
        compiler_params=PARAMS,
        name="front_tiles",
    )(rows, cols, tiles, band, narrow)


def back_kernel(rows, cols, tiles, moved, back, owned, across_pairs, sums):
    to_pairs(moved, across_pairs)
    owned[...] = jnp.sum(moved[:, NV:].astype(F32), axis=0)
    accumulate(rows, cols, tiles, across_pairs, sums, BEHIND)
    per = back.shape[2] // LANES
    for segment in range(back.shape[0]):
        back[segment] = segment_of(sums, segment, per)


def back(rows, cols, tiles, moved, n_row):
    n_col, _, sub = moved.shape
    return pl.pallas_call(
        back_kernel,
        out_shape=(
            jax.ShapeDtypeStruct((n_row, NV, sub), F32),
            jax.ShapeDtypeStruct((NV, sub), F32),
        ),
        in_specs=[SMEM, SMEM, VMEM, VMEM],
        out_specs=(VMEM, VMEM),
        scratch_shapes=[pair_scratch(n_col, sub), pair_scratch(n_row, sub)],
        compiler_params=PARAMS,
        name="back_tiles",
    )(rows, cols, tiles, moved)


def rest_and_sums(owned, returned, current, prior, beta):
    image = owned[...] + jnp.sum(returned[...], axis=0)
    now = current[...]
    rest = image - dot(beta[...], prior[...])
    left = jnp.concatenate([now, rest], axis=0)
    right = jnp.concatenate([image, rest, now], axis=0)
    inner = dot_t(left, right)
    return rest, jnp.concatenate([inner[:NV], inner[NV:, NV : 2 * NV]], axis=1)


def local_kernel(owned, returned, current, prior, beta, ahead, sums):
    rest, blocks = rest_and_sums(owned, returned, current, prior, beta)
    ahead[...] = rest
    packed = [
        jnp.concatenate([blocks[v : v + 1] for v in range(part, part + 4)], axis=1)
        for part in (0, 4)
    ]
    one = jnp.concatenate(packed, axis=0)
    sums[...] = jnp.broadcast_to(one[None], sums.shape)


def local(owned, returned, current, prior, beta, copies):
    return pl.pallas_call(
        local_kernel,
        out_shape=(
            jax.ShapeDtypeStruct(current.shape, F32),
            jax.ShapeDtypeStruct((copies, 2, LANES), F32),
        ),
        in_specs=[VMEM] * 5,
        out_specs=(VMEM, VMEM),
        compiler_params=PARAMS,
        name="local_sums",
    )(owned, returned, current, prior, beta)


def carry_kernel(owned, returned, current, prior, beta, ahead, message):
    rest, blocks = rest_and_sums(owned, returned, current, prior, beta)
    ahead[...] = rest
    pad = jnp.zeros((NV, LANES - 4 * NV), F32)
    one = jnp.concatenate([rest, blocks, pad], axis=1)
    message[...] = jnp.broadcast_to(one[None], message.shape)


def carry(owned, returned, current, prior, beta, n_row):
    sub = current.shape[1]
    return pl.pallas_call(
        carry_kernel,
        out_shape=(
            jax.ShapeDtypeStruct(current.shape, F32),
            jax.ShapeDtypeStruct((n_row, NV, sub + LANES), F32),
        ),
        in_specs=[VMEM] * 5,
        out_specs=(VMEM, VMEM),
        compiler_params=PARAMS,
        name="local_carry",
    )(owned, returned, current, prior, beta)


def whiten_kernel(rows, cols, tiles, got, rest, message, band_pairs, sums):
    n_row = got.shape[0]
    sub = rest.shape[1]
    summed = jnp.sum(got[:, :, sub:], axis=0)[:, : 4 * NV]
    gram = summed[:, 3 * NV :] / float(n_row * sub)
    unit = identity()
    trace = jnp.sum(jnp.sum(gram * unit, axis=1, keepdims=True), axis=0, keepdims=True)
    upper, inverse = factor(gram + (trace * 1e-5 + 1e-30) * unit)
    lower = dot_tn(upper, unit)
    for segment in range(n_row):
        put_pairs(mix(inverse, got[segment, :, :sub]), segment, band_pairs)
    end_pairs(band_pairs)
    own = mix(inverse, rest[...]).astype(BF16)
    wide = jnp.concatenate([lower, jnp.zeros((NV, 3 * NV), F32)], axis=1)
    held = jnp.concatenate([summed, wide], axis=0)
    beside = jnp.concatenate(pieces(held, 3) + [jnp.zeros((2 * NV, 4 * NV), BF16)], axis=1)
    accumulate(cols, rows, tiles, band_pairs, sums, AHEAD)
    per = sub // LANES
    for segment in range(message.shape[0]):
        partial = segment_of(sums, segment, per).astype(BF16)
        both = jnp.concatenate([own, partial], axis=0)
        message[segment] = jnp.concatenate([both, beside], axis=1)


def whiten(rows, cols, tiles, got, rest, n_col):
    n_row = got.shape[0]
    sub = rest.shape[1]
    return pl.pallas_call(
        whiten_kernel,
        out_shape=jax.ShapeDtypeStruct((n_col, 2 * NV, sub + LANES), BF16),
        in_specs=[SMEM, SMEM, VMEM, VMEM, VMEM],
        out_specs=VMEM,
        scratch_shapes=[pair_scratch(n_row, sub), pair_scratch(n_col, sub)],
        compiler_params=PARAMS,
        name="whiten_tiles",
    )(rows, cols, tiles, got, rest)


def joined(held):
    width = 4 * NV
    return held[:, :width] + held[:, width : 2 * width] + held[:, 2 * width : 3 * width]


def settle_kernel(
    total, rows, cols, tiles, moved, before, owned_before, rest, current,
    back, owned, following, upper_out, alphas, across_pairs, sums,
):
    n_col = moved.shape[0]
    sub = rest.shape[1]
    summed = jnp.zeros((NV, LANES), F32)
    for segment in range(n_col):
        summed = summed + moved[segment, :NV, sub:].astype(F32)
    alpha, upper, inverse = factor_of_sums(joined(summed) / total)
    upper_out[...] = upper
    alphas[...] = jnp.zeros_like(alphas)
    alphas[0] = alpha
    turn = dot_t(inverse, alpha)
    following[...] = dot(inverse, rest[...] - dot_tn(alpha, current[...]))

    def settle(segment, gathered):
        held = moved[segment].astype(F32)
        past = before[segment].astype(F32)[:NV]
        lower = joined(held[NV:, sub:])[:, :NV]
        change = mix(inverse, lower)
        put_pairs(mix(change, held[:NV, :sub]) - mix(turn, past), segment, across_pairs)
        return gathered + mix(change, held[NV:, :sub])

    gathered = lax.fori_loop(0, n_col, settle, jnp.zeros((NV, sub), F32), unroll=4)
    owned[...] = gathered - mix(turn, owned_before[...])
    end_pairs(across_pairs)
    accumulate(rows, cols, tiles, across_pairs, sums, BEHIND, split=2)
    per = sub // LANES
    for segment in range(back.shape[0]):
        back[segment] = segment_of(sums, segment, per)


def settle(rows, cols, tiles, moved, before, owned_before, rest, current, total, n_row):
    n_col = moved.shape[0]
    sub = rest.shape[1]
    return pl.pallas_call(
        functools.partial(settle_kernel, total),
        out_shape=(
            jax.ShapeDtypeStruct((n_row, NV, sub), F32),
            jax.ShapeDtypeStruct((NV, sub), F32),
            jax.ShapeDtypeStruct((NV, sub), F32),
            jax.ShapeDtypeStruct((NV, NV), F32),
            jax.ShapeDtypeStruct((STEPS, NV, NV), F32),
        ),
        in_specs=[SMEM, SMEM] + [VMEM] * 6,
        out_specs=(VMEM,) * 5,
        scratch_shapes=[pair_scratch(n_col, sub), pair_scratch(n_row, sub)],
        compiler_params=PARAMS,
        name="settle_tiles",
    )(rows, cols, tiles, moved, before, owned_before, rest, current)


def spread_kernel(parts, sums):
    one = jnp.sum(parts[...], axis=0)
    sums[...] = jnp.broadcast_to(one[None], sums.shape)


def spread(parts, copies):
    return pl.pallas_call(
        spread_kernel,
        out_shape=jax.ShapeDtypeStruct((copies, 2, LANES), F32),
        in_specs=[VMEM],
        out_specs=VMEM,
        compiler_params=PARAMS,
        name="spread_sums",
    )(parts)


def last_kernel(total, parts, rest, current, found, alphas, following):
    packed = jnp.sum(parts[...], axis=0) / total
    width = LANES // 4
    summed = jnp.concatenate(
        [packed[v // 4 : v // 4 + 1, v % 4 * width : (v % 4 + 1) * width] for v in range(NV)],
        axis=0,
    )
    alpha, _, inverse = factor_of_sums(summed)
    alphas[...] = found[...]
    alphas[STEPS - 1] = alpha
    following[...] = dot(inverse, rest[...] - dot_tn(alpha, current[...]))


def last(parts, rest, current, found, total):
    return pl.pallas_call(
        functools.partial(last_kernel, total),
        out_shape=(
            jax.ShapeDtypeStruct(found.shape, F32),
            jax.ShapeDtypeStruct(current.shape, F32),
        ),
        in_specs=[VMEM] * 4,
        out_specs=(VMEM, VMEM),
        compiler_params=PARAMS,
        name="last_block",
    )(parts, rest, current, found)


def swap(blocks, axis, groups=None):
    return lax.all_to_all(blocks, axis, 0, 0, tiled=True, axis_index_groups=groups)


def planes_and_lines(n_row, n_col):
    depth = DEPTH if n_col % DEPTH == 0 else n_col
    lines = [
        [row * n_col + high * depth + z for z in range(depth)]
        for row in range(n_row)
        for high in range(n_col // depth)
    ]
    planes = [[line[z] for line in lines] for z in range(depth)]
    return planes, lines


def shards(tiles, tile_row, tile_col, tile_count, block, previous, coupling):
    slots = tiles.shape[0]
    sub = block.shape[1]
    n_row = lax.axis_size("row")
    n_col = lax.axis_size("col")
    total = float(sub * n_row * n_col)
    squares = tiles.reshape(slots, TILE, TILE)
    live = lax.iota(jnp.int32, slots) < tile_count[0]
    rows = jnp.where(live, tile_row, n_col * sub // TILE)
    cols = jnp.where(live, tile_col, n_row * sub // TILE)
    planes, lines = planes_and_lines(n_row, n_col)
    narrow = block.astype(BF16)

    band = swap(jnp.broadcast_to(narrow[None], (n_row, NV, sub)), "row")
    before = swap(front(rows, cols, squares, band, narrow, n_col), "col")
    partial, owned = back(rows, cols, squares, before, n_row)
    returned = swap(partial, "row")
    rest, message = carry(owned, returned, block, previous, coupling, n_row)

    got = swap(message, "row")
    moved = swap(whiten(rows, cols, squares, got, rest, n_col), "col")
    partial, owned, current, upper, found = settle(
        rows, cols, squares, moved, before, owned, rest, block, total, n_row
    )
    returned = swap(partial, "row")
    rest, sums = local(owned, returned, current, block, upper, len(planes[0]))
    sums = spread(swap(sums, BOTH, planes), len(lines[0]))
    parts = swap(sums, BOTH, lines)
    found, current = last(parts, rest, current, found, total)
    return (current, found)


def solution(mesh):
    in_specs = (
        P(("row", "col"), None),
        P(("row", "col")),
        P(("row", "col")),
        P(("row", "col")),
        P(None, ("row", "col")),
        P(None, ("row", "col")),
        P(),
    )
    out_specs = (P(None, ("row", "col")), P())
    return jax.shard_map(shards, mesh=mesh, in_specs=in_specs, out_specs=out_specs, check_vma=False)
```

time: 215 us -> 202 us (0.940)
  blocking collectives: 177 us -> 159 us
  Pallas kernels: 15 us -> 20.8 us
    all_to_all x9 -> x7, blocking collectives: 177 us -> 159 us  [swap(): lax.all_to_all(blocks, axis, 0, 0, tiled=True, axis_index_groups=groups)]
    pallas_call x2 -> x4, Pallas kernels: 3.6 us -> 15.1 us  [the longest x1 8.5 us: settle(): pl.pallas_call(functools.partial(settle_kernel, total), out_shape=(jax.Sh...]
    pallas_call x2 -> x1, Pallas kernels: 5.59 us -> 2.79 us  [front(): pl.pallas_call(front_kernel, out_shape=jax.ShapeDtypeStruct((n_col, 2 * N...]
    pallas_call x2 -> x1, Pallas kernels: 4.74 us -> 2.35 us  [back(): pl.pallas_call(back_kernel, out_shape=(jax.ShapeDtypeStruct((n_row, NV, s...]
where the time goes in v4:
time: 202 us
  blocking collectives  159 us (79%)
  Pallas kernels  20.8 us (10%)
  starting transfers between devices  13.8 us (7%)
  local copies, waits for them, and re-layouts  5.29 us (3%)
    all_to_all x7, blocking collectives, swap(): lax.all_to_all(blocks, axis, 0, 0, tiled=True, axis_index_groups=groups)  159 us
    all_to_all x1, starting transfers between devices, swap(): lax.all_to_all(blocks, axis, 0, 0, tiled=True, axis_index_groups=groups)  13.8 us
    pallas_call x1, Pallas kernels, settle(): pl.pallas_call(functools.partial(settle_kernel, total), out_shape=(jax.Sh...  8.5 us
    pallas_call x1, Pallas kernels, whiten(): pl.pallas_call(whiten_kernel, out_shape=jax.ShapeDtypeStruct((n_col, 2 *...  4.12 us
  transfers between devices with their start and end apart: 1, of which 1 were waited for; matrix products, arithmetic and copies ran while one was open for 2% of the time, Pallas kernels for 0%

profile of v4, /device:TPU:1, one launch (start us, length us, event | category | flops | bytes accessed | tf_op | source)
XLA Modules:
  0.0 201.5 jit_solution(15600906763991676264)
XLA Ops:
  0.6 0.7 convert_element_type.3.narrow
  1.4 0.7 broadcast_in_dim.15
  2.0 13.8 %all-to-all-start = ((bf16[16,8,512]{2,1,0:T(8,128)(2,1)}), bf16[16,8,512]{2,1,0:T(8,128)(2,1)S(1)}, u32[]{:S(2)}, u32[]{:S(2)}) async-start(bf16[16,8,512]{2,1,0:T(8,128)(2,1)} %broadcast_in_dim.15), calls=%async_computation | async-start | bytes 262144 | tf_op jit(solution)/shard_map/all_to_all | solution.py:398
  16.5 1.6 copy.9
  18.1 0.0 copy-start.3
  18.1 0.0 copy-start.4
  18.1 3.0 %copy.13.tiles = bf16[128,64,64]{2,1,0:T(8,128)(2,1)S(1)} copy(bf16[128,64,64]{0,2,1:T(8,128)(2,1)S(1)} %bitcast.3) | data formatting | bytes 2097152 | tf_op jit(solution)/shard_map/reshape | solution.py:418
  21.1 0.0 copy-done.3
  21.1 0.0 copy-done.4
  21.2 0.9 all-to-all-done.band
  22.1 2.8 %front_tiles.1 = bf16[48,16,512]{2,1,0:T(8,128)(2,1)S(1)} custom-call(s32[128]{0:T(128)S(1)} %get-tuple-element.29.rows, s32[128]{0:T(128)S(1)} %get-tuple-element.28.cols, bf16[128,64,64]{2,1,0:T(8,128)(2,1)S(1)} %copy.13.tiles, bf16[16,8,512]{2,1,0:T(8,128)(2,1)S(1)} %all-to-all-done.band, bf16[8,512]{1,0:T(8,128)(2,1)S(1)} %convert_element_type.3.narrow), custom_call_target="tpu_custom_call" | custom-call | tf_op jit(solution)/shard_map/front_tiles/pallas_call | solution.py:164
  24.9 44.6 %all_to_all.40.moved.before = bf16[48,16,512]{2,1,0:T(8,128)(2,1)S(1)} all-to-all(bf16[48,16,512]{2,1,0:T(8,128)(2,1)S(1)} %front_tiles.1), channel_id=1, replica_groups=mesh['row'=16,'col'=48] {'col'}, dimensions={0} | all-to-all | bytes 1572864 | tf_op jit(solution)/shard_map/all_to_all | solution.py:398
  69.4 0.0 copy-start
  69.4 0.0 copy-start.1
  69.4 0.0 copy-start.2
  69.4 2.3 %back_tiles.1 = (f32[16,8,512]{2,1,0:T(8,128)S(1)}, f32[8,512]{1,0:T(8,128)S(1)}) custom-call(s32[128]{0:T(128)S(1)} %get-tuple-element.29.rows, s32[128]{0:T(128)S(1)} %get-tuple-element.28.cols, bf16[128,64,64]{2,1,0:T(8,128)(2,1)S(1)} %copy.13.tiles, bf16[48,16,512]{2,1,0:T(8,128)(2,1)S(1)} %all_to_all.40.moved.before), custom_call_target="tpu_custom_call" | custom-call | tf_op jit(solution)/shard_map/back_tiles/pallas_call | solution.py:186
  71.8 15.3 %all_to_all.41.returned = f32[16,8,512]{2,1,0:T(8,128)S(1)} all-to-all(f32[16,8,512]{2,1,0:T(8,128)S(1)} %get-tuple-element.16), channel_id=1, replica_groups=mesh['row'=16,'col'=48] {'row'}, dimensions={0} | all-to-all | bytes 524288 | tf_op jit(solution)/shard_map/all_to_all | solution.py:398
  87.1 0.0 copy-done
  87.1 0.0 copy-done.1
  87.1 0.0 copy-done.2
  87.1 0.4 local_carry.1
  87.5 11.2 %all_to_all.42.got = f32[16,8,640]{2,1,0:T(8,128)S(1)} all-to-all(f32[16,8,640]{2,1,0:T(8,128)S(1)} %get-tuple-element.17), channel_id=1, replica_groups=mesh['row'=16,'col'=48] {'row'}, dimensions={0} | all-to-all | bytes 655360 | tf_op jit(solution)/shard_map/all_to_all | solution.py:398
  98.7 4.1 %whiten_tiles.1 = bf16[48,16,640]{2,1,0:T(8,128)(2,1)S(1)} custom-call(s32[128]{0:T(128)S(1)} %get-tuple-element.29.rows, s32[128]{0:T(128)S(1)} %get-tuple-element.28.cols, bf16[128,64,64]{2,1,0:T(8,128)(2,1)S(1)} %copy.13.tiles, f32[16,8,640]{2,1,0:T(8,128)S(1)} %all_to_all.42.got, f32[8,512]{1,0:T(8,128)S(1)} %get-tuple-element.18.rest), custom_call_target="tpu_custom_call" | custom-call | tf_op jit(solution)/shard_map/whiten_tiles/pallas_call | solution.py:285
  102.8 43.8 %all_to_all.43.moved = bf16[48,16,640]{2,1,0:T(8,128)(2,1)S(1)} all-to-all(bf16[48,16,640]{2,1,0:T(8,128)(2,1)S(1)} %whiten_tiles.1), channel_id=1, replica_groups=mesh['row'=16,'col'=48] {'col'}, dimensions={0} | all-to-all | bytes 1966080 | tf_op jit(solution)/shard_map/all_to_all | solution.py:398
  146.6 8.5 %settle_tiles.1 = (f32[16,8,512]{2,1,0:T(8,128)S(1)}, f32[8,512]{1,0:T(8,128)S(1)}, f32[8,512]{1,0:T(8,128)S(1)}, f32[8,8]{1,0:T(8,128)S(1)}, f32[2,8,8]{2,1,0:T(8,128)S(1)}) custom-call(s32[128]{0:T(128)S(1)} %get-tuple-element.29.rows, s32[128]{0:T(128)S(1)} %get-tuple-element.28.cols, bf16[128,64,64]{2,1,0:T(8,128)(2,1)S(1)} %copy.13.tiles, ...), custom_call_target="tpu_custom_call" | custom-call | tf_op jit(solution)/shard_map/settle_tiles/pallas_call | solution.py:337
  155.1 15.8 %all_to_all.44.returned = f32[16,8,512]{2,1,0:T(8,128)S(1)} all-to-all(f32[16,8,512]{2,1,0:T(8,128)S(1)} %get-tuple-element.20), channel_id=1, replica_groups=mesh['row'=16,'col'=48] {'row'}, dimensions={0} | all-to-all | bytes 524288 | tf_op jit(solution)/shard_map/all_to_all | solution.py:398
  170.9 0.5 local_sums.1
  171.4 15.9 %all_to_all.45.parts = f32[64,2,128]{2,1,0:T(2,128)S(1)} all-to-all(f32[64,2,128]{2,1,0:T(2,128)S(1)} %get-tuple-element.23), channel_id=1, replica_groups={{0,12,24,36,48,60,72,84,96,108,120,132,144,156,168,180,192,204,216,228,..., dimensions={0} | all-to-all | bytes 131072 | tf_op jit(solution)/shard_map/all_to_all | solution.py:398
  187.3 0.1 spread_sums.1
  187.4 12.0 %all_to_all.46.parts = f32[12,2,128]{2,1,0:T(2,128)S(1)} all-to-all(f32[12,2,128]{2,1,0:T(2,128)S(1)} %spread_sums.1), channel_id=1, replica_groups={{0,1,2,3,4,5,6,7,8,9,10,11},{12,13,14,15,16,17,18,19,20,21,22,23},{24,2..., dimensions={0} | all-to-all | bytes 24576 | tf_op jit(solution)/shard_map/all_to_all | solution.py:398
  199.4 2.1 %last_block.1 = (f32[2,8,8]{2,1,0:T(8,128)}, f32[8,512]{1,0:T(8,128)}) custom-call(f32[12,2,128]{2,1,0:T(2,128)S(1)} %all_to_all.46.parts, f32[8,512]{1,0:T(8,128)S(1)} %get-tuple-element.24.rest, f32[8,512]{1,0:T(8,128)S(1)} %get-tuple-element.21.current, f32[2,8,8]{2,1,0:T(8,128)S(1)} %get-tuple-element.25.found), custom_call_target="tpu_custom_call" | custom-call | tf_op jit(solution)/shard_map/last_block/pallas_call | solution.py:384
  (1 shorter events, 0.0 us)
Async XLA Ops:
  2.0 20.0 %all-to-all-start = ((bf16[16,8,512]{2,1,0:T(8,128)(2,1)}), bf16[16,8,512]{2,1,0:T(8,128)(2,1)S(1)}, u32[]{:S(2)}, u32[]{:S(2)}) async-start(bf16[16,8,512]{2,1,0:T(8,128)(2,1)} %broadcast_in_dim.15), calls=%async_computation | async-start | bytes 262144 | tf_op jit(solution)/shard_map/all_to_all | solution.py:398
  18.1 3.0 %copy-start.3 = (s32[128]{0:T(128)S(1)}, s32[128]{0:T(128)}, u32[]{:S(2)}) copy-start(s32[128]{0:T(128)} %param.9) | copy-start | bytes 1540
  18.1 3.0 %copy-start.4 = (s32[128]{0:T(128)S(1)}, s32[128]{0:T(128)}, u32[]{:S(2)}) copy-start(s32[128]{0:T(128)} %param.8) | copy-start | bytes 1540
  69.4 17.7 %copy-start = (f32[8,512]{1,0:T(8,128)S(1)}, f32[8,512]{1,0:T(8,128)}, u32[]{:S(2)}) copy-start(f32[8,512]{1,0:T(8,128)} %prior.3) | copy-start | bytes 49156
  69.4 17.7 %copy-start.1 = (f32[8,512]{1,0:T(8,128)S(1)}, f32[8,512]{1,0:T(8,128)}, u32[]{:S(2)}) copy-start(f32[8,512]{1,0:T(8,128)} %prior.2) | copy-start | bytes 49156
  69.4 17.7 %copy-start.2 = (f32[8,8]{1,0:T(8,128)S(1)}, f32[8,8]{1,0:T(8,128)}, u32[]{:S(2)}) copy-start(f32[8,8]{1,0:T(8,128)} %beta.1) | copy-start | bytes 772

commit v5 on v4

--- a/solution.py
+++ b/solution.py
@@ -12,8 +12,6 @@
 STEPS = 2
 LANES = 128
 GROUP = 32
-DEPTH = 12
-BOTH = ("row", "col")
 AHEAD = (((1,), (1,)), ((), ()))
 BEHIND = (((1,), (0,)), ((), ()))
 HIGH = lax.Precision.HIGHEST
@@ -117,8 +115,20 @@
 
 def to_pairs(segments, pairs):
     for segment in range(segments.shape[0]):
-        put_pairs(segments[segment, :NV].astype(F32), segment, pairs)
+        put_pairs(segments[segment].astype(F32), segment, pairs)
     end_pairs(pairs)
+
+
+def part_rows(part):
+    return pl.ds(part * 2 * NV, 2 * NV)
+
+
+def put_message(message, own, sums, per):
+    for segment in range(message.shape[0]):
+        for part in range(per):
+            mine = own[:, part * LANES : (part + 1) * LANES]
+            partial = sums[segment * per + part].astype(BF16)
+            message[segment, part_rows(part)] = jnp.concatenate([mine, partial], axis=0)
 
 
 def segment_of(pairs, segment, per):
@@ -152,18 +162,14 @@
 def front_kernel(rows, cols, tiles, band, narrow, message, band_pairs, sums):
     to_pairs(band, band_pairs)
     accumulate(cols, rows, tiles, band_pairs, sums, AHEAD)
-    per = message.shape[2] // LANES
-    own = narrow[...]
-    for segment in range(message.shape[0]):
-        partial = segment_of(sums, segment, per).astype(BF16)
-        message[segment] = jnp.concatenate([own, partial], axis=0)
+    put_message(message, narrow[...], sums, band.shape[2] // LANES)
 
 
 def front(rows, cols, tiles, band, narrow, n_col):
     n_row, _, sub = band.shape
     return pl.pallas_call(
         front_kernel,
-        out_shape=jax.ShapeDtypeStruct((n_col, 2 * NV, sub), BF16),
+        out_shape=jax.ShapeDtypeStruct((n_col, 2 * NV * sub // LANES, LANES), BF16),
         in_specs=[SMEM, SMEM, VMEM, VMEM, VMEM],
         out_specs=VMEM,
         scratch_shapes=[pair_scratch(n_row, sub), pair_scratch(n_col, sub)],
@@ -173,16 +179,24 @@
 
 
 def back_kernel(rows, cols, tiles, moved, back, owned, across_pairs, sums):
-    to_pairs(moved, across_pairs)
-    owned[...] = jnp.sum(moved[:, NV:].astype(F32), axis=0)
+    per = back.shape[2] // LANES
+    gathered = []
+    for part in range(per):
+        total = jnp.zeros((NV, LANES), F32)
+        for segment in range(moved.shape[0]):
+            held = moved[segment, part_rows(part)].astype(F32)
+            across_pairs[segment * per + part] = held[:NV]
+            total = total + held[NV:]
+        gathered.append(total)
+    end_pairs(across_pairs)
+    owned[...] = jnp.concatenate(gathered, axis=1)
     accumulate(rows, cols, tiles, across_pairs, sums, BEHIND)
-    per = back.shape[2] // LANES
     for segment in range(back.shape[0]):
         back[segment] = segment_of(sums, segment, per)
 
 
-def back(rows, cols, tiles, moved, n_row):
-    n_col, _, sub = moved.shape
+def back(rows, cols, tiles, moved, n_row, sub):
+    n_col = moved.shape[0]
     return pl.pallas_call(
         back_kernel,
         out_shape=(
@@ -268,15 +282,13 @@
         put_pairs(mix(inverse, got[segment, :, :sub]), segment, band_pairs)
     end_pairs(band_pairs)
     own = mix(inverse, rest[...]).astype(BF16)
-    wide = jnp.concatenate([lower, jnp.zeros((NV, 3 * NV), F32)], axis=1)
-    held = jnp.concatenate([summed, wide], axis=0)
-    beside = jnp.concatenate(pieces(held, 3) + [jnp.zeros((2 * NV, 4 * NV), BF16)], axis=1)
+    twice = jnp.concatenate([lower, lower], axis=1)
+    beside = jnp.concatenate(pieces(summed, 3) + pieces(twice, 2), axis=1)
     accumulate(cols, rows, tiles, band_pairs, sums, AHEAD)
     per = sub // LANES
+    put_message(message, own, sums, per)
     for segment in range(message.shape[0]):
-        partial = segment_of(sums, segment, per).astype(BF16)
-        both = jnp.concatenate([own, partial], axis=0)
-        message[segment] = jnp.concatenate([both, beside], axis=1)
+        message[segment, pl.ds(2 * NV * per, NV)] = beside
 
 
 def whiten(rows, cols, tiles, got, rest, n_col):
@@ -284,7 +296,7 @@
     sub = rest.shape[1]
     return pl.pallas_call(
         whiten_kernel,
-        out_shape=jax.ShapeDtypeStruct((n_col, 2 * NV, sub + LANES), BF16),
+        out_shape=jax.ShapeDtypeStruct((n_col, 2 * NV * sub // LANES + NV, LANES), BF16),
         in_specs=[SMEM, SMEM, VMEM, VMEM, VMEM],
         out_specs=VMEM,
         scratch_shapes=[pair_scratch(n_row, sub), pair_scratch(n_col, sub)],
@@ -299,39 +311,58 @@
 
 
 def settle_kernel(
-    total, rows, cols, tiles, moved, before, owned_before, rest, current,
+    total, rows, cols, tiles, moved, before, rest, current,
     back, owned, following, upper_out, alphas, across_pairs, sums,
 ):
     n_col = moved.shape[0]
     sub = rest.shape[1]
+    per = sub // LANES
+    beside = pl.ds(2 * NV * per, NV)
     summed = jnp.zeros((NV, LANES), F32)
     for segment in range(n_col):
-        summed = summed + moved[segment, :NV, sub:].astype(F32)
+        summed = summed + moved[segment, beside].astype(F32)
     alpha, upper, inverse = factor_of_sums(joined(summed) / total)
     upper_out[...] = upper
     alphas[...] = jnp.zeros_like(alphas)
     alphas[0] = alpha
-    turn = dot_t(inverse, alpha)
+    turn = -dot_t(inverse, alpha)
     following[...] = dot(inverse, rest[...] - dot_tn(alpha, current[...]))
+    columns = [jnp.broadcast_to(inverse[:, v : v + 1], (NV, LANES)) for v in range(NV)]
+    four = 4 * NV
+    lane = lax.broadcasted_iota(jnp.int32, (NV, four), 1)
+    segment_lanes = (lane & NV) == 0
+    turns = jnp.concatenate([turn] * 4, axis=1)
 
     def settle(segment, gathered):
-        held = moved[segment].astype(F32)
-        past = before[segment].astype(F32)[:NV]
-        lower = joined(held[NV:, sub:])[:, :NV]
-        change = mix(inverse, lower)
-        put_pairs(mix(change, held[:NV, :sub]) - mix(turn, past), segment, across_pairs)
-        return gathered + mix(change, held[NV:, :sub])
-
-    gathered = lax.fori_loop(0, n_col, settle, jnp.zeros((NV, sub), F32), unroll=4)
-    owned[...] = gathered - mix(turn, owned_before[...])
+        held = moved[segment, beside].astype(F32)
+        held = held + pltpu.roll(held, 2 * NV, 1)
+        change = columns[0] * held[0:1]
+        for v in range(1, NV):
+            change = change + columns[v] * held[v : v + 1]
+        change = pltpu.roll(change, 2 * NV, 1)[:, :four]
+        change = jnp.where(lane < 2 * NV, change, turns)
+        high = change.astype(BF16).astype(F32)
+        both = jnp.concatenate([high, change - high], axis=0)
+        mask = jnp.concatenate([segment_lanes, segment_lanes], axis=0)
+        left = jnp.concatenate([jnp.where(mask, both, 0.0), jnp.where(mask, 0.0, both)], axis=0)
+        parts = []
+        for part in range(per):
+            now = moved[segment, part_rows(part)]
+            past = before[segment, part_rows(part)]
+            parts.append(jnp.concatenate([now, past], axis=0))
+        right = jnp.concatenate(parts, axis=1)
+        out = jnp.dot(left.astype(BF16), right, preferred_element_type=F32)
+        put_pairs(out[:NV] + out[NV : 2 * NV], segment, across_pairs)
+        return gathered + (out[2 * NV : 3 * NV] + out[3 * NV :])
+
+    owned[...] = lax.fori_loop(0, n_col, settle, jnp.zeros((NV, sub), F32), unroll=8)
     end_pairs(across_pairs)
     accumulate(rows, cols, tiles, across_pairs, sums, BEHIND, split=2)
-    per = sub // LANES
     for segment in range(back.shape[0]):
         back[segment] = segment_of(sums, segment, per)
 
 
-def settle(rows, cols, tiles, moved, before, owned_before, rest, current, total, n_row):
+def settle(rows, cols, tiles, moved, before, rest, current, total, n_row):
     n_col = moved.shape[0]
     sub = rest.shape[1]
     return pl.pallas_call(
@@ -343,12 +374,12 @@
             jax.ShapeDtypeStruct((NV, NV), F32),
             jax.ShapeDtypeStruct((STEPS, NV, NV), F32),
         ),
-        in_specs=[SMEM, SMEM] + [VMEM] * 6,
+        in_specs=[SMEM, SMEM] + [VMEM] * 5,
         out_specs=(VMEM,) * 5,
         scratch_shapes=[pair_scratch(n_col, sub), pair_scratch(n_row, sub)],
         compiler_params=PARAMS,
         name="settle_tiles",
-    )(rows, cols, tiles, moved, before, owned_before, rest, current)
+    )(rows, cols, tiles, moved, before, rest, current)
 
 
 def spread_kernel(parts, sums):
@@ -394,19 +425,28 @@
     )(parts, rest, current, found)
 
 
-def swap(blocks, axis, groups=None):
-    return lax.all_to_all(blocks, axis, 0, 0, tiled=True, axis_index_groups=groups)
-
-
-def planes_and_lines(n_row, n_col):
-    depth = DEPTH if n_col % DEPTH == 0 else n_col
-    lines = [
-        [row * n_col + high * depth + z for z in range(depth)]
-        for row in range(n_row)
-        for high in range(n_col // depth)
-    ]
-    planes = [[line[z] for line in lines] for z in range(depth)]
-    return planes, lines
+def round_kernel(block, narrow, copies):
+    held = block[...].astype(BF16)
+    narrow[...] = held
+    copies[...] = jnp.broadcast_to(held[None], copies.shape)
+
+
+def round_block(block, n_row):
+    return pl.pallas_call(
+        round_kernel,
+        out_shape=(
+            jax.ShapeDtypeStruct(block.shape, BF16),
+            jax.ShapeDtypeStruct((n_row, *block.shape), BF16),
+        ),
+        in_specs=[VMEM],
+        out_specs=(VMEM, VMEM),
+        compiler_params=PARAMS,
+        name="round_block",
+    )(block)
+
+
+def swap(blocks, axis):
+    return lax.all_to_all(blocks, axis, 0, 0, tiled=True)
 
 
 def shards(tiles, tile_row, tile_col, tile_count, block, previous, coupling):
@@ -419,24 +459,22 @@
     live = lax.iota(jnp.int32, slots) < tile_count[0]
     rows = jnp.where(live, tile_row, n_col * sub // TILE)
     cols = jnp.where(live, tile_col, n_row * sub // TILE)
-    planes, lines = planes_and_lines(n_row, n_col)
-    narrow = block.astype(BF16)
-
-    band = swap(jnp.broadcast_to(narrow[None], (n_row, NV, sub)), "row")
+    narrow, copies = round_block(block, n_row)
+
+    band = swap(copies, "row")
     before = swap(front(rows, cols, squares, band, narrow, n_col), "col")
-    partial, owned = back(rows, cols, squares, before, n_row)
+    partial, owned = back(rows, cols, squares, before, n_row, sub)
     returned = swap(partial, "row")
     rest, message = carry(owned, returned, block, previous, coupling, n_row)
 
     got = swap(message, "row")
     moved = swap(whiten(rows, cols, squares, got, rest, n_col), "col")
     partial, owned, current, upper, found = settle(
-        rows, cols, squares, moved, before, owned, rest, block, total, n_row
+        rows, cols, squares, moved, before, rest, block, total, n_row
     )
     returned = swap(partial, "row")
-    rest, sums = local(owned, returned, current, block, upper, len(planes[0]))
-    sums = spread(swap(sums, BOTH, planes), len(lines[0]))
-    parts = swap(sums, BOTH, lines)
+    rest, sums = local(owned, returned, current, block, upper, n_row)
+    parts = swap(spread(swap(sums, "row"), n_col), "col")
     found, current = last(parts, rest, current, found, total)
     return (current, found)
 

time: 202 us -> 198 us (0.980)
    pallas_call x1, Pallas kernels: 8.5 us -> 6.08 us  [settle(): pl.pallas_call(functools.partial(settle_kernel, total), out_shape=(jax.Sh...]
where the time goes in v5:
time: 198 us; the launch traced here: 197 us
  blocking collectives  157 us (79%)
  Pallas kernels  19.2 us (10%)
  starting transfers between devices  13.8 us (7%)
  local copies, waits for them, and re-layouts  5.34 us (3%)
    all_to_all x7, blocking collectives, swap(): return lax.all_to_all(blocks, axis, 0, 0, tiled=True)  157 us
    all_to_all x1, starting transfers between devices, swap(): return lax.all_to_all(blocks, axis, 0, 0, tiled=True)  13.8 us
    pallas_call x1, Pallas kernels, settle(): pl.pallas_call(functools.partial(settle_kernel, total), out_shape=(jax.Sh...  6.08 us
    pallas_call x1, Pallas kernels, whiten(): pl.pallas_call(whiten_kernel, out_shape=jax.ShapeDtypeStruct((n_col, 2 *...  4.26 us
  transfers between devices with their start and end apart: 1, of which 1 were waited for; matrix products, arithmetic and copies ran while one was open for 2% of the time, Pallas kernels for 0%

profile of v5, /device:TPU:1, one launch (start us, length us, event | category | flops | bytes accessed | tf_op | source)
XLA Modules:
  0.0 197.3 jit_solution(3497341581842684960)
XLA Ops:
  0.6 0.0 copy-start
  0.6 0.7 copy-done
  1.3 0.7 round_block.1
  2.0 13.8 %all-to-all-start = ((bf16[16,8,512]{2,1,0:T(8,128)(2,1)}), bf16[16,8,512]{2,1,0:T(8,128)(2,1)S(1)}, u32[]{:S(2)}, u32[]{:S(2)}) async-start(bf16[16,8,512]{2,1,0:T(8,128)(2,1)} %get-tuple-element.17), calls=%async_computation | async-start | bytes 262144 | tf_op jit(solution)/shard_map/all_to_all | solution.py:449
  16.5 1.6 copy.9
  18.1 0.0 copy-start.4
  18.1 0.0 copy-start.5
  18.1 3.0 %copy.13.tiles = bf16[128,64,64]{2,1,0:T(8,128)(2,1)S(1)} copy(bf16[128,64,64]{0,2,1:T(8,128)(2,1)S(1)} %bitcast.3) | data formatting | bytes 2097152 | tf_op jit(solution)/shard_map/reshape | solution.py:458
  21.1 0.0 copy-done.4
  21.1 0.0 copy-done.5
  21.2 0.9 all-to-all-done.band
  22.1 2.8 %front_tiles.1 = bf16[48,64,128]{2,1,0:T(8,128)(2,1)S(1)} custom-call(s32[128]{0:T(128)S(1)} %get-tuple-element.33.rows, s32[128]{0:T(128)S(1)} %get-tuple-element.32.cols, bf16[128,64,64]{2,1,0:T(8,128)(2,1)S(1)} %copy.13.tiles, bf16[16,8,512]{2,1,0:T(8,128)(2,1)S(1)} %all-to-all-done.band, bf16[8,512]{1,0:T(8,128)(2,1)S(1)} %get-tuple-element.18.narrow), custom_call_target="tpu_custom_call" | custom-call | tf_op jit(solution)/shard_map/front_tiles/pallas_call | solution.py:170
  24.9 44.5 %all_to_all.40.moved.before = bf16[48,64,128]{2,1,0:T(8,128)(2,1)S(1)} all-to-all(bf16[48,64,128]{2,1,0:T(8,128)(2,1)S(1)} %front_tiles.1), channel_id=1, replica_groups=mesh['row'=16,'col'=48] {'col'}, dimensions={0} | all-to-all | bytes 1572864 | tf_op jit(solution)/shard_map/all_to_all | solution.py:449
  69.4 0.0 copy-start.1
  69.4 0.0 copy-start.2
  69.4 0.0 copy-start.3
  69.4 2.4 %back_tiles.1 = (f32[16,8,512]{2,1,0:T(8,128)S(1)}, f32[8,512]{1,0:T(8,128)S(1)}) custom-call(s32[128]{0:T(128)S(1)} %get-tuple-element.33.rows, s32[128]{0:T(128)S(1)} %get-tuple-element.32.cols, bf16[128,64,64]{2,1,0:T(8,128)(2,1)S(1)} %copy.13.tiles, bf16[48,64,128]{2,1,0:T(8,128)(2,1)S(1)} %all_to_all.40.moved.before), custom_call_target="tpu_custom_call" | custom-call | tf_op jit(solution)/shard_map/back_tiles/pallas_call | solution.py:200
  71.8 15.4 %all_to_all.41.returned = f32[16,8,512]{2,1,0:T(8,128)S(1)} all-to-all(f32[16,8,512]{2,1,0:T(8,128)S(1)} %get-tuple-element.20), channel_id=1, replica_groups=mesh['row'=16,'col'=48] {'row'}, dimensions={0} | all-to-all | bytes 524288 | tf_op jit(solution)/shard_map/all_to_all | solution.py:449
  87.2 0.0 copy-done.1
  87.2 0.0 copy-done.2
  87.2 0.0 copy-done.3
  87.2 0.4 local_carry.1
  87.6 11.2 %all_to_all.42.got = f32[16,8,640]{2,1,0:T(8,128)S(1)} all-to-all(f32[16,8,640]{2,1,0:T(8,128)S(1)} %get-tuple-element.21), channel_id=1, replica_groups=mesh['row'=16,'col'=48] {'row'}, dimensions={0} | all-to-all | bytes 655360 | tf_op jit(solution)/shard_map/all_to_all | solution.py:449
  98.8 4.3 %whiten_tiles.1 = bf16[48,72,128]{2,1,0:T(8,128)(2,1)S(1)} custom-call(s32[128]{0:T(128)S(1)} %get-tuple-element.33.rows, s32[128]{0:T(128)S(1)} %get-tuple-element.32.cols, bf16[128,64,64]{2,1,0:T(8,128)(2,1)S(1)} %copy.13.tiles, f32[16,8,640]{2,1,0:T(8,128)S(1)} %all_to_all.42.got, f32[8,512]{1,0:T(8,128)S(1)} %get-tuple-element.22.rest), custom_call_target="tpu_custom_call" | custom-call | tf_op jit(solution)/shard_map/whiten_tiles/pallas_call | solution.py:297
  103.0 41.0 %all_to_all.43.moved = bf16[48,72,128]{2,1,0:T(8,128)(2,1)S(1)} all-to-all(bf16[48,72,128]{2,1,0:T(8,128)(2,1)S(1)} %whiten_tiles.1), channel_id=1, replica_groups=mesh['row'=16,'col'=48] {'col'}, dimensions={0} | all-to-all | bytes 1769472 | tf_op jit(solution)/shard_map/all_to_all | solution.py:449
  144.1 6.1 %settle_tiles.1 = (f32[16,8,512]{2,1,0:T(8,128)S(1)}, f32[8,512]{1,0:T(8,128)S(1)}, f32[8,512]{1,0:T(8,128)S(1)}, f32[8,8]{1,0:T(8,128)S(1)}, f32[2,8,8]{2,1,0:T(8,128)S(1)}) custom-call(s32[128]{0:T(128)S(1)} %get-tuple-element.33.rows, s32[128]{0:T(128)S(1)} %get-tuple-element.32.cols, bf16[128,64,64]{2,1,0:T(8,128)(2,1)S(1)} %copy.13.tiles, ...), custom_call_target="tpu_custom_call" | custom-call | tf_op jit(solution)/shard_map/settle_tiles/pallas_call | solution.py:368
  150.2 15.5 %all_to_all.44.returned = f32[16,8,512]{2,1,0:T(8,128)S(1)} all-to-all(f32[16,8,512]{2,1,0:T(8,128)S(1)} %get-tuple-element.24), channel_id=1, replica_groups=mesh['row'=16,'col'=48] {'row'}, dimensions={0} | all-to-all | bytes 524288 | tf_op jit(solution)/shard_map/all_to_all | solution.py:449
  165.6 0.4 local_sums.1
  166.1 9.2 %all_to_all.45.parts = f32[16,2,128]{2,1,0:T(2,128)S(1)} all-to-all(f32[16,2,128]{2,1,0:T(2,128)S(1)} %get-tuple-element.27), channel_id=1, replica_groups=mesh['row'=16,'col'=48] {'row'}, dimensions={0} | all-to-all | bytes 32768 | tf_op jit(solution)/shard_map/all_to_all | solution.py:449
  175.4 19.8 %all_to_all.46.parts = f32[48,2,128]{2,1,0:T(2,128)S(1)} all-to-all(f32[48,2,128]{2,1,0:T(2,128)S(1)} %spread_sums.1), channel_id=1, replica_groups=mesh['row'=16,'col'=48] {'col'}, dimensions={0} | all-to-all | bytes 98304 | tf_op jit(solution)/shard_map/all_to_all | solution.py:449
  195.1 2.1 %last_block.1 = (f32[2,8,8]{2,1,0:T(8,128)}, f32[8,512]{1,0:T(8,128)}) custom-call(f32[48,2,128]{2,1,0:T(2,128)S(1)} %all_to_all.46.parts, f32[8,512]{1,0:T(8,128)S(1)} %get-tuple-element.28.rest, f32[8,512]{1,0:T(8,128)S(1)} %get-tuple-element.25.current, f32[2,8,8]{2,1,0:T(8,128)S(1)} %get-tuple-element.29.found), custom_call_target="tpu_custom_call" | custom-call | tf_op jit(solution)/shard_map/last_block/pallas_call | solution.py:415
  (2 shorter events, 0.0 us)
Async XLA Ops:
  0.6 0.7 copy-start
  2.0 20.0 %all-to-all-start = ((bf16[16,8,512]{2,1,0:T(8,128)(2,1)}), bf16[16,8,512]{2,1,0:T(8,128)(2,1)S(1)}, u32[]{:S(2)}, u32[]{:S(2)}) async-start(bf16[16,8,512]{2,1,0:T(8,128)(2,1)} %get-tuple-element.17), calls=%async_computation | async-start | bytes 262144 | tf_op jit(solution)/shard_map/all_to_all | solution.py:449
  18.1 3.0 %copy-start.4 = (s32[128]{0:T(128)S(1)}, s32[128]{0:T(128)}, u32[]{:S(2)}) copy-start(s32[128]{0:T(128)} %param.9) | copy-start | bytes 1540
  18.1 3.0 %copy-start.5 = (s32[128]{0:T(128)S(1)}, s32[128]{0:T(128)}, u32[]{:S(2)}) copy-start(s32[128]{0:T(128)} %param.8) | copy-start | bytes 1540
  69.4 17.8 %copy-start.1 = (f32[8,512]{1,0:T(8,128)S(1)}, f32[8,512]{1,0:T(8,128)}, u32[]{:S(2)}) copy-start(f32[8,512]{1,0:T(8,128)} %prior.3) | copy-start | bytes 49156
  69.4 17.8 %copy-start.2 = (f32[8,512]{1,0:T(8,128)S(1)}, f32[8,512]{1,0:T(8,128)}, u32[]{:S(2)}) copy-start(f32[8,512]{1,0:T(8,128)} %prior.2) | copy-start | bytes 49156
  69.4 17.8 %copy-start.3 = (f32[8,8]{1,0:T(8,128)S(1)}, f32[8,8]{1,0:T(8,128)}, u32[]{:S(2)}) copy-start(f32[8,8]{1,0:T(8,128)} %beta.1) | copy-start | bytes 772

commit v6 on v5

--- a/solution.py
+++ b/solution.py
@@ -11,7 +11,7 @@
 NV = 8
 STEPS = 2
 LANES = 128
-GROUP = 32
+GROUP = 16
 AHEAD = (((1,), (1,)), ((), ()))
 BEHIND = (((1,), (0,)), ((), ()))
 HIGH = lax.Precision.HIGHEST
@@ -81,9 +81,9 @@
     unit = jnp.where(row + NV == lane, 1.0, 0.0).astype(F32)
     work = jnp.concatenate([gram, unit[:, NV:]], axis=1)
     for j in range(NV):
-        pivot = jnp.sqrt(work[j : j + 1, j : j + 1])
-        scaled = work[j : j + 1, :] / pivot
-        column = work[:, j : j + 1] / pivot
+        scale = 1.0 / jnp.sqrt(work[j : j + 1, j : j + 1])
+        scaled = work[j : j + 1, :] * scale
+        column = work[:, j : j + 1] * scale
         work = jnp.where(row == j, scaled, jnp.where(row > j, work - column * scaled, work))
     return jnp.where(row <= lane, work, 0.0)[:, :NV], work[:, NV:]
 
@@ -144,19 +144,16 @@
     half = lane_half()
     sums[...] = jnp.zeros_like(sums)
 
-    def group(g, carry):
+    slots = tiles.shape[0]
+    for first in range(0, slots, GROUP):
         updates = []
-        for u in range(GROUP):
-            k = g * GROUP + u
+        for k in range(first, min(first + GROUP, slots)):
             read, write = reads[k], writes[k]
             picked = narrowed(pairs[lax.shift_right_logical(read, 1)], half == (read & 1))
             out = both_halves(product_of(picked, tiles[k], dims, split), half == (write & 1))
             updates.append((lax.shift_right_logical(write, 1), out))
         for pair, out in updates:
             sums[pair] += out
-        return carry
-
-    lax.fori_loop(0, tiles.shape[0] // GROUP, group, 0)
 
 
 def front_kernel(rows, cols, tiles, band, narrow, message, band_pairs, sums):
@@ -355,7 +352,7 @@
         put_pairs(out[:NV] + out[NV : 2 * NV], segment, across_pairs)
         return gathered + (out[2 * NV : 3 * NV] + out[3 * NV :])
 
-    owned[...] = lax.fori_loop(0, n_col, settle, jnp.zeros((NV, sub), F32), unroll=8)
+    owned[...] = lax.fori_loop(0, n_col, settle, jnp.zeros((NV, sub), F32), unroll=True)
     end_pairs(across_pairs)
     accumulate(rows, cols, tiles, across_pairs, sums, BEHIND, split=2)
     for segment in range(back.shape[0]):

time: 198 us -> 193 us (0.975)
  Pallas kernels: 19.2 us -> 14.4 us
    pallas_call x1, Pallas kernels: 6.08 us -> 3.76 us  [settle(): pl.pallas_call(functools.partial(settle_kernel, total), out_shape=(jax.Sh...]
where the time goes in v6:
time: 193 us
  blocking collectives  157 us (81%)
  Pallas kernels  14.4 us (7%)
  starting transfers between devices  13.8 us (7%)
  local copies, waits for them, and re-layouts  5.34 us (3%)
    all_to_all x7, blocking collectives, swap(): return lax.all_to_all(blocks, axis, 0, 0, tiled=True)  157 us
    all_to_all x1, starting transfers between devices, swap(): return lax.all_to_all(blocks, axis, 0, 0, tiled=True)  13.8 us
  transfers between devices with their start and end apart: 1, of which 1 were waited for; matrix products, arithmetic and copies ran while one was open for 2% of the time, Pallas kernels for 0%

profile of v6, /device:TPU:1, one launch (start us, length us, event | category | flops | bytes accessed | tf_op | source)
XLA Modules:
  0.0 192.6 jit_solution(6575661990314898934)
XLA Ops:
  0.6 0.0 copy-start
  0.6 0.7 copy-done
  1.3 0.7 round_block.1
  2.0 13.8 %all-to-all-start = ((bf16[16,8,512]{2,1,0:T(8,128)(2,1)}), bf16[16,8,512]{2,1,0:T(8,128)(2,1)S(1)}, u32[]{:S(2)}, u32[]{:S(2)}) async-start(bf16[16,8,512]{2,1,0:T(8,128)(2,1)} %get-tuple-element.17), calls=%async_computation | async-start | bytes 262144 | tf_op jit(solution)/shard_map/all_to_all | solution.py:446
  16.5 1.6 copy.9
  18.1 0.0 copy-start.4
  18.1 0.0 copy-start.5
  18.1 3.0 %copy.13.tiles = bf16[128,64,64]{2,1,0:T(8,128)(2,1)S(1)} copy(bf16[128,64,64]{0,2,1:T(8,128)(2,1)S(1)} %bitcast.3) | data formatting | bytes 2097152 | tf_op jit(solution)/shard_map/reshape | solution.py:455
  21.1 0.0 copy-done.4
  21.1 0.0 copy-done.5
  21.2 0.9 all-to-all-done.band
  22.1 2.1 %front_tiles.1 = bf16[48,64,128]{2,1,0:T(8,128)(2,1)S(1)} custom-call(s32[128]{0:T(128)S(1)} %get-tuple-element.33.rows, s32[128]{0:T(128)S(1)} %get-tuple-element.32.cols, bf16[128,64,64]{2,1,0:T(8,128)(2,1)S(1)} %copy.13.tiles, bf16[16,8,512]{2,1,0:T(8,128)(2,1)S(1)} %all-to-all-done.band, bf16[8,512]{1,0:T(8,128)(2,1)S(1)} %get-tuple-element.18.narrow), custom_call_target="tpu_custom_call" | custom-call | tf_op jit(solution)/shard_map/front_tiles/pallas_call | solution.py:167
  24.1 44.6 %all_to_all.40.moved.before = bf16[48,64,128]{2,1,0:T(8,128)(2,1)S(1)} all-to-all(bf16[48,64,128]{2,1,0:T(8,128)(2,1)S(1)} %front_tiles.1), channel_id=1, replica_groups=mesh['row'=16,'col'=48] {'col'}, dimensions={0} | all-to-all | bytes 1572864 | tf_op jit(solution)/shard_map/all_to_all | solution.py:446
  68.7 0.0 copy-start.1
  68.7 0.0 copy-start.2
  68.7 0.0 copy-start.3
  68.7 1.6 back_tiles.1
  70.3 15.3 %all_to_all.41.returned = f32[16,8,512]{2,1,0:T(8,128)S(1)} all-to-all(f32[16,8,512]{2,1,0:T(8,128)S(1)} %get-tuple-element.20), channel_id=1, replica_groups=mesh['row'=16,'col'=48] {'row'}, dimensions={0} | all-to-all | bytes 524288 | tf_op jit(solution)/shard_map/all_to_all | solution.py:446
  85.6 0.0 copy-done.1
  85.7 0.0 copy-done.2
  85.7 0.0 copy-done.3
  85.7 0.4 local_carry.1
  86.0 11.2 %all_to_all.42.got = f32[16,8,640]{2,1,0:T(8,128)S(1)} all-to-all(f32[16,8,640]{2,1,0:T(8,128)S(1)} %get-tuple-element.21), channel_id=1, replica_groups=mesh['row'=16,'col'=48] {'row'}, dimensions={0} | all-to-all | bytes 655360 | tf_op jit(solution)/shard_map/all_to_all | solution.py:446
  97.2 3.3 %whiten_tiles.1 = bf16[48,72,128]{2,1,0:T(8,128)(2,1)S(1)} custom-call(s32[128]{0:T(128)S(1)} %get-tuple-element.33.rows, s32[128]{0:T(128)S(1)} %get-tuple-element.32.cols, bf16[128,64,64]{2,1,0:T(8,128)(2,1)S(1)} %copy.13.tiles, f32[16,8,640]{2,1,0:T(8,128)S(1)} %all_to_all.42.got, f32[8,512]{1,0:T(8,128)S(1)} %get-tuple-element.22.rest), custom_call_target="tpu_custom_call" | custom-call | tf_op jit(solution)/shard_map/whiten_tiles/pallas_call | solution.py:294
  100.5 41.1 %all_to_all.43.moved = bf16[48,72,128]{2,1,0:T(8,128)(2,1)S(1)} all-to-all(bf16[48,72,128]{2,1,0:T(8,128)(2,1)S(1)} %whiten_tiles.1), channel_id=1, replica_groups=mesh['row'=16,'col'=48] {'col'}, dimensions={0} | all-to-all | bytes 1769472 | tf_op jit(solution)/shard_map/all_to_all | solution.py:446
  141.6 3.8 %settle_tiles.1 = (f32[16,8,512]{2,1,0:T(8,128)S(1)}, f32[8,512]{1,0:T(8,128)S(1)}, f32[8,512]{1,0:T(8,128)S(1)}, f32[8,8]{1,0:T(8,128)S(1)}, f32[2,8,8]{2,1,0:T(8,128)S(1)}) custom-call(s32[128]{0:T(128)S(1)} %get-tuple-element.33.rows, s32[128]{0:T(128)S(1)} %get-tuple-element.32.cols, bf16[128,64,64]{2,1,0:T(8,128)(2,1)S(1)} %copy.13.tiles, ...), custom_call_target="tpu_custom_call" | custom-call | tf_op jit(solution)/shard_map/settle_tiles/pallas_call | solution.py:365
  145.4 15.5 %all_to_all.44.returned = f32[16,8,512]{2,1,0:T(8,128)S(1)} all-to-all(f32[16,8,512]{2,1,0:T(8,128)S(1)} %get-tuple-element.24), channel_id=1, replica_groups=mesh['row'=16,'col'=48] {'row'}, dimensions={0} | all-to-all | bytes 524288 | tf_op jit(solution)/shard_map/all_to_all | solution.py:446
  160.9 0.4 local_sums.1
  161.4 9.2 %all_to_all.45.parts = f32[16,2,128]{2,1,0:T(2,128)S(1)} all-to-all(f32[16,2,128]{2,1,0:T(2,128)S(1)} %get-tuple-element.27), channel_id=1, replica_groups=mesh['row'=16,'col'=48] {'row'}, dimensions={0} | all-to-all | bytes 32768 | tf_op jit(solution)/shard_map/all_to_all | solution.py:446
  170.6 19.8 %all_to_all.46.parts = f32[48,2,128]{2,1,0:T(2,128)S(1)} all-to-all(f32[48,2,128]{2,1,0:T(2,128)S(1)} %spread_sums.1), channel_id=1, replica_groups=mesh['row'=16,'col'=48] {'col'}, dimensions={0} | all-to-all | bytes 98304 | tf_op jit(solution)/shard_map/all_to_all | solution.py:446
  190.4 2.1 %last_block.1 = (f32[2,8,8]{2,1,0:T(8,128)}, f32[8,512]{1,0:T(8,128)}) custom-call(f32[48,2,128]{2,1,0:T(2,128)S(1)} %all_to_all.46.parts, f32[8,512]{1,0:T(8,128)S(1)} %get-tuple-element.28.rest, f32[8,512]{1,0:T(8,128)S(1)} %get-tuple-element.25.current, f32[2,8,8]{2,1,0:T(8,128)S(1)} %get-tuple-element.29.found), custom_call_target="tpu_custom_call" | custom-call | tf_op jit(solution)/shard_map/last_block/pallas_call | solution.py:412
  (2 shorter events, 0.0 us)
Async XLA Ops:
  0.6 0.7 copy-start
  2.0 20.0 %all-to-all-start = ((bf16[16,8,512]{2,1,0:T(8,128)(2,1)}), bf16[16,8,512]{2,1,0:T(8,128)(2,1)S(1)}, u32[]{:S(2)}, u32[]{:S(2)}) async-start(bf16[16,8,512]{2,1,0:T(8,128)(2,1)} %get-tuple-element.17), calls=%async_computation | async-start | bytes 262144 | tf_op jit(solution)/shard_map/all_to_all | solution.py:446
  18.1 3.0 %copy-start.4 = (s32[128]{0:T(128)S(1)}, s32[128]{0:T(128)}, u32[]{:S(2)}) copy-start(s32[128]{0:T(128)} %param.9) | copy-start | bytes 1540
  18.1 3.0 %copy-start.5 = (s32[128]{0:T(128)S(1)}, s32[128]{0:T(128)}, u32[]{:S(2)}) copy-start(s32[128]{0:T(128)} %param.8) | copy-start | bytes 1540
  68.7 16.9 %copy-start.1 = (f32[8,512]{1,0:T(8,128)S(1)}, f32[8,512]{1,0:T(8,128)}, u32[]{:S(2)}) copy-start(f32[8,512]{1,0:T(8,128)} %prior.3) | copy-start | bytes 49156
  68.7 16.9 %copy-start.2 = (f32[8,512]{1,0:T(8,128)S(1)}, f32[8,512]{1,0:T(8,128)}, u32[]{:S(2)}) copy-start(f32[8,512]{1,0:T(8,128)} %prior.2) | copy-start | bytes 49156
  68.7 16.9 %copy-start.3 = (f32[8,8]{1,0:T(8,128)S(1)}, f32[8,8]{1,0:T(8,128)}, u32[]{:S(2)}) copy-start(f32[8,8]{1,0:T(8,128)} %beta.1) | copy-start | bytes 772

commit v7 on v6

--- a/solution.py
+++ b/solution.py
@@ -12,6 +12,8 @@
 STEPS = 2
 LANES = 128
 GROUP = 16
+DEPTH = 12
+BOTH = ("row", "col")
 AHEAD = (((1,), (1,)), ((), ()))
 BEHIND = (((1,), (0,)), ((), ()))
 HIGH = lax.Precision.HIGHEST
@@ -156,13 +158,13 @@
             sums[pair] += out
 
 
-def front_kernel(rows, cols, tiles, band, narrow, message, band_pairs, sums):
+def front_kernel(rows, cols, tiles, band, block, message, band_pairs, sums):
     to_pairs(band, band_pairs)
     accumulate(cols, rows, tiles, band_pairs, sums, AHEAD)
-    put_message(message, narrow[...], sums, band.shape[2] // LANES)
-
-
-def front(rows, cols, tiles, band, narrow, n_col):
+    put_message(message, block[...].astype(BF16), sums, band.shape[2] // LANES)
+
+
+def front(rows, cols, tiles, band, block, n_col):
     n_row, _, sub = band.shape
     return pl.pallas_call(
         front_kernel,
@@ -172,7 +174,7 @@
         scratch_shapes=[pair_scratch(n_row, sub), pair_scratch(n_col, sub)],
         compiler_params=PARAMS,
         name="front_tiles",
-    )(rows, cols, tiles, band, narrow)
+    )(rows, cols, tiles, band, block)
 
 
 def back_kernel(rows, cols, tiles, moved, back, owned, across_pairs, sums):
@@ -422,28 +424,18 @@
     )(parts, rest, current, found)
 
 
-def round_kernel(block, narrow, copies):
-    held = block[...].astype(BF16)
-    narrow[...] = held
-    copies[...] = jnp.broadcast_to(held[None], copies.shape)
-
-
-def round_block(block, n_row):
-    return pl.pallas_call(
-        round_kernel,
-        out_shape=(
-            jax.ShapeDtypeStruct(block.shape, BF16),
-            jax.ShapeDtypeStruct((n_row, *block.shape), BF16),
-        ),
-        in_specs=[VMEM],
-        out_specs=(VMEM, VMEM),
-        compiler_params=PARAMS,
-        name="round_block",
-    )(block)
-
-
-def swap(blocks, axis):
-    return lax.all_to_all(blocks, axis, 0, 0, tiled=True)
+def swap(blocks, axis, groups=None):
+    return lax.all_to_all(blocks, axis, 0, 0, tiled=True, axis_index_groups=groups)
+
+
+def lines_and_rest(n_row, n_col):
+    depth = DEPTH if n_col % DEPTH == 0 else n_col
+    lines = [
+        [(chip + core) * n_col + high + z for core in range(2) for z in range(depth)]
+        for chip in range(0, n_row, 2)
+        for high in range(0, n_col, depth)
+    ]
+    return lines, [list(rest) for rest in zip(*lines)]
 
 
 def shards(tiles, tile_row, tile_col, tile_count, block, previous, coupling):
@@ -456,10 +448,11 @@
     live = lax.iota(jnp.int32, slots) < tile_count[0]
     rows = jnp.where(live, tile_row, n_col * sub // TILE)
     cols = jnp.where(live, tile_col, n_row * sub // TILE)
-    narrow, copies = round_block(block, n_row)
-
+    lines, others = lines_and_rest(n_row, n_col)
+
+    copies = jnp.broadcast_to(block.astype(BF16)[None], (n_row, NV, sub))
     band = swap(copies, "row")
-    before = swap(front(rows, cols, squares, band, narrow, n_col), "col")
+    before = swap(front(rows, cols, squares, band, block, n_col), "col")
     partial, owned = back(rows, cols, squares, before, n_row, sub)
     returned = swap(partial, "row")
     rest, message = carry(owned, returned, block, previous, coupling, n_row)
@@ -470,8 +463,8 @@
         rows, cols, squares, moved, before, rest, block, total, n_row
     )
     returned = swap(partial, "row")
-    rest, sums = local(owned, returned, current, block, upper, n_row)
-    parts = swap(spread(swap(sums, "row"), n_col), "col")
+    rest, sums = local(owned, returned, current, block, upper, len(lines[0]))
+    parts = swap(spread(swap(sums, BOTH, lines), len(others[0])), BOTH, others)
     found, current = last(parts, rest, current, found, total)
     return (current, found)
 

time: 193 us -> 191 us (0.990)
  blocking collectives: 157 us -> 155 us
    all_to_all x7, blocking collectives: 157 us -> 155 us  [swap(): lax.all_to_all(blocks, axis, 0, 0, tiled=True, axis_index_groups=groups)]
where the time goes in v7:
time: 191 us
  blocking collectives  155 us (81%)
  starting transfers between devices  13.8 us (7%)
  Pallas kernels  13.7 us (7%)
  local copies, waits for them, and re-layouts  5.29 us (3%)
    all_to_all x7, blocking collectives, swap(): lax.all_to_all(blocks, axis, 0, 0, tiled=True, axis_index_groups=groups)  155 us
    all_to_all x1, starting transfers between devices, swap(): lax.all_to_all(blocks, axis, 0, 0, tiled=True, axis_index_groups=groups)  13.8 us
  transfers between devices with their start and end apart: 1, of which 1 were waited for; matrix products, arithmetic and copies ran while one was open for 2% of the time, Pallas kernels for 0%

profile of v7, /device:TPU:1, one launch (start us, length us, event | category | flops | bytes accessed | tf_op | source)
XLA Modules:
  0.0 190.6 jit_solution(13914515219210852735)
XLA Ops:
  0.6 0.7 convert_element_type.3
  1.4 0.7 broadcast_in_dim.15
  2.0 13.8 %all-to-all-start = ((bf16[16,8,512]{2,1,0:T(8,128)(2,1)}), bf16[16,8,512]{2,1,0:T(8,128)(2,1)S(1)}, u32[]{:S(2)}, u32[]{:S(2)}) async-start(bf16[16,8,512]{2,1,0:T(8,128)(2,1)} %broadcast_in_dim.15), calls=%async_computation | async-start | bytes 262144 | tf_op jit(solution)/shard_map/all_to_all | solution.py:428
  16.5 1.6 copy.9
  18.1 0.0 copy-start.3
  18.1 0.0 copy-start.4
  18.1 0.0 copy-start
  18.1 3.0 %copy.13.tiles = bf16[128,64,64]{2,1,0:T(8,128)(2,1)S(1)} copy(bf16[128,64,64]{0,2,1:T(8,128)(2,1)S(1)} %bitcast.3) | data formatting | bytes 2097152 | tf_op jit(solution)/shard_map/reshape | solution.py:447
  21.1 0.0 copy-done.3
  21.1 0.0 copy-done.4
  21.2 0.9 all-to-all-done.band
  22.1 0.0 copy-done
  22.1 2.1 %front_tiles.1 = bf16[48,64,128]{2,1,0:T(8,128)(2,1)S(1)} custom-call(s32[128]{0:T(128)S(1)} %get-tuple-element.29.rows, s32[128]{0:T(128)S(1)} %get-tuple-element.28.cols, bf16[128,64,64]{2,1,0:T(8,128)(2,1)S(1)} %copy.13.tiles, bf16[16,8,512]{2,1,0:T(8,128)(2,1)S(1)} %all-to-all-done.band, f32[8,512]{1,0:T(8,128)S(1)} %copy-done), custom_call_target="tpu_custom_call" | custom-call | tf_op jit(solution)/shard_map/front_tiles/pallas_call | solution.py:169
  24.2 44.6 %all_to_all.40.moved.before = bf16[48,64,128]{2,1,0:T(8,128)(2,1)S(1)} all-to-all(bf16[48,64,128]{2,1,0:T(8,128)(2,1)S(1)} %front_tiles.1), channel_id=1, replica_groups=mesh['row'=16,'col'=48] {'col'}, dimensions={0} | all-to-all | bytes 1572864 | tf_op jit(solution)/shard_map/all_to_all | solution.py:428
  68.7 0.0 copy-start.1
  68.7 0.0 copy-start.2
  68.7 1.6 back_tiles.1
  70.3 15.3 %all_to_all.41.returned = f32[16,8,512]{2,1,0:T(8,128)S(1)} all-to-all(f32[16,8,512]{2,1,0:T(8,128)S(1)} %get-tuple-element.16), channel_id=1, replica_groups=mesh['row'=16,'col'=48] {'row'}, dimensions={0} | all-to-all | bytes 524288 | tf_op jit(solution)/shard_map/all_to_all | solution.py:428
  85.6 0.0 copy-done.1
  85.6 0.0 copy-done.2
  85.6 0.4 local_carry.1
  86.0 11.2 %all_to_all.42.got = f32[16,8,640]{2,1,0:T(8,128)S(1)} all-to-all(f32[16,8,640]{2,1,0:T(8,128)S(1)} %get-tuple-element.17), channel_id=1, replica_groups=mesh['row'=16,'col'=48] {'row'}, dimensions={0} | all-to-all | bytes 655360 | tf_op jit(solution)/shard_map/all_to_all | solution.py:428
  97.2 3.3 %whiten_tiles.1 = bf16[48,72,128]{2,1,0:T(8,128)(2,1)S(1)} custom-call(s32[128]{0:T(128)S(1)} %get-tuple-element.29.rows, s32[128]{0:T(128)S(1)} %get-tuple-element.28.cols, bf16[128,64,64]{2,1,0:T(8,128)(2,1)S(1)} %copy.13.tiles, f32[16,8,640]{2,1,0:T(8,128)S(1)} %all_to_all.42.got, f32[8,512]{1,0:T(8,128)S(1)} %get-tuple-element.18.rest), custom_call_target="tpu_custom_call" | custom-call | tf_op jit(solution)/shard_map/whiten_tiles/pallas_call | solution.py:296
  100.5 41.1 %all_to_all.43.moved = bf16[48,72,128]{2,1,0:T(8,128)(2,1)S(1)} all-to-all(bf16[48,72,128]{2,1,0:T(8,128)(2,1)S(1)} %whiten_tiles.1), channel_id=1, replica_groups=mesh['row'=16,'col'=48] {'col'}, dimensions={0} | all-to-all | bytes 1769472 | tf_op jit(solution)/shard_map/all_to_all | solution.py:428
  141.6 3.8 %settle_tiles.1 = (f32[16,8,512]{2,1,0:T(8,128)S(1)}, f32[8,512]{1,0:T(8,128)S(1)}, f32[8,512]{1,0:T(8,128)S(1)}, f32[8,8]{1,0:T(8,128)S(1)}, f32[2,8,8]{2,1,0:T(8,128)S(1)}) custom-call(s32[128]{0:T(128)S(1)} %get-tuple-element.29.rows, s32[128]{0:T(128)S(1)} %get-tuple-element.28.cols, bf16[128,64,64]{2,1,0:T(8,128)(2,1)S(1)} %copy.13.tiles, ...), custom_call_target="tpu_custom_call" | custom-call | tf_op jit(solution)/shard_map/settle_tiles/pallas_call | solution.py:367
  145.3 15.5 %all_to_all.44.returned = f32[16,8,512]{2,1,0:T(8,128)S(1)} all-to-all(f32[16,8,512]{2,1,0:T(8,128)S(1)} %get-tuple-element.20), channel_id=1, replica_groups=mesh['row'=16,'col'=48] {'row'}, dimensions={0} | all-to-all | bytes 524288 | tf_op jit(solution)/shard_map/all_to_all | solution.py:428
  160.8 0.5 local_sums.1
  161.3 15.6 %all_to_all.45.parts = f32[24,2,128]{2,1,0:T(2,128)S(1)} all-to-all(f32[24,2,128]{2,1,0:T(2,128)S(1)} %get-tuple-element.23), channel_id=1, replica_groups={{0,1,2,3,4,5,6,7,8,9,10,11,48,49,50,51,52,53,54,55,56,57,58,59},{12,13,..., dimensions={0} | all-to-all | bytes 49152 | tf_op jit(solution)/shard_map/all_to_all | solution.py:428
  176.9 11.5 %all_to_all.46.parts = f32[32,2,128]{2,1,0:T(2,128)S(1)} all-to-all(f32[32,2,128]{2,1,0:T(2,128)S(1)} %spread_sums.1), channel_id=1, replica_groups={{0,12,24,36,96,108,120,132,192,204,216,228,288,300,312,324,384,396,408,..., dimensions={0} | all-to-all | bytes 65536 | tf_op jit(solution)/shard_map/all_to_all | solution.py:428
  188.4 2.1 %last_block.1 = (f32[2,8,8]{2,1,0:T(8,128)}, f32[8,512]{1,0:T(8,128)}) custom-call(f32[32,2,128]{2,1,0:T(2,128)S(1)} %all_to_all.46.parts, f32[8,512]{1,0:T(8,128)S(1)} %get-tuple-element.24.rest, f32[8,512]{1,0:T(8,128)S(1)} %get-tuple-element.21.current, f32[2,8,8]{2,1,0:T(8,128)S(1)} %get-tuple-element.25.found), custom_call_target="tpu_custom_call" | custom-call | tf_op jit(solution)/shard_map/last_block/pallas_call | solution.py:414
  (2 shorter events, 0.0 us)
Async XLA Ops:
  2.0 20.0 %all-to-all-start = ((bf16[16,8,512]{2,1,0:T(8,128)(2,1)}), bf16[16,8,512]{2,1,0:T(8,128)(2,1)S(1)}, u32[]{:S(2)}, u32[]{:S(2)}) async-start(bf16[16,8,512]{2,1,0:T(8,128)(2,1)} %broadcast_in_dim.15), calls=%async_computation | async-start | bytes 262144 | tf_op jit(solution)/shard_map/all_to_all | solution.py:428
  18.1 3.0 %copy-start.3 = (s32[128]{0:T(128)S(1)}, s32[128]{0:T(128)}, u32[]{:S(2)}) copy-start(s32[128]{0:T(128)} %param.9) | copy-start | bytes 1540
  18.1 3.0 %copy-start.4 = (s32[128]{0:T(128)S(1)}, s32[128]{0:T(128)}, u32[]{:S(2)}) copy-start(s32[128]{0:T(128)} %param.8) | copy-start | bytes 1540
  18.1 3.9 %copy-start = (f32[8,512]{1,0:T(8,128)S(1)}, f32[8,512]{1,0:T(8,128)}, u32[]{:S(2)}) copy-start(f32[8,512]{1,0:T(8,128)} %prior.3) | copy-start | bytes 49156
  68.7 16.9 %copy-start.1 = (f32[8,512]{1,0:T(8,128)S(1)}, f32[8,512]{1,0:T(8,128)}, u32[]{:S(2)}) copy-start(f32[8,512]{1,0:T(8,128)} %prior.2) | copy-start | bytes 49156
  68.7 16.9 %copy-start.2 = (f32[8,8]{1,0:T(8,128)S(1)}, f32[8,8]{1,0:T(8,128)}, u32[]{:S(2)}) copy-start(f32[8,8]{1,0:T(8,128)} %beta.1) | copy-start | bytes 772

commit v8 on v7

--- a/solution.py
+++ b/solution.py
@@ -82,11 +82,13 @@
     lane = lax.broadcasted_iota(jnp.int32, (NV, 2 * NV), 1)
     unit = jnp.where(row + NV == lane, 1.0, 0.0).astype(F32)
     work = jnp.concatenate([gram, unit[:, NV:]], axis=1)
+    scales = jnp.zeros((NV, 2 * NV), F32)
     for j in range(NV):
-        scale = 1.0 / jnp.sqrt(work[j : j + 1, j : j + 1])
-        scaled = work[j : j + 1, :] * scale
-        column = work[:, j : j + 1] * scale
-        work = jnp.where(row == j, scaled, jnp.where(row > j, work - column * scaled, work))
+        column = work[:, j : j + 1]
+        inverse = 1.0 / column[j : j + 1]
+        scales = jnp.where(row == j, inverse, scales)
+        work = jnp.where(row > j, work - column * (work[j : j + 1] * inverse), work)
+    work = work * jnp.sqrt(scales)
     return jnp.where(row <= lane, work, 0.0)[:, :NV], work[:, NV:]
 
 
@@ -191,7 +193,7 @@
     owned[...] = jnp.concatenate(gathered, axis=1)
     accumulate(rows, cols, tiles, across_pairs, sums, BEHIND)
     for segment in range(back.shape[0]):
-        back[segment] = segment_of(sums, segment, per)
+        back[segment] = segment_of(sums, segment, per).astype(BF16)
 
 
 def back(rows, cols, tiles, moved, n_row, sub):
@@ -199,7 +201,7 @@
     return pl.pallas_call(
         back_kernel,
         out_shape=(
-            jax.ShapeDtypeStruct((n_row, NV, sub), F32),
+            jax.ShapeDtypeStruct((n_row, NV, sub), BF16),
             jax.ShapeDtypeStruct((NV, sub), F32),
         ),
         in_specs=[SMEM, SMEM, VMEM, VMEM],
@@ -211,7 +213,7 @@
 
 
 def rest_and_sums(owned, returned, current, prior, beta):
-    image = owned[...] + jnp.sum(returned[...], axis=0)
+    image = owned[...] + jnp.sum(returned[...].astype(F32), axis=0)
     now = current[...]
     rest = image - dot(beta[...], prior[...])
     left = jnp.concatenate([now, rest], axis=0)
@@ -283,7 +285,7 @@
     own = mix(inverse, rest[...]).astype(BF16)
     twice = jnp.concatenate([lower, lower], axis=1)
     beside = jnp.concatenate(pieces(summed, 3) + pieces(twice, 2), axis=1)
-    accumulate(cols, rows, tiles, band_pairs, sums, AHEAD)
+    accumulate(cols, rows, tiles, band_pairs, sums, AHEAD, split=2)
     per = sub // LANES
     put_message(message, own, sums, per)
     for segment in range(message.shape[0]):
@@ -358,7 +360,7 @@
     end_pairs(across_pairs)
     accumulate(rows, cols, tiles, across_pairs, sums, BEHIND, split=2)
     for segment in range(back.shape[0]):
-        back[segment] = segment_of(sums, segment, per)
+        back[segment] = segment_of(sums, segment, per).astype(BF16)
 
 
 def settle(rows, cols, tiles, moved, before, rest, current, total, n_row):
@@ -367,7 +369,7 @@
     return pl.pallas_call(
         functools.partial(settle_kernel, total),
         out_shape=(
-            jax.ShapeDtypeStruct((n_row, NV, sub), F32),
+            jax.ShapeDtypeStruct((n_row, NV, sub), BF16),
             jax.ShapeDtypeStruct((NV, sub), F32),
             jax.ShapeDtypeStruct((NV, sub), F32),
             jax.ShapeDtypeStruct((NV, NV), F32),

time: 191 us -> 188 us (0.984)
  blocking collectives: 155 us -> 152 us
    all_to_all x7, blocking collectives: 155 us -> 152 us  [swap(): lax.all_to_all(blocks, axis, 0, 0, tiled=True, axis_index_groups=groups)]
where the time goes in v8:
time: 188 us
  blocking collectives  152 us (81%)
  starting transfers between devices  13.8 us (7%)
  Pallas kernels  13.7 us (7%)
  local copies, waits for them, and re-layouts  5.3 us (3%)
    all_to_all x7, blocking collectives, swap(): lax.all_to_all(blocks, axis, 0, 0, tiled=True, axis_index_groups=groups)  152 us
    all_to_all x1, starting transfers between devices, swap(): lax.all_to_all(blocks, axis, 0, 0, tiled=True, axis_index_groups=groups)  13.8 us
    pallas_call x1, Pallas kernels, settle(): pl.pallas_call(functools.partial(settle_kernel, total), out_shape=(jax.Sh...  3.79 us
  transfers between devices with their start and end apart: 1, of which 1 were waited for; matrix products, arithmetic and copies ran while one was open for 2% of the time, Pallas kernels for 0%

profile of v8, /device:TPU:1, one launch (start us, length us, event | category | flops | bytes accessed | tf_op | source)
XLA Modules:
  0.0 187.7 jit_solution(11612105877477675920)
XLA Ops:
  0.6 0.7 convert_element_type.3
  1.4 0.7 broadcast_in_dim.15
  2.0 13.8 %all-to-all-start = ((bf16[16,8,512]{2,1,0:T(8,128)(2,1)}), bf16[16,8,512]{2,1,0:T(8,128)(2,1)S(1)}, u32[]{:S(2)}, u32[]{:S(2)}) async-start(bf16[16,8,512]{2,1,0:T(8,128)(2,1)} %broadcast_in_dim.15), calls=%async_computation | async-start | bytes 262144 | tf_op jit(solution)/shard_map/all_to_all | solution.py:430
  16.5 1.6 copy.9
  18.1 0.0 copy-start.3
  18.1 0.0 copy-start.4
  18.1 0.0 copy-start
  18.1 3.0 %copy.13.tiles = bf16[128,64,64]{2,1,0:T(8,128)(2,1)S(1)} copy(bf16[128,64,64]{0,2,1:T(8,128)(2,1)S(1)} %bitcast.3) | data formatting | bytes 2097152 | tf_op jit(solution)/shard_map/reshape | solution.py:449
  21.1 0.0 copy-done.3
  21.1 0.0 copy-done.4
  21.2 0.9 all-to-all-done.band
  22.1 0.0 copy-done
  22.1 2.1 %front_tiles.1 = bf16[48,64,128]{2,1,0:T(8,128)(2,1)S(1)} custom-call(s32[128]{0:T(128)S(1)} %get-tuple-element.29.rows, s32[128]{0:T(128)S(1)} %get-tuple-element.28.cols, bf16[128,64,64]{2,1,0:T(8,128)(2,1)S(1)} %copy.13.tiles, bf16[16,8,512]{2,1,0:T(8,128)(2,1)S(1)} %all-to-all-done.band, f32[8,512]{1,0:T(8,128)S(1)} %copy-done), custom_call_target="tpu_custom_call" | custom-call | tf_op jit(solution)/shard_map/front_tiles/pallas_call | solution.py:171
  24.2 0.0 copy-start.1
  24.2 0.0 copy-start.2
  24.2 44.5 %all_to_all.40.moved.before = bf16[48,64,128]{2,1,0:T(8,128)(2,1)S(1)} all-to-all(bf16[48,64,128]{2,1,0:T(8,128)(2,1)S(1)} %front_tiles.1), channel_id=1, replica_groups=mesh['row'=16,'col'=48] {'col'}, dimensions={0} | all-to-all | bytes 1572864 | tf_op jit(solution)/shard_map/all_to_all | solution.py:430
  68.7 1.6 back_tiles.1
  70.3 14.2 %all_to_all.41.returned = bf16[16,8,512]{2,1,0:T(8,128)(2,1)S(1)} all-to-all(bf16[16,8,512]{2,1,0:T(8,128)(2,1)S(1)} %get-tuple-element.16), channel_id=1, replica_groups=mesh['row'=16,'col'=48] {'row'}, dimensions={0} | all-to-all | bytes 262144 | tf_op jit(solution)/shard_map/all_to_all | solution.py:430
  84.5 0.0 copy-done.1
  84.5 0.0 copy-done.2
  84.5 0.4 local_carry.1
  84.9 10.8 %all_to_all.42.got = f32[16,8,640]{2,1,0:T(8,128)S(1)} all-to-all(f32[16,8,640]{2,1,0:T(8,128)S(1)} %get-tuple-element.17), channel_id=1, replica_groups=mesh['row'=16,'col'=48] {'row'}, dimensions={0} | all-to-all | bytes 655360 | tf_op jit(solution)/shard_map/all_to_all | solution.py:430
  95.8 3.3 %whiten_tiles.1 = bf16[48,72,128]{2,1,0:T(8,128)(2,1)S(1)} custom-call(s32[128]{0:T(128)S(1)} %get-tuple-element.29.rows, s32[128]{0:T(128)S(1)} %get-tuple-element.28.cols, bf16[128,64,64]{2,1,0:T(8,128)(2,1)S(1)} %copy.13.tiles, f32[16,8,640]{2,1,0:T(8,128)S(1)} %all_to_all.42.got, f32[8,512]{1,0:T(8,128)S(1)} %get-tuple-element.18.rest), custom_call_target="tpu_custom_call" | custom-call | tf_op jit(solution)/shard_map/whiten_tiles/pallas_call | solution.py:298
  99.1 41.1 %all_to_all.43.moved = bf16[48,72,128]{2,1,0:T(8,128)(2,1)S(1)} all-to-all(bf16[48,72,128]{2,1,0:T(8,128)(2,1)S(1)} %whiten_tiles.1), channel_id=1, replica_groups=mesh['row'=16,'col'=48] {'col'}, dimensions={0} | all-to-all | bytes 1769472 | tf_op jit(solution)/shard_map/all_to_all | solution.py:430
  140.2 3.8 %settle_tiles.1 = (bf16[16,8,512]{2,1,0:T(8,128)(2,1)S(1)}, f32[8,512]{1,0:T(8,128)S(1)}, f32[8,512]{1,0:T(8,128)S(1)}, f32[8,8]{1,0:T(8,128)S(1)}, f32[2,8,8]{2,1,0:T(8,128)S(1)}) custom-call(s32[128]{0:T(128)S(1)} %get-tuple-element.29.rows, s32[128]{0:T(128)S(1)} %get-tuple-element.28.cols, bf16[128,64,64]{2,1,0:T(8,128)(2,1)S(1)} %copy.13.tiles, ...), custom_call_target="tpu_custom_call" | custom-call | tf_op jit(solution)/shard_map/settle_tiles/pallas_call | solution.py:369
  144.0 14.4 %all_to_all.44.returned = bf16[16,8,512]{2,1,0:T(8,128)(2,1)S(1)} all-to-all(bf16[16,8,512]{2,1,0:T(8,128)(2,1)S(1)} %get-tuple-element.20), channel_id=1, replica_groups=mesh['row'=16,'col'=48] {'row'}, dimensions={0} | all-to-all | bytes 262144 | tf_op jit(solution)/shard_map/all_to_all | solution.py:430
  158.4 0.5 local_sums.1
  158.9 15.1 %all_to_all.45.parts = f32[24,2,128]{2,1,0:T(2,128)S(1)} all-to-all(f32[24,2,128]{2,1,0:T(2,128)S(1)} %get-tuple-element.23), channel_id=1, replica_groups={{0,1,2,3,4,5,6,7,8,9,10,11,48,49,50,51,52,53,54,55,56,57,58,59},{12,13,..., dimensions={0} | all-to-all | bytes 49152 | tf_op jit(solution)/shard_map/all_to_all | solution.py:430
  174.1 11.5 %all_to_all.46.parts = f32[32,2,128]{2,1,0:T(2,128)S(1)} all-to-all(f32[32,2,128]{2,1,0:T(2,128)S(1)} %spread_sums.1), channel_id=1, replica_groups={{0,12,24,36,96,108,120,132,192,204,216,228,288,300,312,324,384,396,408,..., dimensions={0} | all-to-all | bytes 65536 | tf_op jit(solution)/shard_map/all_to_all | solution.py:430
  185.6 2.1 %last_block.1 = (f32[2,8,8]{2,1,0:T(8,128)}, f32[8,512]{1,0:T(8,128)}) custom-call(f32[32,2,128]{2,1,0:T(2,128)S(1)} %all_to_all.46.parts, f32[8,512]{1,0:T(8,128)S(1)} %get-tuple-element.24.rest, f32[8,512]{1,0:T(8,128)S(1)} %get-tuple-element.21.current, f32[2,8,8]{2,1,0:T(8,128)S(1)} %get-tuple-element.25.found), custom_call_target="tpu_custom_call" | custom-call | tf_op jit(solution)/shard_map/last_block/pallas_call | solution.py:416
  (2 shorter events, 0.0 us)
Async XLA Ops:
  2.0 20.0 %all-to-all-start = ((bf16[16,8,512]{2,1,0:T(8,128)(2,1)}), bf16[16,8,512]{2,1,0:T(8,128)(2,1)S(1)}, u32[]{:S(2)}, u32[]{:S(2)}) async-start(bf16[16,8,512]{2,1,0:T(8,128)(2,1)} %broadcast_in_dim.15), calls=%async_computation | async-start | bytes 262144 | tf_op jit(solution)/shard_map/all_to_all | solution.py:430
  18.1 3.0 %copy-start.3 = (s32[128]{0:T(128)S(1)}, s32[128]{0:T(128)}, u32[]{:S(2)}) copy-start(s32[128]{0:T(128)} %param.9) | copy-start | bytes 1540
  18.1 3.0 %copy-start.4 = (s32[128]{0:T(128)S(1)}, s32[128]{0:T(128)}, u32[]{:S(2)}) copy-start(s32[128]{0:T(128)} %param.8) | copy-start | bytes 1540
  18.1 3.9 %copy-start = (f32[8,512]{1,0:T(8,128)S(1)}, f32[8,512]{1,0:T(8,128)}, u32[]{:S(2)}) copy-start(f32[8,512]{1,0:T(8,128)} %prior.3) | copy-start | bytes 49156
  24.2 60.4 %copy-start.1 = (f32[8,512]{1,0:T(8,128)S(1)}, f32[8,512]{1,0:T(8,128)}, u32[]{:S(2)}) copy-start(f32[8,512]{1,0:T(8,128)} %prior.2) | copy-start | bytes 49156
  24.2 60.4 %copy-start.2 = (f32[8,8]{1,0:T(8,128)S(1)}, f32[8,8]{1,0:T(8,128)}, u32[]{:S(2)}) copy-start(f32[8,8]{1,0:T(8,128)} %beta.1) | copy-start | bytes 772

commit v9 on v8

--- a/solution.py
+++ b/solution.py
@@ -426,6 +426,25 @@
     )(parts, rest, current, found)
 
 
+def round_kernel(block, copies, held, done):
+    fetch = pltpu.make_async_copy(block, held, done)
+    fetch.start()
+    fetch.wait()
+    copies[...] = jnp.broadcast_to(held[...].astype(BF16)[None], copies.shape)
+
+
+def round_block(block, n_row):
+    return pl.pallas_call(
+        round_kernel,
+        out_shape=jax.ShapeDtypeStruct((n_row, *block.shape), BF16),
+        in_specs=[pl.BlockSpec(memory_space=pltpu.HBM)],
+        out_specs=VMEM,
+        scratch_shapes=[pltpu.VMEM(block.shape, F32), pltpu.SemaphoreType.DMA],
+        compiler_params=pltpu.CompilerParams(vmem_limit_bytes=63 * 1024 * 1024),
+        name="round_block",
+    )(block)
+
+
 def swap(blocks, axis, groups=None):
     return lax.all_to_all(blocks, axis, 0, 0, tiled=True, axis_index_groups=groups)
 
@@ -452,8 +471,7 @@
     cols = jnp.where(live, tile_col, n_row * sub // TILE)
     lines, others = lines_and_rest(n_row, n_col)
 
-    copies = jnp.broadcast_to(block.astype(BF16)[None], (n_row, NV, sub))
-    band = swap(copies, "row")
+    band = swap(round_block(block, n_row), "row")
     before = swap(front(rows, cols, squares, band, block, n_col), "col")
     partial, owned = back(rows, cols, squares, before, n_row, sub)
     returned = swap(partial, "row")

time: 188 us -> 188 us (level)
  no operation moved by 1% of the time
where the time goes in v9:
time: 188 us
  blocking collectives  152 us (81%)
  Pallas kernels  15.2 us (8%)
  starting transfers between devices  13.8 us (7%)
  local copies, waits for them, and re-layouts  4.64 us (2%)
    all_to_all x7, blocking collectives, swap(): lax.all_to_all(blocks, axis, 0, 0, tiled=True, axis_index_groups=groups)  152 us
    all_to_all x1, starting transfers between devices, swap(): lax.all_to_all(blocks, axis, 0, 0, tiled=True, axis_index_groups=groups)  13.8 us
    pallas_call x1, Pallas kernels, settle(): pl.pallas_call(functools.partial(settle_kernel, total), out_shape=(jax.Sh...  3.8 us
  transfers between devices with their start and end apart: 1, of which 1 were waited for; matrix products, arithmetic and copies ran while one was open for 2% of the time, Pallas kernels for 0%

profile of v9, /device:TPU:1, one launch (start us, length us, event | category | flops | bytes accessed | tf_op | source)
XLA Modules:
  0.0 187.8 jit_solution(4338958228884683704)
XLA Ops:
  0.6 1.4 round_block.1
  2.0 13.8 %all-to-all-start = ((bf16[16,8,512]{2,1,0:T(8,128)(2,1)}), bf16[16,8,512]{2,1,0:T(8,128)(2,1)S(1)}, u32[]{:S(2)}, u32[]{:S(2)}) async-start(bf16[16,8,512]{2,1,0:T(8,128)(2,1)} %round_block.1), calls=%async_computation | async-start | bytes 262144 | tf_op jit(solution)/shard_map/all_to_all | solution.py:449
  16.5 1.6 copy.9
  18.1 0.0 copy-start.3
  18.1 0.0 copy-start.4
  18.1 0.0 copy-start
  18.2 3.0 %copy.13.tiles = bf16[128,64,64]{2,1,0:T(8,128)(2,1)S(1)} copy(bf16[128,64,64]{0,2,1:T(8,128)(2,1)S(1)} %bitcast.3) | data formatting | bytes 2097152 | tf_op jit(solution)/shard_map/reshape | solution.py:468
  21.2 0.0 copy-done.3
  21.2 0.0 copy-done.4
  21.2 0.9 all-to-all-done.band
  22.1 0.0 copy-done
  22.1 2.1 %front_tiles.1 = bf16[48,64,128]{2,1,0:T(8,128)(2,1)S(1)} custom-call(s32[128]{0:T(128)S(1)} %get-tuple-element.29.rows, s32[128]{0:T(128)S(1)} %get-tuple-element.28.cols, bf16[128,64,64]{2,1,0:T(8,128)(2,1)S(1)} %copy.13.tiles, bf16[16,8,512]{2,1,0:T(8,128)(2,1)S(1)} %all-to-all-done.band, f32[8,512]{1,0:T(8,128)S(1)} %copy-done), custom_call_target="tpu_custom_call" | custom-call | tf_op jit(solution)/shard_map/front_tiles/pallas_call | solution.py:171
  24.2 0.0 copy-start.1
  24.2 0.0 copy-start.2
  24.2 44.5 %all_to_all.40.moved.before = bf16[48,64,128]{2,1,0:T(8,128)(2,1)S(1)} all-to-all(bf16[48,64,128]{2,1,0:T(8,128)(2,1)S(1)} %front_tiles.1), channel_id=1, replica_groups=mesh['row'=16,'col'=48] {'col'}, dimensions={0} | all-to-all | bytes 1572864 | tf_op jit(solution)/shard_map/all_to_all | solution.py:449
  68.7 1.6 back_tiles.1
  70.4 14.4 %all_to_all.41.returned = bf16[16,8,512]{2,1,0:T(8,128)(2,1)S(1)} all-to-all(bf16[16,8,512]{2,1,0:T(8,128)(2,1)S(1)} %get-tuple-element.16), channel_id=1, replica_groups=mesh['row'=16,'col'=48] {'row'}, dimensions={0} | all-to-all | bytes 262144 | tf_op jit(solution)/shard_map/all_to_all | solution.py:449
  84.8 0.0 copy-done.1
  84.8 0.0 copy-done.2
  84.8 0.4 local_carry.1
  85.2 10.8 %all_to_all.42.got = f32[16,8,640]{2,1,0:T(8,128)S(1)} all-to-all(f32[16,8,640]{2,1,0:T(8,128)S(1)} %get-tuple-element.17), channel_id=1, replica_groups=mesh['row'=16,'col'=48] {'row'}, dimensions={0} | all-to-all | bytes 655360 | tf_op jit(solution)/shard_map/all_to_all | solution.py:449
  96.0 3.3 %whiten_tiles.1 = bf16[48,72,128]{2,1,0:T(8,128)(2,1)S(1)} custom-call(s32[128]{0:T(128)S(1)} %get-tuple-element.29.rows, s32[128]{0:T(128)S(1)} %get-tuple-element.28.cols, bf16[128,64,64]{2,1,0:T(8,128)(2,1)S(1)} %copy.13.tiles, f32[16,8,640]{2,1,0:T(8,128)S(1)} %all_to_all.42.got, f32[8,512]{1,0:T(8,128)S(1)} %get-tuple-element.18.rest), custom_call_target="tpu_custom_call" | custom-call | tf_op jit(solution)/shard_map/whiten_tiles/pallas_call | solution.py:298
  99.3 41.0 %all_to_all.43.moved = bf16[48,72,128]{2,1,0:T(8,128)(2,1)S(1)} all-to-all(bf16[48,72,128]{2,1,0:T(8,128)(2,1)S(1)} %whiten_tiles.1), channel_id=1, replica_groups=mesh['row'=16,'col'=48] {'col'}, dimensions={0} | all-to-all | bytes 1769472 | tf_op jit(solution)/shard_map/all_to_all | solution.py:449
  140.3 3.8 %settle_tiles.1 = (bf16[16,8,512]{2,1,0:T(8,128)(2,1)S(1)}, f32[8,512]{1,0:T(8,128)S(1)}, f32[8,512]{1,0:T(8,128)S(1)}, f32[8,8]{1,0:T(8,128)S(1)}, f32[2,8,8]{2,1,0:T(8,128)S(1)}) custom-call(s32[128]{0:T(128)S(1)} %get-tuple-element.29.rows, s32[128]{0:T(128)S(1)} %get-tuple-element.28.cols, bf16[128,64,64]{2,1,0:T(8,128)(2,1)S(1)} %copy.13.tiles, ...), custom_call_target="tpu_custom_call" | custom-call | tf_op jit(solution)/shard_map/settle_tiles/pallas_call | solution.py:369
  144.1 14.5 %all_to_all.44.returned = bf16[16,8,512]{2,1,0:T(8,128)(2,1)S(1)} all-to-all(bf16[16,8,512]{2,1,0:T(8,128)(2,1)S(1)} %get-tuple-element.20), channel_id=1, replica_groups=mesh['row'=16,'col'=48] {'row'}, dimensions={0} | all-to-all | bytes 262144 | tf_op jit(solution)/shard_map/all_to_all | solution.py:449
  158.6 0.5 local_sums.1
  159.1 15.0 %all_to_all.45.parts = f32[24,2,128]{2,1,0:T(2,128)S(1)} all-to-all(f32[24,2,128]{2,1,0:T(2,128)S(1)} %get-tuple-element.23), channel_id=1, replica_groups={{0,1,2,3,4,5,6,7,8,9,10,11,48,49,50,51,52,53,54,55,56,57,58,59},{12,13,..., dimensions={0} | all-to-all | bytes 49152 | tf_op jit(solution)/shard_map/all_to_all | solution.py:449
  174.2 11.5 %all_to_all.46.parts = f32[32,2,128]{2,1,0:T(2,128)S(1)} all-to-all(f32[32,2,128]{2,1,0:T(2,128)S(1)} %spread_sums.1), channel_id=1, replica_groups={{0,12,24,36,96,108,120,132,192,204,216,228,288,300,312,324,384,396,408,..., dimensions={0} | all-to-all | bytes 65536 | tf_op jit(solution)/shard_map/all_to_all | solution.py:449
  185.7 2.1 %last_block.1 = (f32[2,8,8]{2,1,0:T(8,128)}, f32[8,512]{1,0:T(8,128)}) custom-call(f32[32,2,128]{2,1,0:T(2,128)S(1)} %all_to_all.46.parts, f32[8,512]{1,0:T(8,128)S(1)} %get-tuple-element.24.rest, f32[8,512]{1,0:T(8,128)S(1)} %get-tuple-element.21.current, f32[2,8,8]{2,1,0:T(8,128)S(1)} %get-tuple-element.25.found), custom_call_target="tpu_custom_call" | custom-call | tf_op jit(solution)/shard_map/last_block/pallas_call | solution.py:416
  (2 shorter events, 0.0 us)
Async XLA Ops:
  2.0 20.1 %all-to-all-start = ((bf16[16,8,512]{2,1,0:T(8,128)(2,1)}), bf16[16,8,512]{2,1,0:T(8,128)(2,1)S(1)}, u32[]{:S(2)}, u32[]{:S(2)}) async-start(bf16[16,8,512]{2,1,0:T(8,128)(2,1)} %round_block.1), calls=%async_computation | async-start | bytes 262144 | tf_op jit(solution)/shard_map/all_to_all | solution.py:449
  18.1 3.0 %copy-start.3 = (s32[128]{0:T(128)S(1)}, s32[128]{0:T(128)}, u32[]{:S(2)}) copy-start(s32[128]{0:T(128)} %param.9) | copy-start | bytes 1540
  18.1 3.0 %copy-start.4 = (s32[128]{0:T(128)S(1)}, s32[128]{0:T(128)}, u32[]{:S(2)}) copy-start(s32[128]{0:T(128)} %param.8) | copy-start | bytes 1540
  18.1 3.9 %copy-start = (f32[8,512]{1,0:T(8,128)S(1)}, f32[8,512]{1,0:T(8,128)}, u32[]{:S(2)}) copy-start(f32[8,512]{1,0:T(8,128)} %prior.3) | copy-start | bytes 49156
  24.2 60.6 %copy-start.1 = (f32[8,512]{1,0:T(8,128)S(1)}, f32[8,512]{1,0:T(8,128)}, u32[]{:S(2)}) copy-start(f32[8,512]{1,0:T(8,128)} %prior.2) | copy-start | bytes 49156
  24.2 60.6 %copy-start.2 = (f32[8,8]{1,0:T(8,128)S(1)}, f32[8,8]{1,0:T(8,128)}, u32[]{:S(2)}) copy-start(f32[8,8]{1,0:T(8,128)} %beta.1) | copy-start | bytes 772

commit v10 on v8

--- a/solution.py
+++ b/solution.py
@@ -97,7 +97,7 @@
     mixed = summed[:, NV : 2 * NV]
     own = summed[:, 2 * NV : 3 * NV]
     square = summed[:, 3 * NV : 4 * NV]
-    gram = square - dot_tn(alpha, mixed) - dot_tn(mixed, alpha) + dot_tn(alpha, dot(own, alpha))
+    gram = square + dot_tn(alpha, mix(own, alpha) - mixed) - dot_tn(mixed, alpha)
     return (alpha, *factor(gram))
 
 
@@ -327,7 +327,7 @@
     alphas[...] = jnp.zeros_like(alphas)
     alphas[0] = alpha
     turn = -dot_t(inverse, alpha)
-    following[...] = dot(inverse, rest[...] - dot_tn(alpha, current[...]))
+    following[...] = mix(inverse, rest[...] - dot_tn(alpha, current[...]))
     columns = [jnp.broadcast_to(inverse[:, v : v + 1], (NV, LANES)) for v in range(NV)]
     four = 4 * NV
     lane = lax.broadcasted_iota(jnp.int32, (NV, four), 1)
@@ -409,7 +409,7 @@
     alpha, _, inverse = factor_of_sums(summed)
     alphas[...] = found[...]
     alphas[STEPS - 1] = alpha
-    following[...] = dot(inverse, rest[...] - dot_tn(alpha, current[...]))
+    following[...] = mix(inverse, rest[...] - dot_tn(alpha, current[...]))
 
 
 def last(parts, rest, current, found, total):

time: 188 us -> 188 us (level)
  no operation moved by 1% of the time
where the time goes in v10:
time: 188 us; the launch traced here: 187 us
  blocking collectives  152 us (81%)
  starting transfers between devices  13.8 us (7%)
  Pallas kernels  13.3 us (7%)
  local copies, waits for them, and re-layouts  5.3 us (3%)
    all_to_all x7, blocking collectives, swap(): lax.all_to_all(blocks, axis, 0, 0, tiled=True, axis_index_groups=groups)  152 us
    all_to_all x1, starting transfers between devices, swap(): lax.all_to_all(blocks, axis, 0, 0, tiled=True, axis_index_groups=groups)  13.8 us
  transfers between devices with their start and end apart: 1, of which 1 were waited for; matrix products, arithmetic and copies ran while one was open for 2% of the time, Pallas kernels for 0%

profile of v10, /device:TPU:1, one launch (start us, length us, event | category | flops | bytes accessed | tf_op | source)
XLA Modules:
  0.0 187.5 jit_solution(1578825992775388486)
XLA Ops:
  0.6 0.7 convert_element_type.3
  1.4 0.7 broadcast_in_dim.15
  2.0 13.8 %all-to-all-start = ((bf16[16,8,512]{2,1,0:T(8,128)(2,1)}), bf16[16,8,512]{2,1,0:T(8,128)(2,1)S(1)}, u32[]{:S(2)}, u32[]{:S(2)}) async-start(bf16[16,8,512]{2,1,0:T(8,128)(2,1)} %broadcast_in_dim.15), calls=%async_computation | async-start | bytes 262144 | tf_op jit(solution)/shard_map/all_to_all | solution.py:430
  16.5 1.6 copy.9
  18.1 0.0 copy-start.3
  18.1 0.0 copy-start.4
  18.1 0.0 copy-start
  18.1 3.0 %copy.13.tiles = bf16[128,64,64]{2,1,0:T(8,128)(2,1)S(1)} copy(bf16[128,64,64]{0,2,1:T(8,128)(2,1)S(1)} %bitcast.3) | data formatting | bytes 2097152 | tf_op jit(solution)/shard_map/reshape | solution.py:449
  21.1 0.0 copy-done.3
  21.1 0.0 copy-done.4
  21.2 0.9 all-to-all-done.band
  22.1 0.0 copy-done
  22.1 2.1 %front_tiles.1 = bf16[48,64,128]{2,1,0:T(8,128)(2,1)S(1)} custom-call(s32[128]{0:T(128)S(1)} %get-tuple-element.29.rows, s32[128]{0:T(128)S(1)} %get-tuple-element.28.cols, bf16[128,64,64]{2,1,0:T(8,128)(2,1)S(1)} %copy.13.tiles, bf16[16,8,512]{2,1,0:T(8,128)(2,1)S(1)} %all-to-all-done.band, f32[8,512]{1,0:T(8,128)S(1)} %copy-done), custom_call_target="tpu_custom_call" | custom-call | tf_op jit(solution)/shard_map/front_tiles/pallas_call | solution.py:171
  24.2 0.0 copy-start.1
  24.2 0.0 copy-start.2
  24.2 44.6 %all_to_all.40.moved.before = bf16[48,64,128]{2,1,0:T(8,128)(2,1)S(1)} all-to-all(bf16[48,64,128]{2,1,0:T(8,128)(2,1)S(1)} %front_tiles.1), channel_id=1, replica_groups=mesh['row'=16,'col'=48] {'col'}, dimensions={0} | all-to-all | bytes 1572864 | tf_op jit(solution)/shard_map/all_to_all | solution.py:430
  68.7 1.6 back_tiles.1
  70.3 14.4 %all_to_all.41.returned = bf16[16,8,512]{2,1,0:T(8,128)(2,1)S(1)} all-to-all(bf16[16,8,512]{2,1,0:T(8,128)(2,1)S(1)} %get-tuple-element.16), channel_id=1, replica_groups=mesh['row'=16,'col'=48] {'row'}, dimensions={0} | all-to-all | bytes 262144 | tf_op jit(solution)/shard_map/all_to_all | solution.py:430
  84.7 0.0 copy-done.1
  84.7 0.0 copy-done.2
  84.7 0.4 local_carry.1
  85.1 10.8 %all_to_all.42.got = f32[16,8,640]{2,1,0:T(8,128)S(1)} all-to-all(f32[16,8,640]{2,1,0:T(8,128)S(1)} %get-tuple-element.17), channel_id=1, replica_groups=mesh['row'=16,'col'=48] {'row'}, dimensions={0} | all-to-all | bytes 655360 | tf_op jit(solution)/shard_map/all_to_all | solution.py:430
  96.0 3.3 %whiten_tiles.1 = bf16[48,72,128]{2,1,0:T(8,128)(2,1)S(1)} custom-call(s32[128]{0:T(128)S(1)} %get-tuple-element.29.rows, s32[128]{0:T(128)S(1)} %get-tuple-element.28.cols, bf16[128,64,64]{2,1,0:T(8,128)(2,1)S(1)} %copy.13.tiles, f32[16,8,640]{2,1,0:T(8,128)S(1)} %all_to_all.42.got, f32[8,512]{1,0:T(8,128)S(1)} %get-tuple-element.18.rest), custom_call_target="tpu_custom_call" | custom-call | tf_op jit(solution)/shard_map/whiten_tiles/pallas_call | solution.py:298
  99.2 41.1 %all_to_all.43.moved = bf16[48,72,128]{2,1,0:T(8,128)(2,1)S(1)} all-to-all(bf16[48,72,128]{2,1,0:T(8,128)(2,1)S(1)} %whiten_tiles.1), channel_id=1, replica_groups=mesh['row'=16,'col'=48] {'col'}, dimensions={0} | all-to-all | bytes 1769472 | tf_op jit(solution)/shard_map/all_to_all | solution.py:430
  140.3 3.6 %settle_tiles.1 = (bf16[16,8,512]{2,1,0:T(8,128)(2,1)S(1)}, f32[8,512]{1,0:T(8,128)S(1)}, f32[8,512]{1,0:T(8,128)S(1)}, f32[8,8]{1,0:T(8,128)S(1)}, f32[2,8,8]{2,1,0:T(8,128)S(1)}) custom-call(s32[128]{0:T(128)S(1)} %get-tuple-element.29.rows, s32[128]{0:T(128)S(1)} %get-tuple-element.28.cols, bf16[128,64,64]{2,1,0:T(8,128)(2,1)S(1)} %copy.13.tiles, ...), custom_call_target="tpu_custom_call" | custom-call | tf_op jit(solution)/shard_map/settle_tiles/pallas_call | solution.py:369
  143.9 14.4 %all_to_all.44.returned = bf16[16,8,512]{2,1,0:T(8,128)(2,1)S(1)} all-to-all(bf16[16,8,512]{2,1,0:T(8,128)(2,1)S(1)} %get-tuple-element.20), channel_id=1, replica_groups=mesh['row'=16,'col'=48] {'row'}, dimensions={0} | all-to-all | bytes 262144 | tf_op jit(solution)/shard_map/all_to_all | solution.py:430
  158.3 0.5 local_sums.1
  158.8 15.2 %all_to_all.45.parts = f32[24,2,128]{2,1,0:T(2,128)S(1)} all-to-all(f32[24,2,128]{2,1,0:T(2,128)S(1)} %get-tuple-element.23), channel_id=1, replica_groups={{0,1,2,3,4,5,6,7,8,9,10,11,48,49,50,51,52,53,54,55,56,57,58,59},{12,13,..., dimensions={0} | all-to-all | bytes 49152 | tf_op jit(solution)/shard_map/all_to_all | solution.py:430
  174.0 11.5 %all_to_all.46.parts = f32[32,2,128]{2,1,0:T(2,128)S(1)} all-to-all(f32[32,2,128]{2,1,0:T(2,128)S(1)} %spread_sums.1), channel_id=1, replica_groups={{0,12,24,36,96,108,120,132,192,204,216,228,288,300,312,324,384,396,408,..., dimensions={0} | all-to-all | bytes 65536 | tf_op jit(solution)/shard_map/all_to_all | solution.py:430
  185.6 1.9 last_block.1
  (2 shorter events, 0.0 us)
Async XLA Ops:
  2.0 20.0 %all-to-all-start = ((bf16[16,8,512]{2,1,0:T(8,128)(2,1)}), bf16[16,8,512]{2,1,0:T(8,128)(2,1)S(1)}, u32[]{:S(2)}, u32[]{:S(2)}) async-start(bf16[16,8,512]{2,1,0:T(8,128)(2,1)} %broadcast_in_dim.15), calls=%async_computation | async-start | bytes 262144 | tf_op jit(solution)/shard_map/all_to_all | solution.py:430
  18.1 3.0 %copy-start.3 = (s32[128]{0:T(128)S(1)}, s32[128]{0:T(128)}, u32[]{:S(2)}) copy-start(s32[128]{0:T(128)} %param.9) | copy-start | bytes 1540
  18.1 3.0 %copy-start.4 = (s32[128]{0:T(128)S(1)}, s32[128]{0:T(128)}, u32[]{:S(2)}) copy-start(s32[128]{0:T(128)} %param.8) | copy-start | bytes 1540
  18.1 3.9 %copy-start = (f32[8,512]{1,0:T(8,128)S(1)}, f32[8,512]{1,0:T(8,128)}, u32[]{:S(2)}) copy-start(f32[8,512]{1,0:T(8,128)} %prior.3) | copy-start | bytes 49156
  24.2 60.6 %copy-start.1 = (f32[8,512]{1,0:T(8,128)S(1)}, f32[8,512]{1,0:T(8,128)}, u32[]{:S(2)}) copy-start(f32[8,512]{1,0:T(8,128)} %prior.2) | copy-start | bytes 49156
  24.2 60.6 %copy-start.2 = (f32[8,8]{1,0:T(8,128)S(1)}, f32[8,8]{1,0:T(8,128)}, u32[]{:S(2)}) copy-start(f32[8,8]{1,0:T(8,128)} %beta.1) | copy-start | bytes 772

commit v11 on v10

--- a/solution.py
+++ b/solution.py
@@ -452,7 +452,7 @@
     cols = jnp.where(live, tile_col, n_row * sub // TILE)
     lines, others = lines_and_rest(n_row, n_col)
 
-    copies = jnp.broadcast_to(block.astype(BF16)[None], (n_row, NV, sub))
+    copies = jnp.broadcast_to(block[None], (n_row, NV, sub))
     band = swap(copies, "row")
     before = swap(front(rows, cols, squares, band, block, n_col), "col")
     partial, owned = back(rows, cols, squares, before, n_row, sub)

time: 188 us -> 188 us (level)
  no operation moved by 1% of the time
where the time goes in v11:
time: 188 us; the launch traced here: 187 us
  blocking collectives  151 us (80%)
  starting transfers between devices  13.8 us (7%)
  Pallas kernels  13.2 us (7%)
  local copies, waits for them, and re-layouts  6.08 us (3%)
  waiting for transfers between devices  1.9 us (1%)
    all_to_all x7, blocking collectives, swap(): lax.all_to_all(blocks, axis, 0, 0, tiled=True, axis_index_groups=groups)  151 us
    all_to_all x1, starting transfers between devices, swap(): lax.all_to_all(blocks, axis, 0, 0, tiled=True, axis_index_groups=groups)  13.8 us
  transfers between devices with their start and end apart: 1, of which 1 were waited for; matrix products, arithmetic and copies ran while one was open for 2% of the time, Pallas kernels for 0%

profile of v11, /device:TPU:1, one launch (start us, length us, event | category | flops | bytes accessed | tf_op | source)
XLA Modules:
  0.0 187.5 jit_solution(824910521766229114)
XLA Ops:
  0.6 1.4 broadcast_in_dim.15
  2.1 13.8 %all-to-all-start = ((f32[16,8,512]{2,1,0:T(8,128)}), f32[16,8,512]{2,1,0:T(8,128)S(1)}, u32[]{:S(2)}, u32[]{:S(2)}) async-start(f32[16,8,512]{2,1,0:T(8,128)} %broadcast_in_dim.15), calls=%async_computation | async-start | bytes 524288 | tf_op jit(solution)/shard_map/all_to_all | solution.py:430
  16.6 1.6 copy.9
  18.2 0.0 copy-start.3
  18.2 0.0 copy-start.4
  18.2 0.0 copy-start
  18.2 3.0 %copy.13.tiles = bf16[128,64,64]{2,1,0:T(8,128)(2,1)S(1)} copy(bf16[128,64,64]{0,2,1:T(8,128)(2,1)S(1)} %bitcast.3) | data formatting | bytes 2097152 | tf_op jit(solution)/shard_map/reshape | solution.py:449
  21.2 0.0 copy-done.3
  21.2 0.0 copy-done.4
  21.3 1.9 %all-to-all-done.band = f32[16,8,512]{2,1,0:T(8,128)S(1)} async-done(((f32[16,8,512]{2,1,0:T(8,128)}), f32[16,8,512]{2,1,0:T(8,128)S(1)}, u32[]{:S(2)}, u32[]{:S(2)}) %all-to-all-start) | async-done | bytes 262176 | tf_op jit(solution)/shard_map/all_to_all | solution.py:430
  23.2 0.0 copy-done
  23.2 2.1 %front_tiles.1 = bf16[48,64,128]{2,1,0:T(8,128)(2,1)S(1)} custom-call(s32[128]{0:T(128)S(1)} %get-tuple-element.29.rows, s32[128]{0:T(128)S(1)} %get-tuple-element.28.cols, bf16[128,64,64]{2,1,0:T(8,128)(2,1)S(1)} %copy.13.tiles, f32[16,8,512]{2,1,0:T(8,128)S(1)} %all-to-all-done.band, f32[8,512]{1,0:T(8,128)S(1)} %copy-done), custom_call_target="tpu_custom_call" | custom-call | tf_op jit(solution)/shard_map/front_tiles/pallas_call | solution.py:171
  25.2 0.0 copy-start.1
  25.3 0.0 copy-start.2
  25.3 44.3 %all_to_all.40.moved.before = bf16[48,64,128]{2,1,0:T(8,128)(2,1)S(1)} all-to-all(bf16[48,64,128]{2,1,0:T(8,128)(2,1)S(1)} %front_tiles.1), channel_id=1, replica_groups=mesh['row'=16,'col'=48] {'col'}, dimensions={0} | all-to-all | bytes 1572864 | tf_op jit(solution)/shard_map/all_to_all | solution.py:430
  69.5 1.6 back_tiles.1
  71.1 13.8 %all_to_all.41.returned = bf16[16,8,512]{2,1,0:T(8,128)(2,1)S(1)} all-to-all(bf16[16,8,512]{2,1,0:T(8,128)(2,1)S(1)} %get-tuple-element.16), channel_id=1, replica_groups=mesh['row'=16,'col'=48] {'row'}, dimensions={0} | all-to-all | bytes 262144 | tf_op jit(solution)/shard_map/all_to_all | solution.py:430
  84.9 0.0 copy-done.1
  84.9 0.0 copy-done.2
  84.9 0.4 local_carry.1
  85.3 10.8 %all_to_all.42.got = f32[16,8,640]{2,1,0:T(8,128)S(1)} all-to-all(f32[16,8,640]{2,1,0:T(8,128)S(1)} %get-tuple-element.17), channel_id=1, replica_groups=mesh['row'=16,'col'=48] {'row'}, dimensions={0} | all-to-all | bytes 655360 | tf_op jit(solution)/shard_map/all_to_all | solution.py:430
  96.2 3.3 %whiten_tiles.1 = bf16[48,72,128]{2,1,0:T(8,128)(2,1)S(1)} custom-call(s32[128]{0:T(128)S(1)} %get-tuple-element.29.rows, s32[128]{0:T(128)S(1)} %get-tuple-element.28.cols, bf16[128,64,64]{2,1,0:T(8,128)(2,1)S(1)} %copy.13.tiles, f32[16,8,640]{2,1,0:T(8,128)S(1)} %all_to_all.42.got, f32[8,512]{1,0:T(8,128)S(1)} %get-tuple-element.18.rest), custom_call_target="tpu_custom_call" | custom-call | tf_op jit(solution)/shard_map/whiten_tiles/pallas_call | solution.py:298
  99.4 40.9 %all_to_all.43.moved = bf16[48,72,128]{2,1,0:T(8,128)(2,1)S(1)} all-to-all(bf16[48,72,128]{2,1,0:T(8,128)(2,1)S(1)} %whiten_tiles.1), channel_id=1, replica_groups=mesh['row'=16,'col'=48] {'col'}, dimensions={0} | all-to-all | bytes 1769472 | tf_op jit(solution)/shard_map/all_to_all | solution.py:430
  140.4 3.6 %settle_tiles.1 = (bf16[16,8,512]{2,1,0:T(8,128)(2,1)S(1)}, f32[8,512]{1,0:T(8,128)S(1)}, f32[8,512]{1,0:T(8,128)S(1)}, f32[8,8]{1,0:T(8,128)S(1)}, f32[2,8,8]{2,1,0:T(8,128)S(1)}) custom-call(s32[128]{0:T(128)S(1)} %get-tuple-element.29.rows, s32[128]{0:T(128)S(1)} %get-tuple-element.28.cols, bf16[128,64,64]{2,1,0:T(8,128)(2,1)S(1)} %copy.13.tiles, ...), custom_call_target="tpu_custom_call" | custom-call | tf_op jit(solution)/shard_map/settle_tiles/pallas_call | solution.py:369
  143.9 14.5 %all_to_all.44.returned = bf16[16,8,512]{2,1,0:T(8,128)(2,1)S(1)} all-to-all(bf16[16,8,512]{2,1,0:T(8,128)(2,1)S(1)} %get-tuple-element.20), channel_id=1, replica_groups=mesh['row'=16,'col'=48] {'row'}, dimensions={0} | all-to-all | bytes 262144 | tf_op jit(solution)/shard_map/all_to_all | solution.py:430
  158.5 0.5 local_sums.1
  158.9 15.1 %all_to_all.45.parts = f32[24,2,128]{2,1,0:T(2,128)S(1)} all-to-all(f32[24,2,128]{2,1,0:T(2,128)S(1)} %get-tuple-element.23), channel_id=1, replica_groups={{0,1,2,3,4,5,6,7,8,9,10,11,48,49,50,51,52,53,54,55,56,57,58,59},{12,13,..., dimensions={0} | all-to-all | bytes 49152 | tf_op jit(solution)/shard_map/all_to_all | solution.py:430
  174.1 11.5 %all_to_all.46.parts = f32[32,2,128]{2,1,0:T(2,128)S(1)} all-to-all(f32[32,2,128]{2,1,0:T(2,128)S(1)} %spread_sums.1), channel_id=1, replica_groups={{0,12,24,36,96,108,120,132,192,204,216,228,288,300,312,324,384,396,408,..., dimensions={0} | all-to-all | bytes 65536 | tf_op jit(solution)/shard_map/all_to_all | solution.py:430
  185.6 1.9 last_block.1
  (2 shorter events, 0.0 us)
Async XLA Ops:
  2.1 21.1 %all-to-all-start = ((f32[16,8,512]{2,1,0:T(8,128)}), f32[16,8,512]{2,1,0:T(8,128)S(1)}, u32[]{:S(2)}, u32[]{:S(2)}) async-start(f32[16,8,512]{2,1,0:T(8,128)} %broadcast_in_dim.15), calls=%async_computation | async-start | bytes 524288 | tf_op jit(solution)/shard_map/all_to_all | solution.py:430
  18.2 3.0 %copy-start.3 = (s32[128]{0:T(128)S(1)}, s32[128]{0:T(128)}, u32[]{:S(2)}) copy-start(s32[128]{0:T(128)} %param.9) | copy-start | bytes 1540
  18.2 3.0 %copy-start.4 = (s32[128]{0:T(128)S(1)}, s32[128]{0:T(128)}, u32[]{:S(2)}) copy-start(s32[128]{0:T(128)} %param.8) | copy-start | bytes 1540
  18.2 4.9 %copy-start = (f32[8,512]{1,0:T(8,128)S(1)}, f32[8,512]{1,0:T(8,128)}, u32[]{:S(2)}) copy-start(f32[8,512]{1,0:T(8,128)} %prior.3) | copy-start | bytes 49156
  25.2 59.7 %copy-start.1 = (f32[8,512]{1,0:T(8,128)S(1)}, f32[8,512]{1,0:T(8,128)}, u32[]{:S(2)}) copy-start(f32[8,512]{1,0:T(8,128)} %prior.2) | copy-start | bytes 49156
  25.3 59.7 %copy-start.2 = (f32[8,8]{1,0:T(8,128)S(1)}, f32[8,8]{1,0:T(8,128)}, u32[]{:S(2)}) copy-start(f32[8,8]{1,0:T(8,128)} %beta.1) | copy-start | bytes 772
